TPU v7x, 32 devices: a whole 2x2x4 slice. The times are simulated.
32 devices in a mesh: face: 4 (over y, x), lon: 8 (over z, core).
Axes of the slice: x: 2, y: 2, z: 4, core: 2. Of those that a mesh axis runs over, the one named last changes fastest.
Arguments:
- source: bfloat16 [1024, 8, 128], P(('face', 'lon')), may hold values from -6 to 6
- intersection_weight: bfloat16 [1024, 4, 128, 128], P(('face', 'lon')), may hold values from -0.5 to 0.5
- dest_tile: int32 [1024, 4], P(('face', 'lon')), may hold values from 0 to 31, all different within a row; in each aligned block of 32 rows (0 to 31, 32 to 63, ...) at most 8 rows name the same one
- dest_row: int32 [1024, 4], P(('face', 'lon')), may hold values from 0 to 63
- prior_state: bfloat16 [8, 128, 2048], P(None, 'face', 'lon'), may hold values from -6 to 6
- lift_weight: bfloat16 [8, 64], replicated, may hold values from -9 to 9
- kernel: bfloat16 [9, 64, 64], replicated, may hold values from -0.23570226 to 0.23570226
- readout_weights: bfloat16 [64, 8], replicated, may hold values from -0.75 to 0.75
Outputs:
- remapped_reference: bfloat16 [8, 128, 2048], P(None, 'face', 'lon')
- network_estimate: bfloat16 [8, 128, 2048], P(None, 'face', 'lon')
- grad_lift: float32 [8, 64], replicated
- grad_kernel: float32 [9, 64, 64], replicated
- grad_head: float32 [64, 8], replicated
Inputs may be any that keep to these rules, and one draw needn't show every extreme that they name: `dest_tile`: the 4 intersections of a source block name distinct devices; the source blocks of one device name one device at most 8 times, and exactly 8 times for some device.
All inputs are finite; a program needn't handle non-finite values.
Results may differ from a plain program's by a relative error of at most 0.0013.
The roundings to bfloat16 on the way count: a program that leaves them out, or rounds other values in their place, can miss the bound.
Values may be sent and summed in bfloat16 or wider, within the bound.
No kernel may reach another device: no remote copies, remote signals or barrier semaphores. Data moves between devices by JAX's collectives and lax.ppermute only.
A program may use at most 128 MiB of HBM per device.

v0:
```python
import functools
import math

import jax
import jax.numpy as jnp
from jax import lax
from jax.experimental import pallas as pl
from jax.experimental.pallas import tpu as pltpu
from jax.sharding import PartitionSpec as P

NT = (((1,), (1,)), ((), ()))
VMEM_LIMIT = 40 * 1024 * 1024


def dot(a, b):
    return jnp.dot(a, b, preferred_element_type=jnp.float32)


def dot_nt(a, b):
    return lax.dot_general(a, b, NT, preferred_element_type=jnp.float32)


def regrid_kernel(capacity, tile_ref, row_ref, src_ref, wts_ref, out_ref, count_ref, head_ref):
    step = pl.program_id(0)
    chunk, fields, width = src_ref.shape
    intersections = wts_ref.shape[1]
    devices = out_ref.shape[0]

    @pl.when(step == 0)
    def _():
        out_ref[...] = jnp.zeros_like(out_ref)
        head_ref[...] = jnp.full_like(head_ref, -1.0)

        def clear(d, carry):
            count_ref[d] = 0
            return carry

        lax.fori_loop(0, devices, clear, 0)

    slot_of_lane = lax.rem(lax.broadcasted_iota(jnp.int32, (1, width), 1) // fields, capacity)
    for s in range(chunk):
        block = src_ref[s]
        for pair in range(0, intersections, 2):
            both = jnp.concatenate([wts_ref[s, k] for k in range(pair, min(pair + 2, intersections))], axis=1)
            contrib = dot(block, both).astype(jnp.bfloat16)
            for k in range(pair, min(pair + 2, intersections)):
                tile = tile_ref[step * chunk + s, k]
                slot = count_ref[tile]
                count_ref[tile] = slot + 1
                out_ref[tile, slot] = contrib[:, (k - pair) * width : (k - pair + 1) * width]
                label = row_ref[step * chunk + s, k].astype(jnp.float32)
                head_ref[pl.ds(tile, 1), :] = jnp.where(
                    slot_of_lane == slot, label, head_ref[pl.ds(tile, 1), :]
                )

    @pl.when(step == pl.num_programs(0) - 1)
    def _():
        for d in range(devices):
            out_ref[d, capacity] = jnp.broadcast_to(
                head_ref[d : d + 1, :], (fields, width)
            ).astype(jnp.bfloat16)


def regrid(source, weights, dest_tile, dest_row, devices, capacity):
    blocks, fields, width = source.shape
    intersections = weights.shape[1]
    chunk = math.gcd(blocks, 8)
    return pl.pallas_call(
        functools.partial(regrid_kernel, capacity),
        grid=(blocks // chunk,),
        out_shape=jax.ShapeDtypeStruct((devices, capacity + 1, fields, width), jnp.bfloat16),
        in_specs=[
            pl.BlockSpec(memory_space=pltpu.SMEM),
            pl.BlockSpec(memory_space=pltpu.SMEM),
            pl.BlockSpec((chunk, fields, width), lambda i: (i, 0, 0)),
            pl.BlockSpec((chunk, intersections, width, width), lambda i: (i, 0, 0, 0)),
        ],
        out_specs=pl.BlockSpec((devices, capacity + 1, fields, width), lambda i: (0, 0, 0, 0)),
        scratch_shapes=[
            pltpu.SMEM((devices,), jnp.int32),
            pltpu.VMEM((devices, width), jnp.float32),
        ],
        compiler_params=pltpu.CompilerParams(vmem_limit_bytes=VMEM_LIMIT),
        cost_estimate=pl.CostEstimate(
            flops=2 * weights.size * fields, bytes_accessed=2 * weights.size, transcendentals=0
        ),
        name="regrid",
    )(dest_tile, dest_row, source, weights)


def forward_kernel(
    channels,
    prior_ref,
    edge_ref,
    side_ref,
    lift_ref,
    conv_ref,
    readout_ref,
    feat_ref,
    stack_ref,
    hidden_ref,
    deriv_ref,
    forecast_ref,
    estimate_ref,
    halo_ref,
):
    rows, fields, width = prior_ref.shape
    pitch = lift_ref.shape[0]
    lift = lift_ref[...]

    def lift_row(values, at):
        feat_ref[pl.ds(pl.multiple_of(at * pitch, 16), pitch), :] = dot(lift, values).astype(jnp.bfloat16)

    lift_row(edge_ref[0], 0)
    lift_row(edge_ref[1], rows + 1)

    def lift_rows(y, carry):
        lift_row(prior_ref[y], y + 1)
        return carry

    lax.fori_loop(0, rows, lift_rows, 0, unroll=4)

    side = dot(lift, side_ref[...])
    shifted = [side] + [pltpu.roll(side, 256 - i, 1) for i in (1, 2)]
    stack = jnp.concatenate(shifted, axis=0).astype(jnp.bfloat16)
    stack_ref[...] = stack
    halo_ref[:, :128] = dot(conv_ref[:channels, :], stack[:, :128])
    halo_ref[:, 128:] = dot(conv_ref[2 * channels :, :], stack[:, 128:])
    lane = lax.broadcasted_iota(jnp.int32, (channels, width), 1)

    def one_row(y):
        window = feat_ref[pl.ds(pl.multiple_of(y * pitch, 16), 3 * pitch), :]
        parts = dot(conv_ref[...], window)
        left = pltpu.roll(parts[:channels], 1, 1)
        right = pltpu.roll(parts[2 * channels :], width - 1, 1)
        from_left = pltpu.roll(halo_ref[:, :128], lax.rem(128 - y, 128), 1)
        from_right = pltpu.roll(halo_ref[:, 128:], 127 - y, 1)
        spread = [jnp.zeros_like(from_left)] * (width // 128 - 1)
        left = jnp.where(lane == 0, jnp.concatenate([from_left] + spread, axis=1), left)
        right = jnp.where(lane == width - 1, jnp.concatenate(spread + [from_right], axis=1), right)
        act = parts[channels : 2 * channels] + left + right
        sig = 1.0 / (1.0 + jnp.exp(-act))
        hidden = (act * sig).astype(jnp.bfloat16)
        at = pl.ds(pl.multiple_of(y * channels, 16), channels)
        hidden_ref[at, :] = hidden
        deriv_ref[at, :] = sig * (1.0 + act * (1.0 - sig))
        forecast = prior_ref[y].astype(jnp.float32) + dot(readout_ref[...], hidden)
        forecast_ref[y] = forecast
        estimate_ref[y] = forecast.astype(jnp.bfloat16)

    def some_rows(step, carry):
        for r in range(4):
            one_row(step * 4 + r)
        return carry

    lax.fori_loop(0, rows // 4, some_rows, 0)


def forward(prior, edges, sides, lift, conv, readout, channels):
    rows, fields, width = prior.shape
    pitch = lift.shape[0]
    return pl.pallas_call(
        functools.partial(forward_kernel, channels),
        out_shape=(
            jax.ShapeDtypeStruct(((rows + 2) * pitch, width), jnp.bfloat16),
            jax.ShapeDtypeStruct((3 * pitch, 256), jnp.bfloat16),
            jax.ShapeDtypeStruct((rows * channels, width), jnp.bfloat16),
            jax.ShapeDtypeStruct((rows * channels, width), jnp.float32),
            jax.ShapeDtypeStruct((rows, fields, width), jnp.float32),
            jax.ShapeDtypeStruct((rows, fields, width), jnp.bfloat16),
        ),
        scratch_shapes=[pltpu.VMEM((channels, 256), jnp.float32)],
        compiler_params=pltpu.CompilerParams(vmem_limit_bytes=VMEM_LIMIT),
        cost_estimate=pl.CostEstimate(
            flops=2 * rows * width * 3 * channels * 3 * pitch,
            bytes_accessed=rows * width * channels * 8,
            transcendentals=rows * width * channels * 2,
        ),
        name="forward",
    )(prior, edges, sides, lift, conv, readout)


def backward_kernel(
    capacity,
    channels,
    norm,
    side_bit,
    arrived_hbm,
    feat_hbm,
    hidden_hbm,
    deriv_hbm,
    forecast_hbm,
    stack_ref,
    readout_ref,
    back_ref,
    contract_ref,
    remapped_ref,
    packed_ref,
    arrived_ref,
    feat_ref,
    hidden_ref,
    deriv_ref,
    forecast_ref,
    picked_ref,
    slope_ref,
    total_ref,
    edge_ref,
    small_ref,
    sems,
):
    pairs = (
        (arrived_hbm, arrived_ref),
        (forecast_hbm, forecast_ref),
        (deriv_hbm, deriv_ref),
        (hidden_hbm, hidden_ref),
        (feat_hbm, feat_ref),
    )
    copies = [pltpu.make_async_copy(a, b, sems.at[i]) for i, (a, b) in enumerate(pairs)]
    for copy in copies:
        copy.start()
    rows, fields, width = remapped_ref.shape
    pitch = feat_ref.shape[0] // (rows + 2)
    devices = arrived_ref.shape[0]
    per_row = width // 128
    blocks = rows * per_row
    group = 128 // (fields * capacity)

    total_ref[...] = jnp.zeros_like(total_ref)
    edge_ref[...] = jnp.zeros_like(edge_ref)
    small_ref[...] = jnp.zeros_like(small_ref)
    slope_ref[:channels, :] = jnp.zeros((channels, width), jnp.bfloat16)
    slope_ref[(rows + 1) * channels :, :] = jnp.zeros((channels, width), jnp.bfloat16)
    lane = lax.broadcasted_iota(jnp.int32, (fields, 128), 1)
    sublane = lax.broadcasted_iota(jnp.int32, (fields, 128), 0)
    wanted = lax.broadcasted_iota(jnp.int32, (blocks, fields, 256), 0) * fields

    copies[0].wait()
    picked = None
    for first in range(0, devices, 2 * group):
        labels, data = [], []
        for half in range(2):
            label = None
            for d in range(group):
                device = first + half * group + d
                mine = arrived_ref[device, capacity * fields : (capacity + 1) * fields, :].astype(jnp.float32)
                label = mine if label is None else jnp.where(lane // (fields * capacity) == d, mine, label)
                data.append(arrived_ref[device, : capacity * fields, :])
            labels.append(label.astype(jnp.int32) * fields + lane % fields - sublane)
        hits = jnp.concatenate(labels, axis=1)[None] == wanted
        hits = jnp.where(hits, 1.0, 0.0).reshape(blocks * fields, 256).astype(jnp.bfloat16)
        part = dot(hits, jnp.concatenate(data, axis=0))
        picked = part if picked is None else picked + part
    picked_ref[...] = picked.astype(jnp.bfloat16).astype(jnp.float32).reshape(blocks, fields, 128)

    for copy in copies[1:]:
        copy.wait()
    col = lax.broadcasted_iota(jnp.int32, (channels, width), 1)
    lane = lax.broadcasted_iota(jnp.int32, (channels, 128), 1)
    batch = 4

    def slopes(step, carry):
        features, trios, hiddens, misfits = [], [], [], []
        ends_left, ends_right = edge_ref[:, :128], edge_ref[:, 128:]
        for r in range(batch):
            y = step * batch + r
            target = jnp.concatenate([picked_ref[y * per_row + b] for b in range(per_row)], axis=1)
            remapped_ref[y] = target.astype(jnp.bfloat16)
            misfit = ((forecast_ref[y] - target) * norm).astype(jnp.bfloat16)
            here = pl.ds(pl.multiple_of(y * channels, 16), channels)
            slope = dot(readout_ref[...], misfit) * deriv_ref[here, :]
            slope_ref[pl.ds(pl.multiple_of((y + 1) * channels, 16), channels), :] = slope.astype(jnp.bfloat16)
            before = jnp.where(col == width - 1, 0.0, pltpu.roll(slope, width - 1, 1))
            after = jnp.where(col == 0, 0.0, pltpu.roll(slope, 1, 1))
            trios.append(jnp.concatenate([before, slope, after], axis=0).astype(jnp.bfloat16))
            features.append(feat_ref[pl.ds(pl.multiple_of(y * pitch, 16), 3 * pitch), :])
            hiddens.append(hidden_ref[here, :])
            misfits.append(misfit)
            ends_left += pltpu.roll(jnp.where(lane == 0, slope[:, :128], 0.0), y, 1)
            ends_right += pltpu.roll(jnp.where(lane == 127, slope[:, -128:], 0.0), y + 1, 1)
        edge_ref[:, :128], edge_ref[:, 128:] = ends_left, ends_right
        total_ref[...] += dot_nt(jnp.concatenate(features, axis=1), jnp.concatenate(trios, axis=1))
        small_ref[0] += dot_nt(jnp.concatenate(misfits, axis=1), jnp.concatenate(hiddens, axis=1))
        return carry

    lax.fori_loop(0, rows // batch, slopes, 0)

    def roundings(step, carry):
        deltas, states = [], []
        for r in range(batch):
            y = step * batch + r
            window = slope_ref[pl.ds(pl.multiple_of(y * channels, 16), 3 * channels), :]
            parts = dot(back_ref[...], window)
            grad = (
                parts[channels : 2 * channels]
                + pltpu.roll(parts[:channels], width - 1, 1)
                + pltpu.roll(parts[2 * channels :], 1, 1)
            )
            inside = (col > 0) & (col < width - 1) & (y > 0) & (y < rows - 1)
            delta = jnp.where(inside, grad.astype(jnp.bfloat16).astype(jnp.float32) - grad, 0.0)
            deltas.append(delta.astype(jnp.bfloat16))
            states.append(
                feat_ref[pl.ds(pl.multiple_of((y + 1) * pitch + channels, 16), pitch - channels), :]
            )
        part = dot_nt(jnp.concatenate(states, axis=1), jnp.concatenate(deltas, axis=1))
        small_ref[1] += part[:fields]
        return carry

    lax.fori_loop(0, rows // batch, roundings, 0)

    ends = edge_ref[...].astype(jnp.bfloat16)
    total_ref[:, :channels] += dot_nt(stack_ref[:, :128], ends[:, :128])
    total_ref[:, 2 * channels :] += dot_nt(stack_ref[:, 128:], ends[:, 128:])
    grad_lift = small_ref[1]
    for i in range(3):
        rest = total_ref[i * pitch + channels : i * pitch + channels + fields, :]
        for _ in range(3):
            piece = rest.astype(jnp.bfloat16)
            rest = rest - piece.astype(jnp.float32)
            grad_lift += dot_nt(piece, contract_ref[i])
    taps = [total_ref[i * pitch : i * pitch + channels, :] for i in range(3)]
    half = channels // 2
    last = [t[:, 2 * channels :] for t in taps]
    packed = [t[:, : 2 * channels] for t in taps]
    packed.append(jnp.concatenate(last[:2], axis=1))
    packed.append(jnp.concatenate([last[2][:half], last[2][half:]], axis=1))
    packed.append(jnp.concatenate([grad_lift, small_ref[0]], axis=1))
    packed.append(jnp.zeros((8, 2 * channels), jnp.float32))
    packed = jnp.concatenate(packed, axis=0)
    cut = packed.shape[0] // 2
    odd = lax.rem(lax.axis_index("lon"), 2)
    packed_ref[odd] = packed[:cut]
    packed_ref[1 - odd] = packed[cut:]


def backward(arrived, feat, stack, hidden, deriv, forecast, readout, back, contract, capacity, norm):
    rows, fields, width = forecast.shape
    channels = readout.shape[0]
    pitch = feat.shape[0] // (rows + 2)
    blocks = rows * (width // 128)
    packed_rows = (3 * channels + channels + channels // 2 + fields + 8) // 2
    any_space = pl.BlockSpec(memory_space=pl.ANY)
    vmem = pl.BlockSpec(memory_space=pltpu.VMEM)
    return pl.pallas_call(
        functools.partial(backward_kernel, capacity, channels, norm, 0),
        out_shape=(
            jax.ShapeDtypeStruct((rows, fields, width), jnp.bfloat16),
            jax.ShapeDtypeStruct((2, packed_rows, 2 * channels), jnp.float32),
        ),
        in_specs=[any_space] * 5 + [vmem] * 4,
        out_specs=(vmem, vmem),
        scratch_shapes=[
            pltpu.VMEM(arrived.shape, jnp.bfloat16),
            pltpu.VMEM(feat.shape, jnp.bfloat16),
            pltpu.VMEM(hidden.shape, jnp.bfloat16),
            pltpu.VMEM(deriv.shape, jnp.float32),
            pltpu.VMEM(forecast.shape, jnp.float32),
            pltpu.VMEM((blocks, fields, 128), jnp.float32),
            pltpu.VMEM(((rows + 2) * channels, width), jnp.bfloat16),
            pltpu.VMEM((3 * pitch, 3 * channels), jnp.float32),
            pltpu.VMEM((channels, 256), jnp.float32),
            pltpu.VMEM((2, fields, channels), jnp.float32),
            pltpu.SemaphoreType.DMA((5,)),
        ],
        compiler_params=pltpu.CompilerParams(vmem_limit_bytes=VMEM_LIMIT),
        cost_estimate=pl.CostEstimate(
            flops=4 * rows * width * 3 * channels * 3 * pitch,
            bytes_accessed=rows * width * channels * 8,
            transcendentals=0,
        ),
        name="backward",
    )(arrived, feat, hidden, deriv, forecast, stack, readout, back, contract)


def unpack_kernel(channels, mine_ref, other_ref, kernel_ref, lift_ref, head_ref):
    odd = lax.rem(lax.axis_index("lon"), 2) == 1
    mine, other = mine_ref[...], other_ref[...]
    packed = jnp.concatenate([jnp.where(odd, other, mine), jnp.where(odd, mine, other)], axis=0)
    half = channels // 2
    for i in range(3):
        block = packed[i * channels : (i + 1) * channels]
        kernel_ref[3 * i] = block[:, :channels]
        kernel_ref[3 * i + 1] = block[:, channels:]
    block = packed[3 * channels : 4 * channels]
    kernel_ref[2] = block[:, :channels]
    kernel_ref[5] = block[:, channels:]
    block = packed[4 * channels : 4 * channels + half]
    kernel_ref[8, :half] = block[:, :channels]
    kernel_ref[8, half:] = block[:, channels:]
    block = packed[4 * channels + half : 4 * channels + half + lift_ref.shape[0]]
    lift_ref[...] = block[:, :channels]
    head_ref[...] = block[:, channels:].T


def unpack(mine, other, channels, fields):
    return pl.pallas_call(
        functools.partial(unpack_kernel, channels),
        out_shape=(
            jax.ShapeDtypeStruct((9, channels, channels), jnp.float32),
            jax.ShapeDtypeStruct((fields, channels), jnp.float32),
            jax.ShapeDtypeStruct((channels, fields), jnp.float32),
        ),
        name="unpack",
    )(mine, other)


def swap(x, axis, bit):
    return lax.ppermute(x, axis, [(i, i ^ bit) for i in range(lax.axis_size(axis))])


def sum_over(x, axis, low, high):
    if high // low == 4:
        a, b, c = (swap(x, axis, k * low) for k in (1, 2, 3))
        return (x + a) + (b + c)
    bit = low
    while bit < high:
        x = x + swap(x, axis, bit)
        bit *= 2
    return x


def pair_swap(even_sends, odd_sends, axis, periodic):
    count = lax.axis_size(axis)
    even = lax.rem(lax.axis_index(axis), 2) == 0
    inner = [(i, i ^ 1) for i in range(count)]
    outer = []
    for i in range(1, count, 2):
        if i + 1 < count or periodic:
            outer += [(i, (i + 1) % count), ((i + 1) % count, i)]
    got_inner = lax.ppermute(jnp.where(even, odd_sends, even_sends), axis, inner)
    got_outer = lax.ppermute(jnp.where(even, even_sends, odd_sends), axis, outer)
    return jnp.where(even, got_outer, got_inner), jnp.where(even, got_inner, got_outer)


def per_device(
    source,
    intersection_weight,
    dest_tile,
    dest_row,
    prior_state,
    lift_weight,
    kernel,
    readout_weights,
):
    face_count = lax.axis_size("face")
    lon_count = lax.axis_size("lon")
    devices = face_count * lon_count
    src_blocks, intersections = dest_tile.shape
    fields, rows, width = prior_state.shape
    channels = kernel.shape[1]
    pitch = channels + 16
    capacity = max(2, 2 * src_blocks * intersections // devices)
    norm = 1.0 / math.sqrt(rows * face_count * width * lon_count)

    outgoing = regrid(source, intersection_weight, dest_tile, dest_row, devices, capacity)
    arrived = lax.all_to_all(outgoing, ("face", "lon"), split_axis=0, concat_axis=0, tiled=True)
    arrived = arrived.reshape(devices, (capacity + 1) * fields, source.shape[2])

    prior = prior_state.transpose(1, 0, 2)
    top, bottom = pair_swap(prior[0], prior[rows - 1], "face", False)
    columns = [
        jnp.pad(
            jnp.concatenate([top[:, at : at + 1], prior_state[:, :, at], bottom[:, at : at + 1]], axis=1),
            ((0, 0), (0, 128 - rows - 2)),
        )
        for at in (0, width - 1)
    ]
    left, right = pair_swap(columns[0], columns[1], "lon", True)

    taps = kernel.reshape(3, 3, channels, channels)
    lift = jnp.concatenate(
        [lift_weight.T, jnp.eye(fields, dtype=jnp.bfloat16), jnp.zeros((16 - fields, fields), jnp.bfloat16)]
    )
    conv = jnp.pad(
        taps.transpose(1, 3, 0, 2), ((0, 0), (0, 0), (0, 0), (0, pitch - channels))
    ).reshape(3 * channels, 3 * pitch)
    back = taps[::-1].transpose(1, 2, 0, 3).reshape(3 * channels, 3 * channels)
    contract = taps.transpose(0, 2, 1, 3).reshape(3, channels, 3 * channels)
    feat, stack, hidden, deriv, forecast, estimate = forward(
        prior,
        jnp.stack([top, bottom]),
        jnp.concatenate([left, right], axis=1),
        lift,
        conv,
        readout_weights.T,
        channels,
    )
    remapped, packed = backward(
        arrived, feat, stack, hidden, deriv, forecast, readout_weights, back, contract, capacity, norm
    )
    part = packed[0] + swap(packed[1], "lon", 1)
    part = sum_over(part, "face", 1, face_count)
    part = sum_over(part, "lon", 2, lon_count)
    grad_kernel, grad_lift, grad_head = unpack(part, swap(part, "lon", 1), channels, fields)
    return (
        remapped.transpose(1, 0, 2),
        estimate.transpose(1, 0, 2),
        grad_lift,
        grad_kernel,
        grad_head,
    )


def solution(mesh):
    return jax.shard_map(
        per_device,
        mesh=mesh,
        in_specs=(
            P(("face", "lon"), None, None),
            P(("face", "lon"), None, None, None),
            P(("face", "lon"), None),
            P(("face", "lon"), None),
            P(None, "face", "lon"),
            P(),
            P(),
            P(),
        ),
        out_specs=(P(None, "face", "lon"), P(None, "face", "lon"), P(), P(), P()),
        check_vma=False,
    )
```

profile of v0, /device:TPU:0, one launch (start us, length us, event | category | flops | bytes accessed | tf_op | source)
XLA Modules:
  0.0 85.9 jit_solution(2381151985554004676)
XLA Ops:
  0.6 1.0 %copy.57 = bf16[8,32,256]{2,0,1:T(8,128)(2,1)S(1)} copy(bf16[8,32,256]{2,1,0:T(8,128)(2,1)} %param.12) | data formatting | bytes 262144 | tf_op args[4]
  2.3 5.7 %collective-permute-start.1 = (bf16[8,256]{1,0:T(8,128)(2,1)S(1)}, bf16[8,256]{1,0:T(8,128)(2,1)S(1)}, u32[]{:S(2)}, u32[]{:S(2)}) collective-permute-start(bf16[8,256]{1,0:T(8,128)(2,1)S(1)} %get-tuple-element.45), channel_id=1, source_target_pairs={{0,8},{8,0},{16,24},{24,16},{1,9},{9,1},{17,25},{25,17},{2,10},{10... | collective-permute-start | bytes 12296 | tf_op jit(solution)/shard_map/ppermute | solution.py:429
  8.0 0.8 copy.40.tile_ref
  8.8 0.8 copy.41.row_ref
  9.6 2.2 %copy-done = bf16[32,4,128,128]{3,2,1,0:T(8,128)(2,1)S(1)} copy-done((bf16[32,4,128,128]{3,2,1,0:T(8,128)(2,1)S(1)}, bf16[32,4,128,128]{3,2,1,0:T(8,128)(2,1)}, u32[]{:S(2)}) %copy-start) | copy-done | bytes 4194328
  11.8 0.8 copy-done.6
  12.6 3.3 %regrid.1 = bf16[32,9,8,128]{3,2,1,0:T(8,128)(2,1)} custom-call(s32[32,4]{1,0:T(8,128)S(1)} %copy.40.tile_ref, s32[32,4]{1,0:T(8,128)S(1)} %copy.41.row_ref, bf16[32,8,128]{2,1,0:T(8,128)(2,1)S(1)} %copy-done.6, bf16[32,4,128,128]{3,2,1,0:T(8,128)(2,1)S(1)} %copy-done), custom_call_target="tpu_custom_call" | custom-call | flops 33554432 | bytes 4194304 | tf_op jit(solution)/shard_map/regrid/pallas_call | solution.py:68
  15.9 4.8 %all-to-all-start = ((bf16[32,9,8,128]{3,2,1,0:T(8,128)(2,1)}), bf16[32,9,8,128]{3,2,1,0:T(8,128)(2,1)S(1)}, u32[]{:S(2)}, u32[]{:S(2)}) async-start(bf16[32,9,8,128]{3,2,1,0:T(8,128)(2,1)} %regrid.1), calls=%async_computation | async-start | bytes 1179648 | tf_op jit(solution)/shard_map/all_to_all | solution.py:455
  21.6 0.7 copy.46.lift_ref
  22.7 0.8 rev.3
  23.8 0.8 reshape.31.conv_ref
  24.8 3.4 %collective-permute-start.2 = (bf16[8,128]{1,0:T(8,128)(2,1)S(1)}, bf16[8,128]{1,0:T(8,128)(2,1)S(1)}, u32[]{:S(2)}, u32[]{:S(2)}) collective-permute-start(bf16[8,128]{1,0:T(8,128)(2,1)S(1)} %get-tuple-element.46), channel_id=1, source_target_pairs={{1,2},{2,1},{3,4},{4,3},{5,6},{6,5},{7,0},{0,7},{9,10},{10,9},{11,... | collective-permute-start | bytes 6152 | tf_op jit(solution)/shard_map/ppermute | solution.py:430
  28.2 6.4 %collective-permute-done.2 = bf16[8,128]{1,0:T(8,128)(2,1)S(1)} collective-permute-done((bf16[8,128]{1,0:T(8,128)(2,1)S(1)}, bf16[8,128]{1,0:T(8,128)(2,1)S(1)}, u32[]{:S(2)}, u32[]{:S(2)}) %collective-permute-start.2) | collective-permute-done | bytes 2080 | tf_op jit(solution)/shard_map/ppermute | solution.py:430
  34.6 0.9 %copy-done.5 = bf16[192,240]{1,0:T(8,128)(2,1)S(1)} copy-done((bf16[192,240]{1,0:T(8,128)(2,1)S(1)}, bf16[192,240]{1,0:T(8,128)(2,1)}, u32[]{:S(2)}) %copy-start.5) | copy-done | bytes 92184
  35.4 0.7 copy-done.7
  36.2 10.2 %forward.1 = (bf16[2720,256]{1,0:T(8,128)(2,1)S(1)}, bf16[240,256]{1,0:T(8,128)(2,1)S(1)}, bf16[2048,256]{1,0:T(8,128)(2,1)S(1)}, f32[2048,256]{1,0:T(8,128)S(1)...) custom-call(bf16[32,8,256]{2,1,0:T(8,128)(2,1)S(1)} %bitcast.28, ...), custom_call_target="tpu_custom_call" | custom-call | flops 754974720 | bytes 4194304 | tf_op jit(solution)/shard_map/forward/pallas_call | solution.py:162
  46.3 1.1 %copy-done.1 = bf16[2720,256]{1,0:T(8,128)(2,1)} copy-done((bf16[2720,256]{1,0:T(8,128)(2,1)}, bf16[2720,256]{1,0:T(8,128)(2,1)S(1)}, u32[]{:S(2)}) %copy-start.1) | copy-done | bytes 1392664
  47.5 1.0 %copy-done.3 = bf16[2048,256]{1,0:T(8,128)(2,1)} copy-done((bf16[2048,256]{1,0:T(8,128)(2,1)}, bf16[2048,256]{1,0:T(8,128)(2,1)S(1)}, u32[]{:S(2)}) %copy-start.3) | copy-done | bytes 1048600
  48.4 1.3 %copy-done.2 = bf16[2720,256]{1,0:T(8,128)(2,1)S(1)} copy-done((bf16[2720,256]{1,0:T(8,128)(2,1)S(1)}, bf16[2720,256]{1,0:T(8,128)(2,1)}, u32[]{:S(2)}) %copy-start.2) | copy-done | bytes 1392664
  49.8 1.2 %copy-done.4 = bf16[2048,256]{1,0:T(8,128)(2,1)S(1)} copy-done((bf16[2048,256]{1,0:T(8,128)(2,1)S(1)}, bf16[2048,256]{1,0:T(8,128)(2,1)}, u32[]{:S(2)}) %copy-start.4) | copy-done | bytes 1048600
  51.0 10.0 %backward.1 = (bf16[32,8,256]{2,1,0:T(8,128)(2,1)S(1)}, f32[2,152,128]{2,1,0:T(8,128)S(1)}) custom-call(bf16[32,72,128]{2,1,0:T(8,128)(2,1)S(1)} %bitcast.26, bf16[2720,256]{1,0:T(8,128)(2,1)S(1)} %copy-done.2, bf16[2048,256]{1,0:T(8,128)(2,1)S(1)} %copy-done.4, f32[2048,256]{1,0:T(8,128)S(1)} %get-tuple-element.18.deriv_hbm, ...), custom_call_target="tpu_custom_call" | custom-call | flops 1509949440 | bytes 4194304 | tf_op jit(solution)/shard_map/backward/pallas_call | solution.py:343
  61.2 1.3 %collective-permute-done.4 = f32[152,128]{1,0:T(8,128)S(1)} collective-permute-done((f32[152,128]{1,0:T(8,128)S(1)}, f32[152,128]{1,0:T(8,128)S(1)}, u32[]{:S(2)}, u32[]{:S(2)}) %collective-permute-start.4) | collective-permute-done | bytes 77856 | tf_op jit(solution)/shard_map/ppermute | solution.py:407
  62.4 2.5 %collective-permute-start.7 = (f32[152,128]{1,0:T(8,128)S(1)}, f32[152,128]{1,0:T(8,128)S(1)}, u32[]{:S(2)}, u32[]{:S(2)}) collective-permute-start(f32[152,128]{1,0:T(8,128)S(1)} %bitcast_add_fusion), channel_id=1, source_target_pairs={{0,24},{8,16},{16,8},{24,0},{1,25},{9,17},{17,9},{25,1},{2,26},{10... | collective-permute-start | bytes 233480 | tf_op jit(solution)/shard_map/ppermute | solution.py:407
  66.0 1.9 %collective-permute-done.7 = f32[152,128]{1,0:T(8,128)S(1)} collective-permute-done((f32[152,128]{1,0:T(8,128)S(1)}, f32[152,128]{1,0:T(8,128)S(1)}, u32[]{:S(2)}, u32[]{:S(2)}) %collective-permute-start.7) | collective-permute-done | bytes 77856 | tf_op jit(solution)/shard_map/ppermute | solution.py:407
  67.9 1.6 %collective-permute-done.6 = f32[152,128]{1,0:T(8,128)S(1)} collective-permute-done((f32[152,128]{1,0:T(8,128)S(1)}, f32[152,128]{1,0:T(8,128)S(1)}, u32[]{:S(2)}, u32[]{:S(2)}) %collective-permute-start.6) | collective-permute-done | bytes 77856 | tf_op jit(solution)/shard_map/ppermute | solution.py:407
  69.9 0.8 collective-permute-start.10
  70.7 3.7 %collective-permute-start.9 = (f32[152,128]{1,0:T(8,128)S(1)}, f32[152,128]{1,0:T(8,128)S(1)}, u32[]{:S(2)}, u32[]{:S(2)}) collective-permute-start(f32[152,128]{1,0:T(8,128)S(1)} %add_add_fusion.1), channel_id=1, source_target_pairs={{0,4},{1,5},{2,6},{3,7},{4,0},{5,1},{6,2},{7,3},{8,12},{9,13},{10,... | collective-permute-start | bytes 233480 | tf_op jit(solution)/shard_map/ppermute | solution.py:407
  74.4 2.3 %collective-permute-done.10 = f32[152,128]{1,0:T(8,128)S(1)} collective-permute-done((f32[152,128]{1,0:T(8,128)S(1)}, f32[152,128]{1,0:T(8,128)S(1)}, u32[]{:S(2)}, u32[]{:S(2)}) %collective-permute-start.10) | collective-permute-done | bytes 77856 | tf_op jit(solution)/shard_map/ppermute | solution.py:407
  76.7 3.9 %collective-permute-done.9 = f32[152,128]{1,0:T(8,128)S(1)} collective-permute-done((f32[152,128]{1,0:T(8,128)S(1)}, f32[152,128]{1,0:T(8,128)S(1)}, u32[]{:S(2)}, u32[]{:S(2)}) %collective-permute-start.9) | collective-permute-done | bytes 77856 | tf_op jit(solution)/shard_map/ppermute | solution.py:407
  80.7 0.7 copy.52
  82.7 1.8 %unpack.1 = (f32[9,64,64]{2,1,0:T(8,128)}, f32[8,64]{1,0:T(8,128)}, f32[64,8]{1,0:T(8,128)}) custom-call(f32[152,128]{1,0:T(8,128)} %copy-done.11, f32[152,128]{1,0:T(8,128)} %copy-done.12), custom_call_target="tpu_custom_call" | custom-call | tf_op jit(solution)/shard_map/unpack/pallas_call | solution.py:395
  84.5 1.4 %copy.53 = f32[64,8]{0,1:T(8,128)} copy(f32[64,8]{1,0:T(8,128)} %get-tuple-element.41) | data formatting | bytes 4096
  (60 shorter events, 5.3 us)
Async XLA Ops:
  1.6 23.0 %collective-permute-start = (bf16[8,256]{1,0:T(8,128)(2,1)S(1)}, bf16[8,256]{1,0:T(8,128)(2,1)S(1)}, u32[]{:S(2)}, u32[]{:S(2)}) collective-permute-start(bf16[8,256]{1,0:T(8,128)(2,1)S(1)} %get-tuple-element.44), channel_id=1, source_target_pairs={{8,16},{16,8},{9,17},{17,9},{10,18},{18,10},{11,19},{19,11},{12,20... | collective-permute-start | bytes 12296 | tf_op jit(solution)/shard_map/ppermute | solution.py:430
  2.3 22.3 %collective-permute-start.1 = (bf16[8,256]{1,0:T(8,128)(2,1)S(1)}, bf16[8,256]{1,0:T(8,128)(2,1)S(1)}, u32[]{:S(2)}, u32[]{:S(2)}) collective-permute-start(bf16[8,256]{1,0:T(8,128)(2,1)S(1)} %get-tuple-element.45), channel_id=1, source_target_pairs={{0,8},{8,0},{16,24},{24,16},{1,9},{9,1},{17,25},{25,17},{2,10},{10... | collective-permute-start | bytes 12296 | tf_op jit(solution)/shard_map/ppermute | solution.py:429
  9.6 2.2 %copy-start = (bf16[32,4,128,128]{3,2,1,0:T(8,128)(2,1)S(1)}, bf16[32,4,128,128]{3,2,1,0:T(8,128)(2,1)}, u32[]{:S(2)}) copy-start(bf16[32,4,128,128]{3,2,1,0:T(8,128)(2,1)} %wts_ref.1) | copy-start | bytes 12582916
  11.8 0.8 copy-start.6
  12.6 8.2 %copy-start.10 = (bf16[8,32,256]{2,1,0:T(8,128)(2,1)S(1)}, bf16[8,32,256]{2,1,0:T(8,128)(2,1)}, u32[]{:S(2)}) copy-start(bf16[8,32,256]{2,1,0:T(8,128)(2,1)} %param.12) | copy-start | bytes 393220
  12.6 8.4 %copy-start.13 = (bf16[8,64]{1,0:T(8,128)(2,1)S(1)}, bf16[8,64]{1,0:T(8,128)(2,1)}, u32[]{:S(2)}) copy-start(bf16[8,64]{1,0:T(8,128)(2,1)} %param.13) | copy-start | bytes 3076
  12.6 8.4 %copy-start.9 = (bf16[9,64,64]{2,1,0:T(8,128)(2,1)S(1)}, bf16[9,64,64]{2,1,0:T(8,128)(2,1)}, u32[]{:S(2)}) copy-start(bf16[9,64,64]{2,1,0:T(8,128)(2,1)} %param.14) | copy-start | bytes 221188
  15.9 5.6 %copy-start.8 = (bf16[64,8]{0,1:T(8,128)(2,1)S(1)}, bf16[64,8]{0,1:T(8,128)(2,1)}, u32[]{:S(2)}) copy-start(bf16[64,8]{0,1:T(8,128)(2,1)} %param.15) | copy-start | bytes 3076
  15.9 32.5 %all-to-all-start = ((bf16[32,9,8,128]{3,2,1,0:T(8,128)(2,1)}), bf16[32,9,8,128]{3,2,1,0:T(8,128)(2,1)S(1)}, u32[]{:S(2)}, u32[]{:S(2)}) async-start(bf16[32,9,8,128]{3,2,1,0:T(8,128)(2,1)} %regrid.1), calls=%async_computation | async-start | bytes 1179648 | tf_op jit(solution)/shard_map/all_to_all | solution.py:455
  24.8 9.7 %collective-permute-start.2 = (bf16[8,128]{1,0:T(8,128)(2,1)S(1)}, bf16[8,128]{1,0:T(8,128)(2,1)S(1)}, u32[]{:S(2)}, u32[]{:S(2)}) collective-permute-start(bf16[8,128]{1,0:T(8,128)(2,1)S(1)} %get-tuple-element.46), channel_id=1, source_target_pairs={{1,2},{2,1},{3,4},{4,3},{5,6},{6,5},{7,0},{0,7},{9,10},{10,9},{11,... | collective-permute-start | bytes 6152 | tf_op jit(solution)/shard_map/ppermute | solution.py:430
  28.2 6.4 %collective-permute-start.3 = (bf16[8,128]{1,0:T(8,128)(2,1)S(1)}, bf16[8,128]{1,0:T(8,128)(2,1)S(1)}, u32[]{:S(2)}, u32[]{:S(2)}) collective-permute-start(bf16[8,128]{1,0:T(8,128)(2,1)S(1)} %get-tuple-element.47), channel_id=1, source_target_pairs={{0,1},{1,0},{2,3},{3,2},{4,5},{5,4},{6,7},{7,6},{8,9},{9,8},{10,11... | collective-permute-start | bytes 6152 | tf_op jit(solution)/shard_map/ppermute | solution.py:429
  34.5 0.9 %copy-start.5 = (bf16[192,240]{1,0:T(8,128)(2,1)S(1)}, bf16[192,240]{1,0:T(8,128)(2,1)}, u32[]{:S(2)}) copy-start(bf16[192,240]{1,0:T(8,128)(2,1)} %reshape.31.conv_ref) | copy-start | bytes 276484
  35.4 0.7 copy-start.7
  46.3 1.1 %copy-start.1 = (bf16[2720,256]{1,0:T(8,128)(2,1)}, bf16[2720,256]{1,0:T(8,128)(2,1)S(1)}, u32[]{:S(2)}) copy-start(bf16[2720,256]{1,0:T(8,128)(2,1)S(1)} %get-tuple-element.16.feat_hbm) | copy-start | bytes 4177924
  47.5 1.0 %copy-start.3 = (bf16[2048,256]{1,0:T(8,128)(2,1)}, bf16[2048,256]{1,0:T(8,128)(2,1)S(1)}, u32[]{:S(2)}) copy-start(bf16[2048,256]{1,0:T(8,128)(2,1)S(1)} %get-tuple-element.17.hidden_hbm) | copy-start | bytes 3145732
  48.4 1.3 %copy-start.2 = (bf16[2720,256]{1,0:T(8,128)(2,1)S(1)}, bf16[2720,256]{1,0:T(8,128)(2,1)}, u32[]{:S(2)}) copy-start(bf16[2720,256]{1,0:T(8,128)(2,1)} %copy-done.1) | copy-start | bytes 4177924
  49.8 1.2 %copy-start.4 = (bf16[2048,256]{1,0:T(8,128)(2,1)S(1)}, bf16[2048,256]{1,0:T(8,128)(2,1)}, u32[]{:S(2)}) copy-start(bf16[2048,256]{1,0:T(8,128)(2,1)} %copy-done.3) | copy-start | bytes 3145732
  61.1 1.3 %collective-permute-start.4 = (f32[152,128]{1,0:T(8,128)S(1)}, f32[152,128]{1,0:T(8,128)S(1)}, u32[]{:S(2)}, u32[]{:S(2)}) collective-permute-start(f32[152,128]{1,0:T(8,128)S(1)} %slice_bitcast_fusion), channel_id=1, source_target_pairs={{0,1},{1,0},{2,3},{3,2},{4,5},{5,4},{6,7},{7,6},{8,9},{9,8},{10,11... | collective-permute-start | bytes 233480 | tf_op jit(solution)/shard_map/ppermute | solution.py:407
  62.4 5.4 %collective-permute-start.7 = (f32[152,128]{1,0:T(8,128)S(1)}, f32[152,128]{1,0:T(8,128)S(1)}, u32[]{:S(2)}, u32[]{:S(2)}) collective-permute-start(f32[152,128]{1,0:T(8,128)S(1)} %bitcast_add_fusion), channel_id=1, source_target_pairs={{0,24},{8,16},{16,8},{24,0},{1,25},{9,17},{17,9},{25,1},{2,26},{10... | collective-permute-start | bytes 233480 | tf_op jit(solution)/shard_map/ppermute | solution.py:407
  64.9 4.6 %collective-permute-start.6 = (f32[152,128]{1,0:T(8,128)S(1)}, f32[152,128]{1,0:T(8,128)S(1)}, u32[]{:S(2)}, u32[]{:S(2)}) collective-permute-start(f32[152,128]{1,0:T(8,128)S(1)} %bitcast_add_fusion), channel_id=1, source_target_pairs={{0,16},{8,24},{16,0},{24,8},{1,17},{9,25},{17,1},{25,9},{2,18},{10... | collective-permute-start | bytes 233480 | tf_op jit(solution)/shard_map/ppermute | solution.py:407
  65.4 4.4 %collective-permute-start.5 = (f32[152,128]{1,0:T(8,128)S(1)}, f32[152,128]{1,0:T(8,128)S(1)}, u32[]{:S(2)}, u32[]{:S(2)}) collective-permute-start(f32[152,128]{1,0:T(8,128)S(1)} %bitcast_add_fusion), channel_id=1, source_target_pairs={{0,8},{8,0},{16,24},{24,16},{1,9},{9,1},{17,25},{25,17},{2,10},{10... | collective-permute-start | bytes 233480 | tf_op jit(solution)/shard_map/ppermute | solution.py:407
  69.9 6.8 %collective-permute-start.10 = (f32[152,128]{1,0:T(8,128)S(1)}, f32[152,128]{1,0:T(8,128)S(1)}, u32[]{:S(2)}, u32[]{:S(2)}) collective-permute-start(f32[152,128]{1,0:T(8,128)S(1)} %add_add_fusion.1), channel_id=1, source_target_pairs={{0,6},{1,7},{2,4},{3,5},{4,2},{5,3},{6,0},{7,1},{8,14},{9,15},{10,... | collective-permute-start | bytes 233480 | tf_op jit(solution)/shard_map/ppermute | solution.py:407
  70.7 9.9 %collective-permute-start.9 = (f32[152,128]{1,0:T(8,128)S(1)}, f32[152,128]{1,0:T(8,128)S(1)}, u32[]{:S(2)}, u32[]{:S(2)}) collective-permute-start(f32[152,128]{1,0:T(8,128)S(1)} %add_add_fusion.1), channel_id=1, source_target_pairs={{0,4},{1,5},{2,6},{3,7},{4,0},{5,1},{6,2},{7,3},{8,12},{9,13},{10,... | collective-permute-start | bytes 233480 | tf_op jit(solution)/shard_map/ppermute | solution.py:407
  74.4 6.2 %collective-permute-start.8 = (f32[152,128]{1,0:T(8,128)S(1)}, f32[152,128]{1,0:T(8,128)S(1)}, u32[]{:S(2)}, u32[]{:S(2)}) collective-permute-start(f32[152,128]{1,0:T(8,128)S(1)} %add_add_fusion.1), channel_id=1, source_target_pairs={{0,2},{1,3},{2,0},{3,1},{4,6},{5,7},{6,4},{7,5},{8,10},{9,11},{10,... | collective-permute-start | bytes 233480 | tf_op jit(solution)/shard_map/ppermute | solution.py:407
  80.6 1.5 %copy-start.11 = (f32[152,128]{1,0:T(8,128)}, f32[152,128]{1,0:T(8,128)S(1)}, u32[]{:S(2)}) copy-start(f32[152,128]{1,0:T(8,128)S(1)} %add_add_fusion.mine_ref) | copy-start | bytes 233476
  80.6 1.4 %collective-permute-start.11 = (f32[152,128]{1,0:T(8,128)S(1)}, f32[152,128]{1,0:T(8,128)S(1)}, u32[]{:S(2)}, u32[]{:S(2)}) collective-permute-start(f32[152,128]{1,0:T(8,128)S(1)} %add_add_fusion.mine_ref), channel_id=1, source_target_pairs={{0,1},{1,0},{2,3},{3,2},{4,5},{5,4},{6,7},{7,6},{8,9},{9,8},{10,11... | collective-permute-start | bytes 233480 | tf_op jit(solution)/shard_map/ppermute | solution.py:407
  82.1 0.6 copy-start.12
where the time goes:
time: 86.6 us; the launch traced here: 85.9 us
  Pallas kernels  25.3 us (29%)
  starting transfers between devices  22.8 us (26%)
  local copies, waits for them, and re-layouts  19 us (22%)
  waiting for transfers between devices  17.7 us (20%)
    unnamed x37, local copies, waits for them, and re-layouts  15.6 us
    ppermute x8, waiting for transfers between devices, swap(): lax.ppermute(x, axis, [(i, i ^ bit) for i in range(lax.axis_size(axis))])  11.3 us
    pallas_call x1, Pallas kernels, forward(): pl.pallas_call(functools.partial(forward_kernel, channels), out_shape=(ja...  10.2 us
    pallas_call x1, Pallas kernels, backward(): pl.pallas_call(functools.partial(backward_kernel, capacity, channels, nor...  10 us
    ppermute x8, starting transfers between devices, swap(): lax.ppermute(x, axis, [(i, i ^ bit) for i in range(lax.axis_size(axis))])  8.22 us
    ppermute x2, waiting for transfers between devices, pair_swap(): lax.ppermute(jnp.where(even, even_sends, odd_sends), axis, outer)  6.36 us
    ppermute x2, starting transfers between devices, pair_swap(): lax.ppermute(jnp.where(even, odd_sends, even_sends), axis, inner)  5.74 us
    all_to_all x1, starting transfers between devices, per_device(): lax.all_to_all(outgoing, ('face', 'lon'), split_axis=0, concat_axis=0, ti...  4.84 us
  transfers between devices with their start and end apart: 13, of which 7 were waited for; matrix products, arithmetic and copies ran while one was open for 8% of the time, Pallas kernels for 16%

commit v1 on v0

v1 whole, which is shorter than its diff:
```python
import functools
import math

import jax
import jax.numpy as jnp
from jax import lax
from jax.experimental import pallas as pl
from jax.experimental.pallas import tpu as pltpu
from jax.sharding import PartitionSpec as P

NT = (((1,), (1,)), ((), ()))
VMEM_LIMIT = 24 * 1024 * 1024
REGRID_VMEM = 60 * 1024 * 1024


def dot(a, b):
    return jnp.dot(a, b, preferred_element_type=jnp.float32)


def dot_nt(a, b):
    return lax.dot_general(a, b, NT, preferred_element_type=jnp.float32)


def sigmoid(x):
    return 1.0 / (1.0 + jnp.exp(-x))


def regrid_kernel(capacity, tile_ref, row_ref, src_ref, wts_hbm, out_ref, wts_ref, count_ref, slot_ref, head_ref, sems):
    blocks, fields, width = src_ref.shape
    intersections = wts_ref.shape[1]
    devices = out_ref.shape[0]
    chunks = sems.shape[0]
    chunk = blocks // chunks
    copies = [
        pltpu.make_async_copy(
            wts_hbm.at[pl.ds(i * chunk, chunk)], wts_ref.at[pl.ds(i * chunk, chunk)], sems.at[i]
        )
        for i in range(chunks)
    ]
    for copy in copies:
        copy.start()
    head_ref[...] = jnp.full_like(head_ref, -1.0)
    for d in range(devices):
        count_ref[d] = 0
    slot_of_lane = lax.rem(lax.broadcasted_iota(jnp.int32, (1, width), 1) // fields, capacity)
    for s in range(blocks):
        for k in range(intersections):
            tile = tile_ref[k, s]
            slot = count_ref[tile]
            count_ref[tile] = slot + 1
            slot_ref[k, s] = slot
            label = row_ref[k, s].astype(jnp.float32)
            head_ref[pl.ds(tile, 1), :] = jnp.where(slot_of_lane == slot, label, head_ref[pl.ds(tile, 1), :])
    out_ref[...] = jnp.zeros_like(out_ref)
    for d in range(devices):
        out_ref[d, capacity] = jnp.broadcast_to(head_ref[d : d + 1, :], (fields, width)).astype(jnp.bfloat16)
    for i in range(chunks):
        copies[i].wait()
        for s in range(i * chunk, (i + 1) * chunk):
            block = src_ref[s]
            for pair in range(0, intersections, 2):
                both = range(pair, min(pair + 2, intersections))
                contrib = dot(block, jnp.concatenate([wts_ref[s, k] for k in both], axis=1)).astype(jnp.bfloat16)
                for k in both:
                    out_ref[tile_ref[k, s], slot_ref[k, s]] = contrib[:, (k - pair) * width : (k - pair + 1) * width]


def regrid(source, weights, dest_tile, dest_row, devices, capacity):
    blocks, fields, width = source.shape
    intersections = weights.shape[1]
    chunks = math.gcd(blocks, 4)
    smem = pl.BlockSpec(memory_space=pltpu.SMEM)
    vmem = pl.BlockSpec(memory_space=pltpu.VMEM)
    return pl.pallas_call(
        functools.partial(regrid_kernel, capacity),
        out_shape=jax.ShapeDtypeStruct((devices, capacity + 1, fields, width), jnp.bfloat16),
        in_specs=[smem, smem, vmem, pl.BlockSpec(memory_space=pltpu.HBM)],
        out_specs=vmem,
        scratch_shapes=[
            pltpu.VMEM(weights.shape, jnp.bfloat16),
            pltpu.SMEM((devices,), jnp.int32),
            pltpu.SMEM((intersections, blocks), jnp.int32),
            pltpu.VMEM((devices, width), jnp.float32),
            pltpu.SemaphoreType.DMA((chunks,)),
        ],
        compiler_params=pltpu.CompilerParams(vmem_limit_bytes=REGRID_VMEM),
        cost_estimate=pl.CostEstimate(
            flops=2 * weights.size * fields, bytes_accessed=2 * weights.size, transcendentals=0
        ),
        name="regrid",
    )(dest_tile.T, dest_row.T, source, weights)


def lift_tile(prior_ref, edge_ref, side_ref, lift, feat_ref):
    rows, fields, width = prior_ref.shape
    pitch = lift.shape[0]
    for at in range(rows + 2):
        values = edge_ref[0] if at == 0 else edge_ref[1] if at == rows + 1 else prior_ref[at - 1]
        feat_ref[at * pitch : (at + 1) * pitch, :] = dot(lift, values).astype(jnp.bfloat16)
    side = dot(lift, side_ref[...])
    shifted = [side] + [pltpu.roll(side, 256 - i, 1) for i in (1, 2)]
    return jnp.concatenate(shifted, axis=0).astype(jnp.bfloat16)


def forward_kernel(
    prior_ref,
    edge_ref,
    side_ref,
    lift_weight_ref,
    kernel_ref,
    readout_ref,
    act_ref,
    forecast_ref,
    estimate_ref,
    lift_ref,
    back_ref,
    contract_ref,
    feat_ref,
    halo_ref,
    conv_ref,
    hidden_ref,
):
    rows, fields, width = prior_ref.shape
    channels = kernel_ref.shape[1]
    pitch = lift_ref.shape[0]

    taps = [kernel_ref[t].astype(jnp.float32) for t in range(9)]
    for i in range(3):
        back_ref[i * channels : (i + 1) * channels, :] = jnp.concatenate(
            [taps[6 + i], taps[3 + i], taps[i]], axis=1
        ).astype(jnp.bfloat16)
        contract_ref[i] = jnp.concatenate(taps[3 * i : 3 * i + 3], axis=1).astype(jnp.bfloat16)
    empty = jnp.zeros((pitch - channels, 3 * channels), jnp.float32)
    by_input = [piece for i in range(3) for piece in (jnp.concatenate(taps[3 * i : 3 * i + 3], axis=1), empty)]
    conv_ref[...] = jnp.concatenate(by_input, axis=0).T.astype(jnp.bfloat16)
    same = lax.broadcasted_iota(jnp.int32, (fields, pitch - channels), 0) == lax.broadcasted_iota(
        jnp.int32, (fields, pitch - channels), 1
    )
    lift = jnp.concatenate([lift_weight_ref[...].astype(jnp.float32), jnp.where(same, 1.0, 0.0)], axis=1)
    lift_ref[...] = lift.T.astype(jnp.bfloat16)
    readout = readout_ref[...].astype(jnp.float32).T.astype(jnp.bfloat16)

    stack = lift_tile(prior_ref, edge_ref, side_ref, lift_ref[...], feat_ref)
    halo_ref[:, :128] = dot(conv_ref[:channels, :], stack[:, :128])
    halo_ref[:, 128:] = dot(conv_ref[2 * channels :, :], stack[:, 128:])
    lane = lax.broadcasted_iota(jnp.int32, (channels, width), 1)
    for y in range(rows):
        parts = dot(conv_ref[...], feat_ref[y * pitch : (y + 3) * pitch, :])
        left = pltpu.roll(parts[:channels], 1, 1)
        right = pltpu.roll(parts[2 * channels :], width - 1, 1)
        from_left = pltpu.roll(halo_ref[:, :128], (128 - y) % 128, 1)
        from_right = pltpu.roll(halo_ref[:, 128:], 127 - y, 1)
        spread = [jnp.zeros_like(from_left)] * (width // 128 - 1)
        left = jnp.where(lane == 0, jnp.concatenate([from_left] + spread, axis=1), left)
        right = jnp.where(lane == width - 1, jnp.concatenate(spread + [from_right], axis=1), right)
        act = parts[channels : 2 * channels] + left + right
        act_ref[y * channels : (y + 1) * channels, :] = act
        hidden_ref[y * channels : (y + 1) * channels, :] = (act * sigmoid(act)).astype(jnp.bfloat16)
    for y in range(rows):
        increment = dot(readout, hidden_ref[y * channels : (y + 1) * channels, :])
        forecast = prior_ref[y].astype(jnp.float32) + increment
        forecast_ref[y] = forecast
    estimate_ref[...] = jnp.transpose(forecast_ref[...], (1, 0, 2)).astype(jnp.bfloat16)


def forward(prior, edges, sides, lift_weight, kernel, readout):
    rows, fields, width = prior.shape
    channels = kernel.shape[1]
    pitch = channels + 16
    vmem = pl.BlockSpec(memory_space=pltpu.VMEM)
    return pl.pallas_call(
        forward_kernel,
        out_shape=(
            jax.ShapeDtypeStruct((rows * channels, width), jnp.float32),
            jax.ShapeDtypeStruct((rows, fields, width), jnp.float32),
            jax.ShapeDtypeStruct((fields, rows, width), jnp.bfloat16),
            jax.ShapeDtypeStruct((pitch, fields), jnp.bfloat16),
            jax.ShapeDtypeStruct((3 * channels, 3 * channels), jnp.bfloat16),
            jax.ShapeDtypeStruct((3, channels, 3 * channels), jnp.bfloat16),
        ),
        in_specs=[vmem] * 6,
        out_specs=[vmem] * 6,
        scratch_shapes=[
            pltpu.VMEM(((rows + 2) * pitch, width), jnp.bfloat16),
            pltpu.VMEM((channels, 256), jnp.float32),
            pltpu.VMEM((3 * channels, 3 * pitch), jnp.bfloat16),
            pltpu.VMEM((rows * channels, width), jnp.bfloat16),
        ],
        compiler_params=pltpu.CompilerParams(vmem_limit_bytes=VMEM_LIMIT),
        cost_estimate=pl.CostEstimate(
            flops=2 * rows * width * 3 * channels * 3 * pitch,
            bytes_accessed=rows * width * channels * 8,
            transcendentals=rows * width * channels * 2,
        ),
        name="forward",
    )(prior, edges, sides, lift_weight, kernel, readout)


def backward_kernel(
    capacity,
    channels,
    norm,
    arrived_hbm,
    prior_ref,
    edge_ref,
    side_ref,
    lift_ref,
    act_ref,
    forecast_ref,
    readout_ref,
    back_ref,
    contract_ref,
    remapped_ref,
    packed_ref,
    arrived_ref,
    feat_ref,
    hidden_ref,
    misfit_ref,
    slope_ref,
    before_ref,
    after_ref,
    delta_ref,
    sem,
):
    copy = pltpu.make_async_copy(arrived_hbm, arrived_ref, sem)
    copy.start()
    fields, rows, width = remapped_ref.shape
    pitch = lift_ref.shape[0]
    devices = arrived_ref.shape[0]
    per_row = width // 128
    blocks = rows * per_row
    group = 128 // (fields * capacity)

    stack = lift_tile(prior_ref, edge_ref, side_ref, lift_ref[...], feat_ref)
    slope_ref[:channels, :] = jnp.zeros((channels, width), jnp.bfloat16)
    slope_ref[(rows + 1) * channels :, :] = jnp.zeros((channels, width), jnp.bfloat16)
    lane = lax.broadcasted_iota(jnp.int32, (fields, 128), 1)
    sublane = lax.broadcasted_iota(jnp.int32, (fields, 128), 0)
    wanted = lax.broadcasted_iota(jnp.int32, (blocks, fields, 256), 0) * fields

    copy.wait()
    picked = None
    for first in range(0, devices, 2 * group):
        labels, data = [], []
        for half in range(2):
            label = None
            for d in range(group):
                device = first + half * group + d
                mine = arrived_ref[device, capacity * fields : (capacity + 1) * fields, :].astype(jnp.float32)
                label = mine if label is None else jnp.where(lane // (fields * capacity) == d, mine, label)
                data.append(arrived_ref[device, : capacity * fields, :])
            labels.append(label.astype(jnp.int32) * fields + lane % fields - sublane)
        hits = jnp.concatenate(labels, axis=1)[None] == wanted
        hits = jnp.where(hits, 1.0, 0.0).reshape(blocks * fields, 256).astype(jnp.bfloat16)
        part = dot(hits, jnp.concatenate(data, axis=0))
        picked = part if picked is None else picked + part
    picked = picked.astype(jnp.bfloat16).astype(jnp.float32).reshape(rows, per_row, fields, 128)
    for b in range(per_row):
        remapped_ref[:, :, b * 128 : (b + 1) * 128] = jnp.transpose(picked[:, b], (1, 0, 2)).astype(jnp.bfloat16)
    for y in range(rows):
        target = jnp.concatenate([picked[y, b] for b in range(per_row)], axis=1)
        misfit = (forecast_ref[y] - target) * norm
        misfit_ref[:, y * width : (y + 1) * width] = misfit.astype(jnp.bfloat16)

    col = lax.broadcasted_iota(jnp.int32, (channels, width), 1)
    lane = lax.broadcasted_iota(jnp.int32, (channels, 128), 1)
    ends_left = ends_right = jnp.zeros((channels, 128), jnp.float32)
    for y in range(rows):
        here = slice(y * channels, (y + 1) * channels)
        latent = dot(readout_ref[...], misfit_ref[:, y * width : (y + 1) * width])
        act = act_ref[here, :]
        sig = sigmoid(act)
        hidden_ref[here, :] = (act * sig).astype(jnp.bfloat16)
        slope = latent * sig * (1.0 + act * (1.0 - sig))
        slope_ref[(y + 1) * channels : (y + 2) * channels, :] = slope.astype(jnp.bfloat16)
        before_ref[here, :] = jnp.where(col == width - 1, 0.0, pltpu.roll(slope, width - 1, 1)).astype(jnp.bfloat16)
        after_ref[here, :] = jnp.where(col == 0, 0.0, pltpu.roll(slope, 1, 1)).astype(jnp.bfloat16)
        ends_left += pltpu.roll(jnp.where(lane == 0, slope[:, :128], 0.0), y, 1)
        ends_right += pltpu.roll(jnp.where(lane == 127, slope[:, -128:], 0.0), y + 1, 1)

    batch = 4
    total = None
    for first in range(0, rows, batch):
        span = range(first, first + batch)
        features = jnp.concatenate([feat_ref[y * pitch : (y + 3) * pitch, :] for y in span], axis=1)
        trios = jnp.concatenate(
            [
                jnp.concatenate([ref[(y + d) * channels : (y + d + 1) * channels, :] for y in span], axis=1)
                for ref, d in ((before_ref, 0), (slope_ref, 1), (after_ref, 0))
            ],
            axis=0,
        )
        part = dot_nt(features, trios)
        total = part if total is None else total + part
    from_left = dot_nt(stack[:, :128], ends_left.astype(jnp.bfloat16))
    from_right = dot_nt(stack[:, 128:], ends_right.astype(jnp.bfloat16))
    middle = jnp.zeros((3 * pitch, channels), jnp.float32)
    total += jnp.concatenate([from_left, middle, from_right], axis=1)

    delta_ref[:channels, :] = jnp.zeros((channels, width), jnp.bfloat16)
    delta_ref[(rows - 1) * channels :, :] = jnp.zeros((channels, width), jnp.bfloat16)
    for y in range(1, rows - 1):
        parts = dot(back_ref[...], slope_ref[y * channels : (y + 3) * channels, :])
        grad = (
            parts[channels : 2 * channels]
            + pltpu.roll(parts[:channels], width - 1, 1)
            + pltpu.roll(parts[2 * channels :], 1, 1)
        )
        inside = (col > 0) & (col < width - 1)
        delta = jnp.where(inside, grad.astype(jnp.bfloat16).astype(jnp.float32) - grad, 0.0)
        delta_ref[y * channels : (y + 1) * channels, :] = delta.astype(jnp.bfloat16)

    grad_lift = grad_head = jnp.zeros((fields, channels), jnp.float32)
    for first in range(0, rows, batch):
        span = range(first, first + batch)
        here = [slice(y * channels, (y + 1) * channels) for y in span]
        grad_head += dot_nt(
            misfit_ref[:, first * width : (first + batch) * width],
            jnp.concatenate([hidden_ref[h, :] for h in here], axis=1),
        )
        states = jnp.concatenate(
            [feat_ref[(y + 1) * pitch + channels : (y + 2) * pitch, :] for y in span], axis=1
        )
        grad_lift += dot_nt(states, jnp.concatenate([delta_ref[h, :] for h in here], axis=1))[:fields]
    for i in range(3):
        rest = total[i * pitch + channels : i * pitch + channels + fields, :]
        for _ in range(3):
            piece = rest.astype(jnp.bfloat16)
            rest = rest - piece.astype(jnp.float32)
            grad_lift += dot_nt(piece, contract_ref[i])
    taps = [total[i * pitch : i * pitch + channels, :] for i in range(3)]
    half = channels // 2
    last = [t[:, 2 * channels :] for t in taps]
    packed = [t[:, : 2 * channels] for t in taps]
    packed.append(jnp.concatenate(last[:2], axis=1))
    packed.append(jnp.concatenate([last[2][:half], last[2][half:]], axis=1))
    packed.append(jnp.concatenate([grad_lift, grad_head], axis=1))
    packed.append(jnp.zeros((8, 2 * channels), jnp.float32))
    packed = jnp.concatenate(packed, axis=0)
    cut = packed.shape[0] // 2
    odd = lax.rem(lax.axis_index("lon"), 2)
    packed_ref[odd] = packed[:cut]
    packed_ref[1 - odd] = packed[cut:]


def backward(arrived, prior, edges, sides, lift, act, forecast, readout, back, contract, capacity, norm):
    rows, fields, width = forecast.shape
    channels = readout.shape[0]
    pitch = lift.shape[0]
    packed_rows = (3 * channels + channels + channels // 2 + fields + 8) // 2
    vmem = pl.BlockSpec(memory_space=pltpu.VMEM)
    return pl.pallas_call(
        functools.partial(backward_kernel, capacity, channels, norm),
        out_shape=(
            jax.ShapeDtypeStruct((fields, rows, width), jnp.bfloat16),
            jax.ShapeDtypeStruct((2, packed_rows, 2 * channels), jnp.float32),
        ),
        in_specs=[pl.BlockSpec(memory_space=pl.ANY)] + [vmem] * 9,
        out_specs=(vmem, vmem),
        scratch_shapes=[
            pltpu.VMEM(arrived.shape, jnp.bfloat16),
            pltpu.VMEM(((rows + 2) * pitch, width), jnp.bfloat16),
            pltpu.VMEM((rows * channels, width), jnp.bfloat16),
            pltpu.VMEM((fields, rows * width), jnp.bfloat16),
            pltpu.VMEM(((rows + 2) * channels, width), jnp.bfloat16),
            pltpu.VMEM((rows * channels, width), jnp.bfloat16),
            pltpu.VMEM((rows * channels, width), jnp.bfloat16),
            pltpu.VMEM((rows * channels, width), jnp.bfloat16),
            pltpu.SemaphoreType.DMA,
        ],
        compiler_params=pltpu.CompilerParams(vmem_limit_bytes=VMEM_LIMIT),
        cost_estimate=pl.CostEstimate(
            flops=4 * rows * width * 3 * channels * 3 * pitch,
            bytes_accessed=rows * width * channels * 8,
            transcendentals=0,
        ),
        name="backward",
    )(arrived, prior, edges, sides, lift, act, forecast, readout, back, contract)


def unpack_kernel(channels, mine_ref, other_ref, kernel_ref, lift_ref, head_ref):
    odd = lax.rem(lax.axis_index("lon"), 2) == 1
    mine, other = mine_ref[...], other_ref[...]
    packed = jnp.concatenate([jnp.where(odd, other, mine), jnp.where(odd, mine, other)], axis=0)
    half = channels // 2
    for i in range(3):
        block = packed[i * channels : (i + 1) * channels]
        kernel_ref[3 * i] = block[:, :channels]
        kernel_ref[3 * i + 1] = block[:, channels:]
    block = packed[3 * channels : 4 * channels]
    kernel_ref[2] = block[:, :channels]
    kernel_ref[5] = block[:, channels:]
    block = packed[4 * channels : 4 * channels + half]
    kernel_ref[8, :half] = block[:, :channels]
    kernel_ref[8, half:] = block[:, channels:]
    block = packed[4 * channels + half : 4 * channels + half + lift_ref.shape[0]]
    lift_ref[...] = block[:, :channels]
    head_ref[...] = block[:, channels:]


def unpack(mine, other, channels, fields):
    return pl.pallas_call(
        functools.partial(unpack_kernel, channels),
        out_shape=(
            jax.ShapeDtypeStruct((9, channels, channels), jnp.float32),
            jax.ShapeDtypeStruct((fields, channels), jnp.float32),
            jax.ShapeDtypeStruct((fields, channels), jnp.float32),
        ),
        compiler_params=pltpu.CompilerParams(vmem_limit_bytes=VMEM_LIMIT),
        name="unpack",
    )(mine, other)


def swap(x, axis, bit):
    return lax.ppermute(x, axis, [(i, i ^ bit) for i in range(lax.axis_size(axis))])


def sum_over(x, axis, low, high):
    if high // low == 4:
        a, b, c = (swap(x, axis, k * low) for k in (1, 2, 3))
        return (x + a) + (b + c)
    bit = low
    while bit < high:
        x = x + swap(x, axis, bit)
        bit *= 2
    return x


def pair_swap(even_sends, odd_sends, axis, periodic):
    count = lax.axis_size(axis)
    even = lax.rem(lax.axis_index(axis), 2) == 0
    inner = [(i, i ^ 1) for i in range(count)]
    outer = []
    for i in range(1, count, 2):
        if i + 1 < count or periodic:
            outer += [(i, (i + 1) % count), ((i + 1) % count, i)]
    got_inner = lax.ppermute(jnp.where(even, odd_sends, even_sends), axis, inner)
    got_outer = lax.ppermute(jnp.where(even, even_sends, odd_sends), axis, outer)
    return jnp.where(even, got_outer, got_inner), jnp.where(even, got_inner, got_outer)


def per_device(
    source,
    intersection_weight,
    dest_tile,
    dest_row,
    prior_state,
    lift_weight,
    kernel,
    readout_weights,
):
    face_count = lax.axis_size("face")
    lon_count = lax.axis_size("lon")
    devices = face_count * lon_count
    src_blocks, intersections = dest_tile.shape
    fields, rows, width = prior_state.shape
    channels = kernel.shape[1]
    capacity = max(2, 2 * src_blocks * intersections // devices)
    norm = 1.0 / math.sqrt(rows * face_count * width * lon_count)

    outgoing = regrid(source, intersection_weight, dest_tile, dest_row, devices, capacity)
    outgoing, prior_state, kernel, lift_weight, readout_weights = lax.optimization_barrier(
        (outgoing, prior_state, kernel, lift_weight, readout_weights)
    )
    arrived = lax.all_to_all(outgoing, ("face", "lon"), split_axis=0, concat_axis=0, tiled=True)
    arrived = arrived.reshape(devices, (capacity + 1) * fields, source.shape[2])

    prior = prior_state.transpose(1, 0, 2)
    top, bottom = pair_swap(prior[0], prior[rows - 1], "face", False)
    columns = [
        jnp.pad(
            jnp.concatenate([top[:, at : at + 1], prior_state[:, :, at], bottom[:, at : at + 1]], axis=1),
            ((0, 0), (0, 128 - rows - 2)),
        )
        for at in (0, width - 1)
    ]
    left, right = pair_swap(columns[0], columns[1], "lon", True)

    edges = jnp.stack([top, bottom])
    sides = jnp.concatenate([left, right], axis=1)
    act, forecast, estimate, lift, back, contract = forward(
        prior, edges, sides, lift_weight, kernel, readout_weights
    )
    remapped, packed = backward(
        arrived, prior, edges, sides, lift, act, forecast, readout_weights, back, contract, capacity, norm
    )
    part = packed[0] + swap(packed[1], "lon", 1)
    part = sum_over(part, "face", 1, face_count)
    part = sum_over(part, "lon", 2, lon_count)
    grad_kernel, grad_lift, grad_head = unpack(part, swap(part, "lon", 1), channels, fields)
    return (
        remapped,
        estimate,
        grad_lift,
        grad_kernel,
        grad_head.T,
    )


def solution(mesh):
    return jax.shard_map(
        per_device,
        mesh=mesh,
        in_specs=(
            P(("face", "lon"), None, None),
            P(("face", "lon"), None, None, None),
            P(("face", "lon"), None),
            P(("face", "lon"), None),
            P(None, "face", "lon"),
            P(),
            P(),
            P(),
        ),
        out_specs=(P(None, "face", "lon"), P(None, "face", "lon"), P(), P(), P()),
        check_vma=False,
    )
```

time: 86.6 us -> 57.8 us (0.67)
  local copies, waits for them, and re-layouts: 19 us -> 0.6 us
  Pallas kernels: 25.3 us -> 14.5 us
  waiting for transfers between devices: 17.7 us -> 18.6 us
    unnamed x37 -> x8, local copies, waits for them, and re-layouts: 15.6 us -> 0.02 us
    pallas_call x2, Pallas kernels: 13.5 us -> 7.75 us  [the longest x1 4.22 us: regrid(): pl.pallas_call(functools.partial(regrid_kernel, capacity), out_shape=jax....]
    pallas_call x1, Pallas kernels: 10 us -> 5.93 us  [backward(): pl.pallas_call(functools.partial(backward_kernel, capacity, channels, nor...]
    all_to_all x1, starting transfers between devices: 4.84 us -> 7.3 us  [per_device(): lax.all_to_all(outgoing, ('face', 'lon'), split_axis=0, concat_axis=0, ti...]
    ppermute x2, waiting for transfers between devices: 6.36 us -> 4.3 us  [pair_swap(): lax.ppermute(jnp.where(even, even_sends, odd_sends), axis, outer)]
    reshape x6 -> x0, local copies, waits for them, and re-layouts: 1.54 us -> none  [the longest x1 0.78 us: per_device(): conv = jnp.pad(taps.transpose(1, 3, 0, 2), ((0, 0), (0, 0), (0, 0), (0, p...]
    ppermute x2, waiting for transfers between devices: 0.01 us -> 1.33 us  [pair_swap(): lax.ppermute(jnp.where(even, odd_sends, even_sends), axis, inner)]
    ppermute x8, waiting for transfers between devices: 11.3 us -> 12.6 us  [swap(): lax.ppermute(x, axis, [(i, i ^ bit) for i in range(lax.axis_size(axis))])]
  transfers between devices with their start and end apart: 13 -> 13, of which waited for: 7 -> 9; matrix products, arithmetic and copies ran while one was open for 8% -> 1% of each run, Pallas kernels for 16% -> 6%
where the time goes in v1:
time: 57.8 us; the launch traced here: 57.6 us
  starting transfers between devices  22.8 us (39%)
  waiting for transfers between devices  18.6 us (32%)
  Pallas kernels  14.5 us (25%)
  between operations  0.83 us (1%)
  local copies, waits for them, and re-layouts  0.6 us (1%)
    ppermute x8, waiting for transfers between devices, swap(): lax.ppermute(x, axis, [(i, i ^ bit) for i in range(lax.axis_size(axis))])  12.6 us
    ppermute x8, starting transfers between devices, swap(): lax.ppermute(x, axis, [(i, i ^ bit) for i in range(lax.axis_size(axis))])  8.15 us
    all_to_all x1, starting transfers between devices, per_device(): lax.all_to_all(outgoing, ('face', 'lon'), split_axis=0, concat_axis=0, ti...  7.3 us
    pallas_call x1, Pallas kernels, backward(): pl.pallas_call(functools.partial(backward_kernel, capacity, channels, nor...  5.93 us
    ppermute x2, starting transfers between devices, pair_swap(): lax.ppermute(jnp.where(even, odd_sends, even_sends), axis, inner)  4.55 us
    ppermute x2, waiting for transfers between devices, pair_swap(): lax.ppermute(jnp.where(even, even_sends, odd_sends), axis, outer)  4.3 us
    pallas_call x1, Pallas kernels, regrid(): pl.pallas_call(functools.partial(regrid_kernel, capacity), out_shape=jax....  4.22 us
    pallas_call x1, Pallas kernels, forward(): pl.pallas_call(forward_kernel, out_shape=(jax.ShapeDtypeStruct((rows * ch...  3.53 us
  transfers between devices with their start and end apart: 13, of which 9 were waited for; matrix products, arithmetic and copies ran while one was open for 1% of the time, Pallas kernels for 6%

profile of v1, /device:TPU:0, one launch (start us, length us, event | category | flops | bytes accessed | tf_op | source)
XLA Modules:
  0.0 57.6 jit_solution(14261631324254280284)
XLA Ops:
  0.7 4.2 %regrid.1 = bf16[32,9,8,128]{3,2,1,0:T(8,128)(2,1)} custom-call(s32[4,32]{1,0:T(4,128)} %bitcast.27, s32[4,32]{1,0:T(4,128)} %bitcast.28, bf16[32,8,128]{2,1,0:T(8,128)(2,1)} %src_ref.1, bf16[32,4,128,128]{3,2,1,0:T(8,128)(2,1)} %wts_hbm.1), custom_call_target="tpu_custom_call" | custom-call | flops 33554432 | bytes 4194304 | tf_op jit(solution)/shard_map/regrid/pallas_call | solution.py:74
  4.9 7.3 %all-to-all-start = ((bf16[32,9,8,128]{3,2,1,0:T(8,128)(2,1)}), bf16[32,9,8,128]{3,2,1,0:T(8,128)(2,1)S(1)}, u32[]{:S(2)}, u32[]{:S(2)}) async-start(bf16[32,9,8,128]{3,2,1,0:T(8,128)(2,1)} %regrid.1), calls=%async_computation | async-start | bytes 1179648 | tf_op jit(solution)/shard_map/all_to_all | solution.py:465
  12.2 0.1 copy.19
  12.3 0.7 %collective-permute-start = (bf16[8,256]{1,0:T(8,128)(2,1)S(1)}, bf16[8,256]{1,0:T(8,128)(2,1)S(1)}, u32[]{:S(2)}, u32[]{:S(2)}) collective-permute-start(bf16[8,256]{1,0:T(8,128)(2,1)S(1)} %get-tuple-element.39), channel_id=1, source_target_pairs={{8,16},{16,8},{9,17},{17,9},{10,18},{18,10},{11,19},{19,11},{12,20... | collective-permute-start | bytes 12296 | tf_op jit(solution)/shard_map/ppermute | solution.py:438
  13.0 4.5 %collective-permute-start.1 = (bf16[8,256]{1,0:T(8,128)(2,1)S(1)}, bf16[8,256]{1,0:T(8,128)(2,1)S(1)}, u32[]{:S(2)}, u32[]{:S(2)}) collective-permute-start(bf16[8,256]{1,0:T(8,128)(2,1)S(1)} %get-tuple-element.40), channel_id=1, source_target_pairs={{0,8},{8,0},{16,24},{24,16},{1,9},{9,1},{17,25},{25,17},{2,10},{10... | collective-permute-start | bytes 12296 | tf_op jit(solution)/shard_map/ppermute | solution.py:437
  17.5 0.3 copy.14
  17.9 0.1 copy.16.readout_ref
  18.0 1.3 %collective-permute-done.1 = bf16[8,256]{1,0:T(8,128)(2,1)S(1)} collective-permute-done((bf16[8,256]{1,0:T(8,128)(2,1)S(1)}, bf16[8,256]{1,0:T(8,128)(2,1)S(1)}, u32[]{:S(2)}, u32[]{:S(2)}) %collective-permute-start.1) | collective-permute-done | bytes 4128 | tf_op jit(solution)/shard_map/ppermute | solution.py:437
  19.3 0.1 fusion.10
  19.4 0.1 broadcast_select_fusion.5
  19.5 2.2 %collective-permute-start.2 = (bf16[8,128]{1,0:T(8,128)(2,1)S(1)}, bf16[8,128]{1,0:T(8,128)(2,1)S(1)}, u32[]{:S(2)}, u32[]{:S(2)}) collective-permute-start(bf16[8,128]{1,0:T(8,128)(2,1)S(1)} %get-tuple-element.41), channel_id=1, source_target_pairs={{1,2},{2,1},{3,4},{4,3},{5,6},{6,5},{7,0},{0,7},{9,10},{10,9},{11,... | collective-permute-start | bytes 6152 | tf_op jit(solution)/shard_map/ppermute | solution.py:438
  21.7 0.0 collective-permute-start.3
  21.7 4.3 %collective-permute-done.2 = bf16[8,128]{1,0:T(8,128)(2,1)S(1)} collective-permute-done((bf16[8,128]{1,0:T(8,128)(2,1)S(1)}, bf16[8,128]{1,0:T(8,128)(2,1)S(1)}, u32[]{:S(2)}, u32[]{:S(2)}) %collective-permute-start.2) | collective-permute-done | bytes 2080 | tf_op jit(solution)/shard_map/ppermute | solution.py:438
  26.0 0.0 collective-permute-done.3
  26.0 3.5 %forward.1 = (f32[2048,256]{1,0:T(8,128)S(1)}, f32[32,8,256]{2,1,0:T(8,128)S(1)}, bf16[8,32,256]{2,1,0:T(8,128)(2,1)}, bf16[80,8]{1,0:T(8,128)(2,1)S(1)}, bf16[1...) custom-call(bf16[32,8,256]{2,1,0:T(8,128)(2,1)S(1)} %bitcast.23, ...), custom_call_target="tpu_custom_call" | custom-call | flops 754974720 | bytes 4194304 | tf_op jit(solution)/shard_map/forward/pallas_call | solution.py:171
  29.6 0.4 all-to-all-done
  30.0 5.9 %backward.1 = (bf16[8,32,256]{2,1,0:T(8,128)(2,1)}, f32[2,152,128]{2,1,0:T(8,128)S(1)}) custom-call(bf16[32,72,128]{2,1,0:T(8,128)(2,1)S(1)} %bitcast.21, bf16[32,8,256]{2,1,0:T(8,128)(2,1)S(1)} %bitcast.24, bf16[2,8,256]{2,1,0:T(8,128)(2,1)S(1)} %pad_maximum_fusion.edge_ref, bf16[8,256]{1,0:T(8,128)(2,1)S(1)} %pad_maximum_fusion.1.side_ref, ...), custom_call_target="tpu_custom_call" | custom-call | flops 1509949440 | bytes 4194304 | tf_op jit(solution)/shard_map/backward/pallas_call | solution.py:352
  36.0 0.1 collective-permute-start.4
  36.0 1.3 %collective-permute-done.4 = f32[152,128]{1,0:T(8,128)S(1)} collective-permute-done((f32[152,128]{1,0:T(8,128)S(1)}, f32[152,128]{1,0:T(8,128)S(1)}, u32[]{:S(2)}, u32[]{:S(2)}) %collective-permute-start.4) | collective-permute-done | bytes 77856 | tf_op jit(solution)/shard_map/ppermute | solution.py:415
  37.3 2.1 %collective-permute-start.7 = (f32[152,128]{1,0:T(8,128)S(1)}, f32[152,128]{1,0:T(8,128)S(1)}, u32[]{:S(2)}, u32[]{:S(2)}) collective-permute-start(f32[152,128]{1,0:T(8,128)S(1)} %bitcast_add_fusion), channel_id=1, source_target_pairs={{0,24},{8,16},{16,8},{24,0},{1,25},{9,17},{17,9},{25,1},{2,26},{10... | collective-permute-start | bytes 233480 | tf_op jit(solution)/shard_map/ppermute | solution.py:415
  39.4 0.5 collective-permute-start.6
  39.9 1.0 %collective-permute-start.5 = (f32[152,128]{1,0:T(8,128)S(1)}, f32[152,128]{1,0:T(8,128)S(1)}, u32[]{:S(2)}, u32[]{:S(2)}) collective-permute-start(f32[152,128]{1,0:T(8,128)S(1)} %bitcast_add_fusion), channel_id=1, source_target_pairs={{0,8},{8,0},{16,24},{24,16},{1,9},{9,1},{17,25},{25,17},{2,10},{10... | collective-permute-start | bytes 233480 | tf_op jit(solution)/shard_map/ppermute | solution.py:415
  40.9 1.9 %collective-permute-done.7 = f32[152,128]{1,0:T(8,128)S(1)} collective-permute-done((f32[152,128]{1,0:T(8,128)S(1)}, f32[152,128]{1,0:T(8,128)S(1)}, u32[]{:S(2)}, u32[]{:S(2)}) %collective-permute-start.7) | collective-permute-done | bytes 77856 | tf_op jit(solution)/shard_map/ppermute | solution.py:415
  42.8 1.6 %collective-permute-done.6 = f32[152,128]{1,0:T(8,128)S(1)} collective-permute-done((f32[152,128]{1,0:T(8,128)S(1)}, f32[152,128]{1,0:T(8,128)S(1)}, u32[]{:S(2)}, u32[]{:S(2)}) %collective-permute-start.6) | collective-permute-done | bytes 77856 | tf_op jit(solution)/shard_map/ppermute | solution.py:415
  44.4 0.9 %collective-permute-start.10 = (f32[152,128]{1,0:T(8,128)S(1)}, f32[152,128]{1,0:T(8,128)S(1)}, u32[]{:S(2)}, u32[]{:S(2)}) collective-permute-start(f32[152,128]{1,0:T(8,128)S(1)} %add_add_fusion.1), channel_id=1, source_target_pairs={{0,6},{1,7},{2,4},{3,5},{4,2},{5,3},{6,0},{7,1},{8,14},{9,15},{10,... | collective-permute-start | bytes 233480 | tf_op jit(solution)/shard_map/ppermute | solution.py:415
  45.3 3.5 %collective-permute-start.9 = (f32[152,128]{1,0:T(8,128)S(1)}, f32[152,128]{1,0:T(8,128)S(1)}, u32[]{:S(2)}, u32[]{:S(2)}) collective-permute-start(f32[152,128]{1,0:T(8,128)S(1)} %add_add_fusion.1), channel_id=1, source_target_pairs={{0,4},{1,5},{2,6},{3,7},{4,0},{5,1},{6,2},{7,3},{8,12},{9,13},{10,... | collective-permute-start | bytes 233480 | tf_op jit(solution)/shard_map/ppermute | solution.py:415
  48.8 0.0 collective-permute-start.8
  48.8 2.4 %collective-permute-done.10 = f32[152,128]{1,0:T(8,128)S(1)} collective-permute-done((f32[152,128]{1,0:T(8,128)S(1)}, f32[152,128]{1,0:T(8,128)S(1)}, u32[]{:S(2)}, u32[]{:S(2)}) %collective-permute-start.10) | collective-permute-done | bytes 77856 | tf_op jit(solution)/shard_map/ppermute | solution.py:415
  51.2 4.1 %collective-permute-done.9 = f32[152,128]{1,0:T(8,128)S(1)} collective-permute-done((f32[152,128]{1,0:T(8,128)S(1)}, f32[152,128]{1,0:T(8,128)S(1)}, u32[]{:S(2)}, u32[]{:S(2)}) %collective-permute-start.9) | collective-permute-done | bytes 77856 | tf_op jit(solution)/shard_map/ppermute | solution.py:415
  55.4 0.1 collective-permute-start.11
  55.5 1.3 %collective-permute-done.11.other_ref = f32[152,128]{1,0:T(8,128)S(1)} collective-permute-done((f32[152,128]{1,0:T(8,128)S(1)}, f32[152,128]{1,0:T(8,128)S(1)}, u32[]{:S(2)}, u32[]{:S(2)}) %collective-permute-start.11) | collective-permute-done | bytes 77856 | tf_op jit(solution)/shard_map/ppermute | solution.py:415
  56.8 0.8 %unpack.1 = (f32[9,64,64]{2,1,0:T(8,128)}, f32[8,64]{1,0:T(8,128)}, f32[8,64]{1,0:T(8,128)}) custom-call(f32[152,128]{1,0:T(8,128)S(1)} %add_add_fusion.mine_ref, f32[152,128]{1,0:T(8,128)S(1)} %collective-permute-done.11.other_ref), custom_call_target="tpu_custom_call" | custom-call | tf_op jit(solution)/shard_map/unpack/pallas_call | solution.py:402
  (21 shorter events, 0.1 us)
Async XLA Ops:
  0.6 17.3 %copy-start.3 = (bf16[64,8]{0,1:T(8,128)(2,1)S(1)}, bf16[64,8]{0,1:T(8,128)(2,1)}, u32[]{:S(2)}) copy-start(bf16[64,8]{0,1:T(8,128)(2,1)} %param.15) | copy-start | bytes 3076
  0.6 25.4 %copy-start = (bf16[9,64,64]{2,1,0:T(8,128)(2,1)S(1)}, bf16[9,64,64]{2,1,0:T(8,128)(2,1)}, u32[]{:S(2)}) copy-start(bf16[9,64,64]{2,1,0:T(8,128)(2,1)} %kernel_ref) | copy-start | bytes 221188
  0.7 25.4 %copy-start.1 = (bf16[8,64]{1,0:T(8,128)(2,1)S(1)}, bf16[8,64]{1,0:T(8,128)(2,1)}, u32[]{:S(2)}) copy-start(bf16[8,64]{1,0:T(8,128)(2,1)} %lift_weight_ref) | copy-start | bytes 3076
  0.7 11.6 %copy-start.2 = (bf16[8,32,256]{2,1,0:T(8,128)(2,1)S(1)}, bf16[8,32,256]{2,1,0:T(8,128)(2,1)}, u32[]{:S(2)}) copy-start(bf16[8,32,256]{2,1,0:T(8,128)(2,1)} %param.12) | copy-start | bytes 393220
  4.9 25.1 %all-to-all-start = ((bf16[32,9,8,128]{3,2,1,0:T(8,128)(2,1)}), bf16[32,9,8,128]{3,2,1,0:T(8,128)(2,1)S(1)}, u32[]{:S(2)}, u32[]{:S(2)}) async-start(bf16[32,9,8,128]{3,2,1,0:T(8,128)(2,1)} %regrid.1), calls=%async_computation | async-start | bytes 1179648 | tf_op jit(solution)/shard_map/all_to_all | solution.py:465
  12.3 5.7 %collective-permute-start = (bf16[8,256]{1,0:T(8,128)(2,1)S(1)}, bf16[8,256]{1,0:T(8,128)(2,1)S(1)}, u32[]{:S(2)}, u32[]{:S(2)}) collective-permute-start(bf16[8,256]{1,0:T(8,128)(2,1)S(1)} %get-tuple-element.39), channel_id=1, source_target_pairs={{8,16},{16,8},{9,17},{17,9},{10,18},{18,10},{11,19},{19,11},{12,20... | collective-permute-start | bytes 12296 | tf_op jit(solution)/shard_map/ppermute | solution.py:438
  13.0 6.3 %collective-permute-start.1 = (bf16[8,256]{1,0:T(8,128)(2,1)S(1)}, bf16[8,256]{1,0:T(8,128)(2,1)S(1)}, u32[]{:S(2)}, u32[]{:S(2)}) collective-permute-start(bf16[8,256]{1,0:T(8,128)(2,1)S(1)} %get-tuple-element.40), channel_id=1, source_target_pairs={{0,8},{8,0},{16,24},{24,16},{1,9},{9,1},{17,25},{25,17},{2,10},{10... | collective-permute-start | bytes 12296 | tf_op jit(solution)/shard_map/ppermute | solution.py:437
  19.5 6.5 %collective-permute-start.2 = (bf16[8,128]{1,0:T(8,128)(2,1)S(1)}, bf16[8,128]{1,0:T(8,128)(2,1)S(1)}, u32[]{:S(2)}, u32[]{:S(2)}) collective-permute-start(bf16[8,128]{1,0:T(8,128)(2,1)S(1)} %get-tuple-element.41), channel_id=1, source_target_pairs={{1,2},{2,1},{3,4},{4,3},{5,6},{6,5},{7,0},{0,7},{9,10},{10,9},{11,... | collective-permute-start | bytes 6152 | tf_op jit(solution)/shard_map/ppermute | solution.py:438
  21.7 4.3 %collective-permute-start.3 = (bf16[8,128]{1,0:T(8,128)(2,1)S(1)}, bf16[8,128]{1,0:T(8,128)(2,1)S(1)}, u32[]{:S(2)}, u32[]{:S(2)}) collective-permute-start(bf16[8,128]{1,0:T(8,128)(2,1)S(1)} %get-tuple-element.42), channel_id=1, source_target_pairs={{0,1},{1,0},{2,3},{3,2},{4,5},{5,4},{6,7},{7,6},{8,9},{9,8},{10,11... | collective-permute-start | bytes 6152 | tf_op jit(solution)/shard_map/ppermute | solution.py:437
  36.0 1.3 %collective-permute-start.4 = (f32[152,128]{1,0:T(8,128)S(1)}, f32[152,128]{1,0:T(8,128)S(1)}, u32[]{:S(2)}, u32[]{:S(2)}) collective-permute-start(f32[152,128]{1,0:T(8,128)S(1)} %slice_bitcast_fusion), channel_id=1, source_target_pairs={{0,1},{1,0},{2,3},{3,2},{4,5},{5,4},{6,7},{7,6},{8,9},{9,8},{10,11... | collective-permute-start | bytes 233480 | tf_op jit(solution)/shard_map/ppermute | solution.py:415
  37.3 5.5 %collective-permute-start.7 = (f32[152,128]{1,0:T(8,128)S(1)}, f32[152,128]{1,0:T(8,128)S(1)}, u32[]{:S(2)}, u32[]{:S(2)}) collective-permute-start(f32[152,128]{1,0:T(8,128)S(1)} %bitcast_add_fusion), channel_id=1, source_target_pairs={{0,24},{8,16},{16,8},{24,0},{1,25},{9,17},{17,9},{25,1},{2,26},{10... | collective-permute-start | bytes 233480 | tf_op jit(solution)/shard_map/ppermute | solution.py:415
  39.4 5.0 %collective-permute-start.6 = (f32[152,128]{1,0:T(8,128)S(1)}, f32[152,128]{1,0:T(8,128)S(1)}, u32[]{:S(2)}, u32[]{:S(2)}) collective-permute-start(f32[152,128]{1,0:T(8,128)S(1)} %bitcast_add_fusion), channel_id=1, source_target_pairs={{0,16},{8,24},{16,0},{24,8},{1,17},{9,25},{17,1},{25,9},{2,18},{10... | collective-permute-start | bytes 233480 | tf_op jit(solution)/shard_map/ppermute | solution.py:415
  39.9 4.5 %collective-permute-start.5 = (f32[152,128]{1,0:T(8,128)S(1)}, f32[152,128]{1,0:T(8,128)S(1)}, u32[]{:S(2)}, u32[]{:S(2)}) collective-permute-start(f32[152,128]{1,0:T(8,128)S(1)} %bitcast_add_fusion), channel_id=1, source_target_pairs={{0,8},{8,0},{16,24},{24,16},{1,9},{9,1},{17,25},{25,17},{2,10},{10... | collective-permute-start | bytes 233480 | tf_op jit(solution)/shard_map/ppermute | solution.py:415
  44.4 6.9 %collective-permute-start.10 = (f32[152,128]{1,0:T(8,128)S(1)}, f32[152,128]{1,0:T(8,128)S(1)}, u32[]{:S(2)}, u32[]{:S(2)}) collective-permute-start(f32[152,128]{1,0:T(8,128)S(1)} %add_add_fusion.1), channel_id=1, source_target_pairs={{0,6},{1,7},{2,4},{3,5},{4,2},{5,3},{6,0},{7,1},{8,14},{9,15},{10,... | collective-permute-start | bytes 233480 | tf_op jit(solution)/shard_map/ppermute | solution.py:415
  45.3 10.1 %collective-permute-start.9 = (f32[152,128]{1,0:T(8,128)S(1)}, f32[152,128]{1,0:T(8,128)S(1)}, u32[]{:S(2)}, u32[]{:S(2)}) collective-permute-start(f32[152,128]{1,0:T(8,128)S(1)} %add_add_fusion.1), channel_id=1, source_target_pairs={{0,4},{1,5},{2,6},{3,7},{4,0},{5,1},{6,2},{7,3},{8,12},{9,13},{10,... | collective-permute-start | bytes 233480 | tf_op jit(solution)/shard_map/ppermute | solution.py:415
  48.8 6.6 %collective-permute-start.8 = (f32[152,128]{1,0:T(8,128)S(1)}, f32[152,128]{1,0:T(8,128)S(1)}, u32[]{:S(2)}, u32[]{:S(2)}) collective-permute-start(f32[152,128]{1,0:T(8,128)S(1)} %add_add_fusion.1), channel_id=1, source_target_pairs={{0,2},{1,3},{2,0},{3,1},{4,6},{5,7},{6,4},{7,5},{8,10},{9,11},{10,... | collective-permute-start | bytes 233480 | tf_op jit(solution)/shard_map/ppermute | solution.py:415
  55.4 1.3 %collective-permute-start.11 = (f32[152,128]{1,0:T(8,128)S(1)}, f32[152,128]{1,0:T(8,128)S(1)}, u32[]{:S(2)}, u32[]{:S(2)}) collective-permute-start(f32[152,128]{1,0:T(8,128)S(1)} %add_add_fusion.mine_ref), channel_id=1, source_target_pairs={{0,1},{1,0},{2,3},{3,2},{4,5},{5,4},{6,7},{7,6},{8,9},{9,8},{10,11... | collective-permute-start | bytes 233480 | tf_op jit(solution)/shard_map/ppermute | solution.py:415

commit v2 on v1

v2 whole, which is shorter than its diff:
```python
import functools
import math

import jax
import jax.numpy as jnp
from jax import lax
from jax.experimental import pallas as pl
from jax.experimental.pallas import tpu as pltpu
from jax.sharding import PartitionSpec as P

NT = (((1,), (1,)), ((), ()))
VMEM_LIMIT = 24 * 1024 * 1024
REGRID_VMEM = 60 * 1024 * 1024


def dot(a, b):
    return jnp.dot(a, b, preferred_element_type=jnp.float32)


def dot_nt(a, b):
    return lax.dot_general(a, b, NT, preferred_element_type=jnp.float32)


def sigmoid(x):
    return 1.0 / (1.0 + jnp.exp(-x))


def regrid_kernel(capacity, tile_ref, row_ref, src_ref, wts_hbm, out_ref, wts_ref, count_ref, slot_ref, head_ref, sems):
    blocks, fields, width = src_ref.shape
    intersections = wts_ref.shape[1]
    devices = out_ref.shape[0]
    chunks = sems.shape[0]
    chunk = blocks // chunks
    copies = [
        pltpu.make_async_copy(
            wts_hbm.at[pl.ds(i * chunk, chunk)], wts_ref.at[pl.ds(i * chunk, chunk)], sems.at[i]
        )
        for i in range(chunks)
    ]
    for copy in copies:
        copy.start()
    head_ref[...] = jnp.full_like(head_ref, -1.0)
    for d in range(devices):
        count_ref[d] = 0
    slot_of_lane = lax.rem(lax.broadcasted_iota(jnp.int32, (1, width), 1), capacity)
    for s in range(blocks):
        for k in range(intersections):
            tile = tile_ref[k, s]
            slot = count_ref[tile]
            count_ref[tile] = slot + 1
            slot_ref[k, s] = slot
            label = row_ref[k, s].astype(jnp.float32)
            head_ref[pl.ds(tile, 1), :] = jnp.where(slot_of_lane == slot, label, head_ref[pl.ds(tile, 1), :])
    out_ref[...] = jnp.zeros_like(out_ref)
    for d in range(devices):
        out_ref[d, capacity] = jnp.broadcast_to(head_ref[d : d + 1, :], (fields, width)).astype(jnp.bfloat16)
    for i in range(chunks):
        copies[i].wait()
        for s in range(i * chunk, (i + 1) * chunk):
            block = src_ref[s]
            for pair in range(0, intersections, 2):
                both = range(pair, min(pair + 2, intersections))
                contrib = dot(block, jnp.concatenate([wts_ref[s, k] for k in both], axis=1)).astype(jnp.bfloat16)
                for k in both:
                    out_ref[tile_ref[k, s], slot_ref[k, s]] = contrib[:, (k - pair) * width : (k - pair + 1) * width]


def regrid(source, weights, dest_tile, dest_row, devices, capacity):
    blocks, fields, width = source.shape
    intersections = weights.shape[1]
    chunks = math.gcd(blocks, 4)
    smem = pl.BlockSpec(memory_space=pltpu.SMEM)
    vmem = pl.BlockSpec(memory_space=pltpu.VMEM)
    return pl.pallas_call(
        functools.partial(regrid_kernel, capacity),
        out_shape=jax.ShapeDtypeStruct((devices, capacity + 1, fields, width), jnp.bfloat16),
        in_specs=[smem, smem, vmem, pl.BlockSpec(memory_space=pl.ANY)],
        out_specs=vmem,
        scratch_shapes=[
            pltpu.VMEM(weights.shape, jnp.bfloat16),
            pltpu.SMEM((devices,), jnp.int32),
            pltpu.SMEM((intersections, blocks), jnp.int32),
            pltpu.VMEM((devices, width), jnp.float32),
            pltpu.SemaphoreType.DMA((chunks,)),
        ],
        compiler_params=pltpu.CompilerParams(vmem_limit_bytes=REGRID_VMEM),
        cost_estimate=pl.CostEstimate(
            flops=2 * weights.size * fields, bytes_accessed=2 * weights.size, transcendentals=0
        ),
        name="regrid",
    )(dest_tile.T, dest_row.T, source, weights)


def lift_rows(prior_ref, edge_ref, lift, feat_ref):
    rows = prior_ref.shape[0]
    pitch = lift.shape[0]
    for at in range(rows + 2):
        values = edge_ref[0] if at == 0 else edge_ref[1] if at == rows + 1 else prior_ref[at - 1]
        feat_ref[at * pitch : (at + 1) * pitch, :] = dot(lift, values).astype(jnp.bfloat16)


def convolve_kernel(
    prior_ref,
    edge_ref,
    lift_weight_ref,
    kernel_ref,
    act_ref,
    lift_ref,
    conv_ref,
    back_ref,
    contract_ref,
    feat_ref,
):
    rows, fields, width = prior_ref.shape
    channels = kernel_ref.shape[1]
    pitch = lift_ref.shape[0]

    taps = [kernel_ref[t].astype(jnp.float32) for t in range(9)]
    for i in range(3):
        back_ref[i * channels : (i + 1) * channels, :] = jnp.concatenate(
            [taps[6 + i], taps[3 + i], taps[i]], axis=1
        ).astype(jnp.bfloat16)
        contract_ref[i] = jnp.concatenate(taps[3 * i : 3 * i + 3], axis=1).astype(jnp.bfloat16)
    empty = jnp.zeros((pitch - channels, 3 * channels), jnp.float32)
    by_input = [piece for i in range(3) for piece in (jnp.concatenate(taps[3 * i : 3 * i + 3], axis=1), empty)]
    conv_ref[...] = jnp.concatenate(by_input, axis=0).T.astype(jnp.bfloat16)
    same = lax.broadcasted_iota(jnp.int32, (fields, pitch - channels), 0) == lax.broadcasted_iota(
        jnp.int32, (fields, pitch - channels), 1
    )
    lift = jnp.concatenate([lift_weight_ref[...].astype(jnp.float32), jnp.where(same, 1.0, 0.0)], axis=1)
    lift_ref[...] = lift.T.astype(jnp.bfloat16)

    lift_rows(prior_ref, edge_ref, lift_ref[...], feat_ref)
    lane = lax.broadcasted_iota(jnp.int32, (channels, width), 1)
    for y in range(rows):
        parts = dot(conv_ref[...], feat_ref[y * pitch : (y + 3) * pitch, :])
        left = jnp.where(lane == 0, 0.0, pltpu.roll(parts[:channels], 1, 1))
        right = jnp.where(lane == width - 1, 0.0, pltpu.roll(parts[2 * channels :], width - 1, 1))
        act_ref[y * channels : (y + 1) * channels, :] = parts[channels : 2 * channels] + left + right


def convolve(prior, edges, lift_weight, kernel):
    rows, fields, width = prior.shape
    channels = kernel.shape[1]
    pitch = channels + 16
    vmem = pl.BlockSpec(memory_space=pltpu.VMEM)
    return pl.pallas_call(
        convolve_kernel,
        out_shape=(
            jax.ShapeDtypeStruct((rows * channels, width), jnp.float32),
            jax.ShapeDtypeStruct((pitch, fields), jnp.bfloat16),
            jax.ShapeDtypeStruct((3 * channels, 3 * pitch), jnp.bfloat16),
            jax.ShapeDtypeStruct((3 * channels, 3 * channels), jnp.bfloat16),
            jax.ShapeDtypeStruct((3, channels, 3 * channels), jnp.bfloat16),
        ),
        in_specs=[vmem] * 4,
        out_specs=[vmem] * 5,
        scratch_shapes=[pltpu.VMEM(((rows + 2) * pitch, width), jnp.bfloat16)],
        compiler_params=pltpu.CompilerParams(vmem_limit_bytes=VMEM_LIMIT),
        cost_estimate=pl.CostEstimate(
            flops=2 * rows * width * 3 * channels * 3 * pitch,
            bytes_accessed=rows * width * channels * 8,
            transcendentals=0,
        ),
        name="convolve",
    )(prior, edges, lift_weight, kernel)


def finish_kernel(
    part_ref,
    prior_ref,
    side_ref,
    lift_ref,
    conv_ref,
    readout_ref,
    act_ref,
    stack_ref,
    forecast_ref,
    estimate_ref,
    halo_ref,
    hidden_ref,
    by_row_ref,
):
    rows, fields, width = prior_ref.shape
    channels = readout_ref.shape[0]
    side = dot(lift_ref[...], side_ref[...])
    shifted = [side] + [pltpu.roll(side, 256 - i, 1) for i in (1, 2)]
    stack = jnp.concatenate(shifted, axis=0).astype(jnp.bfloat16)
    stack_ref[...] = stack
    halo_ref[:, :128] = dot(conv_ref[:channels, :], stack[:, :128])
    halo_ref[:, 128:] = dot(conv_ref[2 * channels :, :], stack[:, 128:])
    readout = readout_ref[...].astype(jnp.float32).T.astype(jnp.bfloat16)
    lane = lax.broadcasted_iota(jnp.int32, (channels, 128), 1)
    spread = [jnp.zeros((channels, 128), jnp.float32)] * (width // 128 - 1)
    for y in range(rows):
        here = slice(y * channels, (y + 1) * channels)
        from_left = jnp.where(lane == 0, pltpu.roll(halo_ref[:, :128], (128 - y) % 128, 1), 0.0)
        from_right = jnp.where(lane == 127, pltpu.roll(halo_ref[:, 128:], 127 - y, 1), 0.0)
        act = (
            part_ref[here, :]
            + jnp.concatenate([from_left] + spread, axis=1)
            + jnp.concatenate(spread + [from_right], axis=1)
        )
        act_ref[here, :] = act
        hidden_ref[here, :] = (act * sigmoid(act)).astype(jnp.bfloat16)
    for y in range(rows):
        increment = dot(readout, hidden_ref[y * channels : (y + 1) * channels, :])
        by_row_ref[y] = prior_ref[y].astype(jnp.float32) + increment
    forecast = jnp.transpose(by_row_ref[...], (1, 0, 2))
    forecast_ref[...] = forecast
    estimate_ref[...] = forecast.astype(jnp.bfloat16)


def finish(part, prior, sides, lift, conv, readout):
    rows, fields, width = prior.shape
    channels = readout.shape[0]
    vmem = pl.BlockSpec(memory_space=pltpu.VMEM)
    return pl.pallas_call(
        finish_kernel,
        out_shape=(
            jax.ShapeDtypeStruct(part.shape, jnp.float32),
            jax.ShapeDtypeStruct((conv.shape[1], 256), jnp.bfloat16),
            jax.ShapeDtypeStruct((fields, rows, width), jnp.float32),
            jax.ShapeDtypeStruct((fields, rows, width), jnp.bfloat16),
        ),
        in_specs=[vmem] * 6,
        out_specs=[vmem] * 4,
        scratch_shapes=[
            pltpu.VMEM((channels, 256), jnp.float32),
            pltpu.VMEM((rows * channels, width), jnp.bfloat16),
            pltpu.VMEM((rows, fields, width), jnp.float32),
        ],
        input_output_aliases={0: 0},
        compiler_params=pltpu.CompilerParams(vmem_limit_bytes=VMEM_LIMIT),
        cost_estimate=pl.CostEstimate(
            flops=2 * rows * width * channels * fields,
            bytes_accessed=rows * width * channels * 8,
            transcendentals=rows * width * channels * 2,
        ),
        name="finish",
    )(part, prior, sides, lift, conv, readout)


def backward_kernel(
    capacity,
    channels,
    norm,
    arrived_ref,
    prior_ref,
    edge_ref,
    stack_ref,
    lift_ref,
    act_ref,
    forecast_ref,
    readout_ref,
    remapped_ref,
    packed_ref,
    slope_ref,
    moment_ref,
    feat_ref,
    hidden_ref,
    block_ref,
    misfit_ref,
    state_ref,
    before_ref,
    after_ref,
):
    fields, rows, width = remapped_ref.shape
    pitch = lift_ref.shape[0]
    devices = arrived_ref.shape[0]
    per_row = width // 128
    slots = devices * capacity

    lift_rows(prior_ref, edge_ref, lift_ref[...], feat_ref)
    slope_ref[:channels, :] = jnp.zeros((channels, width), jnp.bfloat16)
    slope_ref[(rows + 1) * channels :, :] = jnp.zeros((channels, width), jnp.bfloat16)
    depth = fields * rows
    lane = lax.broadcasted_iota(jnp.int32, (fields, depth), 1)
    spread = jnp.where(lane // rows == lax.broadcasted_iota(jnp.int32, (fields, depth), 0), 1.0, 0.0)
    spread = dot(readout_ref[...], spread.astype(jnp.bfloat16))
    lane = lax.broadcasted_iota(jnp.int32, (channels, depth), 1) % rows
    for y in range(rows):
        block_ref[y * channels : (y + 1) * channels, :] = jnp.where(lane == y, spread, 0.0).astype(jnp.bfloat16)

    labels = []
    for first in range(0, devices, 128 // capacity):
        lane = lax.broadcasted_iota(jnp.int32, (fields, 128), 1) // capacity
        label = None
        for d in range(min(devices, 128 // capacity)):
            mine = arrived_ref[first + d, capacity * fields : (capacity + 1) * fields, :].astype(jnp.float32)
            label = mine if label is None else jnp.where(lane == d, mine, label)
        labels.append(label)
    labels = jnp.concatenate(labels, axis=1).astype(jnp.int32)
    tile_blocks = rows * per_row
    labels = jnp.concatenate([labels] * (tile_blocks // fields), axis=0)
    at = lax.broadcasted_iota(jnp.int32, (tile_blocks, slots), 0)
    hits = jnp.where(labels == (at % rows) * per_row + at // rows, 1.0, 0.0).astype(jnp.bfloat16)
    data = arrived_ref[:, : capacity * fields, :].astype(jnp.float32).reshape(slots, fields, 128)
    data = jnp.transpose(data, (1, 0, 2)).astype(jnp.bfloat16)
    for f in range(0, fields, 2):
        picked = dot(hits, jnp.concatenate([data[f], data[f + 1]], axis=1))
        for g in range(2):
            target = picked[:, g * 128 : (g + 1) * 128].astype(jnp.bfloat16)
            target = jnp.concatenate([target[b * rows : (b + 1) * rows] for b in range(per_row)], axis=1)
            remapped_ref[f + g] = target
            misfit_ref[f + g] = (forecast_ref[f + g] - target.astype(jnp.float32)) * norm
    by_row = jnp.transpose(misfit_ref[...], (1, 0, 2))
    empty = jnp.zeros((fields, width), jnp.float32)
    for y in range(rows):
        state_ref[:, y * width : (y + 1) * width] = jnp.concatenate([by_row[y], empty], axis=0).astype(jnp.bfloat16)

    col = lax.broadcasted_iota(jnp.int32, (channels, width), 1)
    lane = lax.broadcasted_iota(jnp.int32, (channels, 128), 1)
    ends_left = ends_right = jnp.zeros((channels, 128), jnp.float32)
    batch = 8
    misfits = misfit_ref[...].reshape(depth, width).astype(jnp.bfloat16)
    for first in range(0, rows, batch):
        latents = dot(block_ref[first * channels : (first + batch) * channels, :], misfits)
        for y in range(first, first + batch):
            here = slice(y * channels, (y + 1) * channels)
            act = act_ref[here, :]
            sig = sigmoid(act)
            hidden_ref[here, :] = (act * sig).astype(jnp.bfloat16)
            latent = latents[(y - first) * channels : (y - first + 1) * channels]
            slope = latent * sig * (1.0 + act * (1.0 - sig))
            slope_ref[(y + 1) * channels : (y + 2) * channels, :] = slope.astype(jnp.bfloat16)
            before = jnp.where(col == width - 1, 0.0, pltpu.roll(slope, width - 1, 1))
            before_ref[here, :] = before.astype(jnp.bfloat16)
            after_ref[here, :] = jnp.where(col == 0, 0.0, pltpu.roll(slope, 1, 1)).astype(jnp.bfloat16)
            ends_left += pltpu.roll(jnp.where(lane == 0, slope[:, :128], 0.0), y, 1)
            ends_right += pltpu.roll(jnp.where(lane == 127, slope[:, -128:], 0.0), y + 1, 1)

    total = None
    for first in range(0, rows, batch):
        span = range(first, first + batch)
        features = jnp.concatenate([feat_ref[y * pitch : (y + 3) * pitch, :] for y in span], axis=1)
        features = jnp.concatenate([features, state_ref[:, first * width : (first + batch) * width]], axis=0)
        others = jnp.concatenate(
            [
                jnp.concatenate([ref[(y + d) * channels : (y + d + 1) * channels, :] for y in span], axis=1)
                for ref, d in ((before_ref, 0), (slope_ref, 1), (after_ref, 0), (hidden_ref, 0))
            ],
            axis=0,
        )
        part = dot_nt(features, others)
        total = part if total is None else total + part
    grad_head = total[3 * pitch : 3 * pitch + fields, 3 * channels :]
    stack = stack_ref[...]
    from_left = dot_nt(stack[:, :128], ends_left.astype(jnp.bfloat16))
    from_right = dot_nt(stack[:, 128:], ends_right.astype(jnp.bfloat16))
    middle = jnp.zeros((3 * pitch, channels), jnp.float32)
    total = total[: 3 * pitch, : 3 * channels] + jnp.concatenate([from_left, middle, from_right], axis=1)
    for i in range(3):
        moment_ref[i] = total[i * pitch + channels : i * pitch + channels + fields, :]
    taps = [total[i * pitch : i * pitch + channels, :] for i in range(3)]
    half = channels // 2
    last = [t[:, 2 * channels :] for t in taps]
    packed = [t[:, : 2 * channels] for t in taps]
    packed.append(jnp.concatenate(last[:2], axis=1))
    packed.append(jnp.concatenate([last[2][:half], last[2][half:]], axis=1))
    packed.append(jnp.concatenate([grad_head, jnp.zeros_like(grad_head)], axis=1))
    packed.append(jnp.zeros((8, 2 * channels), jnp.float32))
    packed = jnp.concatenate(packed, axis=0)
    cut = packed.shape[0] // 2
    odd = lax.rem(lax.axis_index("lon"), 2)
    packed_ref[odd] = packed[:cut]
    packed_ref[1 - odd] = packed[cut:]


def backward(arrived, prior, edges, stack, lift, act, forecast, readout, capacity, norm):
    fields, rows, width = forecast.shape
    channels = readout.shape[0]
    pitch = lift.shape[0]
    packed_rows = (3 * channels + channels + channels // 2 + fields + 8) // 2
    vmem = pl.BlockSpec(memory_space=pltpu.VMEM)
    return pl.pallas_call(
        functools.partial(backward_kernel, capacity, channels, norm),
        out_shape=(
            jax.ShapeDtypeStruct((fields, rows, width), jnp.bfloat16),
            jax.ShapeDtypeStruct((2, packed_rows, 2 * channels), jnp.float32),
            jax.ShapeDtypeStruct(((rows + 2) * channels, width), jnp.bfloat16),
            jax.ShapeDtypeStruct((3, fields, 3 * channels), jnp.float32),
        ),
        in_specs=[vmem] * 8,
        out_specs=[vmem] * 4,
        scratch_shapes=[
            pltpu.VMEM(((rows + 2) * pitch, width), jnp.bfloat16),
            pltpu.VMEM((rows * channels, width), jnp.bfloat16),
            pltpu.VMEM((rows * channels, rows * fields), jnp.bfloat16),
            pltpu.VMEM((fields, rows, width), jnp.float32),
            pltpu.VMEM((2 * fields, rows * width), jnp.bfloat16),
            pltpu.VMEM((rows * channels, width), jnp.bfloat16),
            pltpu.VMEM((rows * channels, width), jnp.bfloat16),
        ],
        compiler_params=pltpu.CompilerParams(vmem_limit_bytes=VMEM_LIMIT),
        cost_estimate=pl.CostEstimate(
            flops=2 * rows * width * 3 * channels * 3 * pitch,
            bytes_accessed=rows * width * channels * 8,
            transcendentals=0,
        ),
        name="backward",
    )(arrived, prior, edges, stack, lift, act, forecast, readout)


def lift_gradient_kernel(slope_ref, prior_ref, back_ref, contract_ref, moment_ref, out_ref, delta_ref):
    rows, fields, width = prior_ref.shape
    channels = contract_ref.shape[1]
    col = lax.broadcasted_iota(jnp.int32, (channels, width), 1)
    delta_ref[:channels, :] = jnp.zeros((channels, width), jnp.bfloat16)
    delta_ref[(rows - 1) * channels :, :] = jnp.zeros((channels, width), jnp.bfloat16)
    for y in range(1, rows - 1):
        parts = dot(back_ref[...], slope_ref[y * channels : (y + 3) * channels, :])
        grad = (
            parts[channels : 2 * channels]
            + pltpu.roll(parts[:channels], width - 1, 1)
            + pltpu.roll(parts[2 * channels :], 1, 1)
        )
        inside = (col > 0) & (col < width - 1)
        delta = jnp.where(inside, grad.astype(jnp.bfloat16).astype(jnp.float32) - grad, 0.0)
        delta_ref[y * channels : (y + 1) * channels, :] = delta.astype(jnp.bfloat16)
    grad_lift = jnp.zeros((fields, channels), jnp.float32)
    batch = 4
    for first in range(0, rows, batch):
        span = range(first, first + batch)
        states = jnp.concatenate([prior_ref[y] for y in span], axis=1)
        deltas = jnp.concatenate([delta_ref[y * channels : (y + 1) * channels, :] for y in span], axis=1)
        grad_lift += dot_nt(states, deltas)
    for i in range(3):
        rest = moment_ref[i]
        for _ in range(3):
            piece = rest.astype(jnp.bfloat16)
            rest = rest - piece.astype(jnp.float32)
            grad_lift += dot_nt(piece, contract_ref[i])
    out_ref[...] = jnp.concatenate([grad_lift, jnp.zeros_like(grad_lift)], axis=1)


def lift_gradient(slope, prior, back, contract, moment):
    rows, fields, width = prior.shape
    channels = contract.shape[1]
    vmem = pl.BlockSpec(memory_space=pltpu.VMEM)
    return pl.pallas_call(
        lift_gradient_kernel,
        out_shape=jax.ShapeDtypeStruct((fields, 2 * channels), jnp.float32),
        in_specs=[vmem] * 5,
        out_specs=vmem,
        scratch_shapes=[pltpu.VMEM((rows * channels, width), jnp.bfloat16)],
        compiler_params=pltpu.CompilerParams(vmem_limit_bytes=VMEM_LIMIT),
        cost_estimate=pl.CostEstimate(
            flops=2 * rows * width * 9 * channels * channels, bytes_accessed=slope.size * 2, transcendentals=0
        ),
        name="lift_gradient",
    )(slope, prior, back, contract, moment)


def unpack_kernel(channels, mine_ref, other_ref, kernel_ref, lift_ref, head_ref):
    odd = lax.rem(lax.axis_index("lon"), 2) == 1
    fields = lift_ref.shape[0]
    lift_ref[...] = (mine_ref[-fields:, :] + other_ref[-fields:, :])[:, :channels]
    mine, other = mine_ref[:-fields, :], other_ref[:-fields, :]
    packed = jnp.concatenate([jnp.where(odd, other, mine), jnp.where(odd, mine, other)], axis=0)
    half = channels // 2
    for i in range(3):
        block = packed[i * channels : (i + 1) * channels]
        kernel_ref[3 * i] = block[:, :channels]
        kernel_ref[3 * i + 1] = block[:, channels:]
    block = packed[3 * channels : 4 * channels]
    kernel_ref[2] = block[:, :channels]
    kernel_ref[5] = block[:, channels:]
    block = packed[4 * channels : 4 * channels + half]
    kernel_ref[8, :half] = block[:, :channels]
    kernel_ref[8, half:] = block[:, channels:]
    head_ref[...] = packed[4 * channels + half : 4 * channels + half + fields, :channels]


def unpack(mine, other, channels, fields):
    return pl.pallas_call(
        functools.partial(unpack_kernel, channels),
        out_shape=(
            jax.ShapeDtypeStruct((9, channels, channels), jnp.float32),
            jax.ShapeDtypeStruct((fields, channels), jnp.float32),
            jax.ShapeDtypeStruct((fields, channels), jnp.float32),
        ),
        compiler_params=pltpu.CompilerParams(vmem_limit_bytes=VMEM_LIMIT),
        name="unpack",
    )(mine, other)


def swap(x, axis, bit):
    return lax.ppermute(x, axis, [(i, i ^ bit) for i in range(lax.axis_size(axis))])


def sum_over(x, axis, low, high):
    if high // low == 4:
        a, b, c = (swap(x, axis, k * low) for k in (1, 2, 3))
        return (x + a) + (b + c)
    bit = low
    while bit < high:
        x = x + swap(x, axis, bit)
        bit *= 2
    return x


def pair_swap(even_sends, odd_sends, axis, periodic):
    count = lax.axis_size(axis)
    even = lax.rem(lax.axis_index(axis), 2) == 0
    inner = [(i, i ^ 1) for i in range(count)]
    outer = []
    for i in range(1, count, 2):
        if i + 1 < count or periodic:
            outer += [(i, (i + 1) % count), ((i + 1) % count, i)]
    got_inner = lax.ppermute(jnp.where(even, odd_sends, even_sends), axis, inner)
    got_outer = lax.ppermute(jnp.where(even, even_sends, odd_sends), axis, outer)
    return jnp.where(even, got_outer, got_inner), jnp.where(even, got_inner, got_outer)


def per_device(
    source,
    intersection_weight,
    dest_tile,
    dest_row,
    prior_state,
    lift_weight,
    kernel,
    readout_weights,
):
    face_count = lax.axis_size("face")
    lon_count = lax.axis_size("lon")
    devices = face_count * lon_count
    src_blocks, intersections = dest_tile.shape
    fields, rows, width = prior_state.shape
    channels = kernel.shape[1]
    capacity = max(2, 2 * src_blocks * intersections // devices)
    norm = 1.0 / math.sqrt(rows * face_count * width * lon_count)

    outgoing = regrid(source, intersection_weight, dest_tile, dest_row, devices, capacity)
    outgoing, prior_state, kernel, lift_weight, readout_weights = lax.optimization_barrier(
        (outgoing, prior_state, kernel, lift_weight, readout_weights)
    )
    arrived = lax.all_to_all(outgoing, ("face", "lon"), split_axis=0, concat_axis=0, tiled=True)
    arrived = arrived.reshape(devices, (capacity + 1) * fields, source.shape[2])

    prior = prior_state.transpose(1, 0, 2)
    top, bottom = pair_swap(prior[0], prior[rows - 1], "face", False)
    columns = [
        jnp.pad(
            jnp.concatenate([top[:, at : at + 1], prior_state[:, :, at], bottom[:, at : at + 1]], axis=1),
            ((0, 0), (0, 128 - rows - 2)),
        )
        for at in (0, width - 1)
    ]
    left, right = pair_swap(columns[0], columns[1], "lon", True)

    edges = jnp.stack([top, bottom])
    sides = jnp.concatenate([left, right], axis=1)
    part, lift, conv, back, contract = convolve(prior, edges, lift_weight, kernel)
    act, stack, forecast, estimate = finish(part, prior, sides, lift, conv, readout_weights)
    remapped, packed, slope, moment = backward(
        arrived, prior, edges, stack, lift, act, forecast, readout_weights, capacity, norm
    )
    part = packed[0] + swap(packed[1], "lon", 1)
    part = jnp.concatenate([part, lift_gradient(slope, prior, back, contract, moment)])
    part = sum_over(part, "face", 1, face_count)
    part = sum_over(part, "lon", 2, lon_count)
    grad_kernel, grad_lift, grad_head = unpack(part, swap(part, "lon", 1), channels, fields)
    return (
        remapped,
        estimate,
        grad_lift,
        grad_kernel,
        grad_head.T,
    )


def solution(mesh):
    return jax.shard_map(
        per_device,
        mesh=mesh,
        in_specs=(
            P(("face", "lon"), None, None),
            P(("face", "lon"), None, None, None),
            P(("face", "lon"), None),
            P(("face", "lon"), None),
            P(None, "face", "lon"),
            P(),
            P(),
            P(),
        ),
        out_specs=(P(None, "face", "lon"), P(None, "face", "lon"), P(), P(), P()),
        check_vma=False,
    )
```

time: 57.8 us -> 55.8 us (0.965)
  waiting for transfers between devices: 18.6 us -> 16.3 us
    pallas_call x1 -> x3, Pallas kernels: 3.53 us -> 6.17 us  [the longest x1 2.63 us: finish(): pl.pallas_call(finish_kernel, out_shape=(jax.ShapeDtypeStruct(part.shape,...]
    pallas_call x1, Pallas kernels: 5.93 us -> 3.7 us  [backward(): pl.pallas_call(functools.partial(backward_kernel, capacity, channels, nor...]
    ppermute x2, waiting for transfers between devices: 4.3 us -> 2.41 us  [pair_swap(): lax.ppermute(jnp.where(even, even_sends, odd_sends), axis, outer)]
    ppermute x8, waiting for transfers between devices: 12.6 us -> 11.2 us  [swap(): lax.ppermute(x, axis, [(i, i ^ bit) for i in range(lax.axis_size(axis))])]
    all_to_all x1, waiting for transfers between devices: 0.44 us -> 1.36 us  [per_device(): lax.all_to_all(outgoing, ('face', 'lon'), split_axis=0, concat_axis=0, ti...]
  transfers between devices with their start and end apart: 13 -> 13, of which waited for: 9 -> 9; matrix products, arithmetic and copies ran while one was open for 1% -> 1% of each run, Pallas kernels for 6% -> 11%
where the time goes in v2:
time: 55.8 us; the launch traced here: 55.6 us
  starting transfers between devices  22.8 us (41%)
  waiting for transfers between devices  16.3 us (29%)
  Pallas kernels  14.9 us (27%)
  between operations  0.83 us (1%)
  local copies, waits for them, and re-layouts  0.6 us (1%)
    ppermute x8, waiting for transfers between devices, swap(): lax.ppermute(x, axis, [(i, i ^ bit) for i in range(lax.axis_size(axis))])  11.2 us
    ppermute x8, starting transfers between devices, swap(): lax.ppermute(x, axis, [(i, i ^ bit) for i in range(lax.axis_size(axis))])  8.08 us
    all_to_all x1, starting transfers between devices, per_device(): lax.all_to_all(outgoing, ('face', 'lon'), split_axis=0, concat_axis=0, ti...  7.3 us
    ppermute x2, starting transfers between devices, pair_swap(): lax.ppermute(jnp.where(even, odd_sends, even_sends), axis, inner)  4.55 us
    pallas_call x1, Pallas kernels, regrid(): pl.pallas_call(functools.partial(regrid_kernel, capacity), out_shape=jax....  4.19 us
    pallas_call x1, Pallas kernels, backward(): pl.pallas_call(functools.partial(backward_kernel, capacity, channels, nor...  3.7 us
    ppermute x2, starting transfers between devices, pair_swap(): lax.ppermute(jnp.where(even, even_sends, odd_sends), axis, outer)  2.85 us
    pallas_call x1, Pallas kernels, finish(): pl.pallas_call(finish_kernel, out_shape=(jax.ShapeDtypeStruct(part.shape,...  2.63 us
  transfers between devices with their start and end apart: 13, of which 9 were waited for; matrix products, arithmetic and copies ran while one was open for 1% of the time, Pallas kernels for 11%

profile of v2, /device:TPU:0, one launch (start us, length us, event | category | flops | bytes accessed | tf_op | source)
XLA Modules:
  0.0 55.6 jit_solution(13806495115568619405)
XLA Ops:
  0.6 4.2 %regrid.1 = bf16[32,9,8,128]{3,2,1,0:T(8,128)(2,1)} custom-call(s32[4,32]{1,0:T(4,128)} %bitcast.29, s32[4,32]{1,0:T(4,128)} %bitcast.30, bf16[32,8,128]{2,1,0:T(8,128)(2,1)} %src_ref.1, bf16[32,4,128,128]{3,2,1,0:T(8,128)(2,1)} %wts_hbm.1), custom_call_target="tpu_custom_call" | custom-call | flops 33554432 | bytes 4194304 | tf_op jit(solution)/shard_map/regrid/pallas_call | solution.py:74
  4.8 0.0 copy-start.3
  4.9 7.3 %all-to-all-start = ((bf16[32,9,8,128]{3,2,1,0:T(8,128)(2,1)}), bf16[32,9,8,128]{3,2,1,0:T(8,128)(2,1)S(1)}, u32[]{:S(2)}, u32[]{:S(2)}) async-start(bf16[32,9,8,128]{3,2,1,0:T(8,128)(2,1)} %regrid.1), calls=%async_computation | async-start | bytes 1179648 | tf_op jit(solution)/shard_map/all_to_all | solution.py:539
  12.2 0.1 copy.20
  12.3 0.7 %collective-permute-start = (bf16[8,256]{1,0:T(8,128)(2,1)S(1)}, bf16[8,256]{1,0:T(8,128)(2,1)S(1)}, u32[]{:S(2)}, u32[]{:S(2)}) collective-permute-start(bf16[8,256]{1,0:T(8,128)(2,1)S(1)} %get-tuple-element.49), channel_id=1, source_target_pairs={{8,16},{16,8},{9,17},{17,9},{10,18},{18,10},{11,19},{19,11},{12,20... | collective-permute-start | bytes 12296 | tf_op jit(solution)/shard_map/ppermute | solution.py:512
  13.0 4.5 %collective-permute-start.1 = (bf16[8,256]{1,0:T(8,128)(2,1)S(1)}, bf16[8,256]{1,0:T(8,128)(2,1)S(1)}, u32[]{:S(2)}, u32[]{:S(2)}) collective-permute-start(bf16[8,256]{1,0:T(8,128)(2,1)S(1)} %get-tuple-element.50), channel_id=1, source_target_pairs={{0,8},{8,0},{16,24},{24,16},{1,9},{9,1},{17,25},{25,17},{2,10},{10... | collective-permute-start | bytes 12296 | tf_op jit(solution)/shard_map/ppermute | solution.py:511
  17.5 0.3 copy.15
  17.9 0.1 copy.17.readout_ref
  18.0 1.3 %collective-permute-done.1 = bf16[8,256]{1,0:T(8,128)(2,1)S(1)} collective-permute-done((bf16[8,256]{1,0:T(8,128)(2,1)S(1)}, bf16[8,256]{1,0:T(8,128)(2,1)S(1)}, u32[]{:S(2)}, u32[]{:S(2)}) %collective-permute-start.1) | collective-permute-done | bytes 4128 | tf_op jit(solution)/shard_map/ppermute | solution.py:511
  19.3 0.1 fusion.10
  19.4 0.1 broadcast_select_fusion.5
  19.5 2.2 %collective-permute-start.2 = (bf16[8,128]{1,0:T(8,128)(2,1)S(1)}, bf16[8,128]{1,0:T(8,128)(2,1)S(1)}, u32[]{:S(2)}, u32[]{:S(2)}) collective-permute-start(bf16[8,128]{1,0:T(8,128)(2,1)S(1)} %get-tuple-element.51), channel_id=1, source_target_pairs={{1,2},{2,1},{3,4},{4,3},{5,6},{6,5},{7,0},{0,7},{9,10},{10,9},{11,... | collective-permute-start | bytes 6152 | tf_op jit(solution)/shard_map/ppermute | solution.py:512
  21.7 1.9 %convolve.1 = (f32[2048,256]{1,0:T(8,128)S(1)}, bf16[80,8]{1,0:T(8,128)(2,1)S(1)}, bf16[192,240]{1,0:T(8,128)(2,1)S(1)}, bf16[192,192]{1,0:T(8,128)(2,1)S(1)}, bf16[3,64,192]{2,1,0:T(8,128)(2,1)S(1)}) custom-call(bf16[32,8,256]{2,1,0:T(8,128)(2,1)S(1)} %bitcast.23, bf16[2,8,256]{2,1,0:T(8,128)(2,1)S(1)} %pad_maximum_fusion.1.edge_ref, ...), custom_call_target="tpu_custom_call" | custom-call | flops 754974720 | bytes 4194304 | tf_op jit(solution)/shard_map/convolve/pallas_call | solution.py:147
  23.5 2.4 %collective-permute-done.2 = bf16[8,128]{1,0:T(8,128)(2,1)S(1)} collective-permute-done((bf16[8,128]{1,0:T(8,128)(2,1)S(1)}, bf16[8,128]{1,0:T(8,128)(2,1)S(1)}, u32[]{:S(2)}, u32[]{:S(2)}) %collective-permute-start.2) | collective-permute-done | bytes 2080 | tf_op jit(solution)/shard_map/ppermute | solution.py:512
  26.0 2.6 %finish.1 = (f32[2048,256]{1,0:T(8,128)S(1)}, bf16[240,256]{1,0:T(8,128)(2,1)S(1)}, f32[8,32,256]{2,1,0:T(8,128)S(1)}, bf16[8,32,256]{2,1,0:T(8,128)(2,1)}) custom-call(f32[2048,256]{1,0:T(8,128)S(1)} %get-tuple-element.30.part_ref, bf16[32,8,256]{2,1,0:T(8,128)(2,1)S(1)} %bitcast.24, ...), custom_call_target="tpu_custom_call", output_to_operand_aliasing={{0}: (0, {})} | custom-call | flops 8388608 | bytes 4194304 | tf_op jit(solution)/shard_map/finish/pallas_call | solution.py:218
  28.6 1.4 %all-to-all-done = bf16[32,9,8,128]{3,2,1,0:T(8,128)(2,1)S(1)} async-done(((bf16[32,9,8,128]{3,2,1,0:T(8,128)(2,1)}), bf16[32,9,8,128]{3,2,1,0:T(8,128)(2,1)S(1)}, u32[]{:S(2)}, u32[]{:S(2)}) %all-to-all-start) | async-done | bytes 589856 | tf_op jit(solution)/shard_map/all_to_all | solution.py:539
  30.0 3.7 %backward.1 = (bf16[8,32,256]{2,1,0:T(8,128)(2,1)}, f32[2,152,128]{2,1,0:T(8,128)S(1)}, bf16[2176,256]{1,0:T(8,128)(2,1)S(1)}, f32[3,8,192]{2,1,0:T(8,128)S(1)}) custom-call(bf16[32,72,128]{2,1,0:T(8,128)(2,1)S(1)} %bitcast.21, bf16[32,8,256]{2,1,0:T(8,128)(2,1)S(1)} %bitcast.25, bf16[2,8,256]{2,1,0:T(8,128)(2,1)S(1)} %pad_maximum_fusion.1.edge_ref, ...), custom_call_target="tpu_custom_call" | custom-call | flops 754974720 | bytes 4194304 | tf_op jit(solution)/shard_map/backward/pallas_call | solution.py:376
  33.7 1.7 %lift_gradient.1 = f32[8,128]{1,0:T(8,128)S(1)} custom-call(bf16[2176,256]{1,0:T(8,128)(2,1)S(1)} %get-tuple-element.40.slope_ref, bf16[32,8,256]{2,1,0:T(8,128)(2,1)S(1)} %bitcast.26, bf16[192,192]{1,0:T(8,128)(2,1)S(1)} %get-tuple-element.41.back_ref, bf16[3,64,192]{2,1,0:T(8,128)(2,1)S(1)} %get-tuple-element.42.contract_ref, ...), custom_call_target="tpu_custom_call" | custom-call | flops 603979776 | bytes 1114112 | tf_op jit(solution)/shard_map/lift_gradient/pallas_call | solution.py:441
  35.4 0.9 %collective-permute-start.6 = (f32[160,128]{1,0:T(8,128)S(1)}, f32[160,128]{1,0:T(8,128)S(1)}, u32[]{:S(2)}, u32[]{:S(2)}) collective-permute-start(f32[160,128]{1,0:T(8,128)S(1)} %pad_maximum_fusion), channel_id=1, source_target_pairs={{0,16},{8,24},{16,0},{24,8},{1,17},{9,25},{17,1},{25,9},{2,18},{10... | collective-permute-start | bytes 245768 | tf_op jit(solution)/shard_map/ppermute | solution.py:489
  36.3 1.5 %collective-permute-start.7 = (f32[160,128]{1,0:T(8,128)S(1)}, f32[160,128]{1,0:T(8,128)S(1)}, u32[]{:S(2)}, u32[]{:S(2)}) collective-permute-start(f32[160,128]{1,0:T(8,128)S(1)} %pad_maximum_fusion), channel_id=1, source_target_pairs={{0,24},{8,16},{16,8},{24,0},{1,25},{9,17},{17,9},{25,1},{2,26},{10... | collective-permute-start | bytes 245768 | tf_op jit(solution)/shard_map/ppermute | solution.py:489
  37.8 1.2 %collective-permute-start.5 = (f32[160,128]{1,0:T(8,128)S(1)}, f32[160,128]{1,0:T(8,128)S(1)}, u32[]{:S(2)}, u32[]{:S(2)}) collective-permute-start(f32[160,128]{1,0:T(8,128)S(1)} %pad_maximum_fusion), channel_id=1, source_target_pairs={{0,8},{8,0},{16,24},{24,16},{1,9},{9,1},{17,25},{25,17},{2,10},{10... | collective-permute-start | bytes 245768 | tf_op jit(solution)/shard_map/ppermute | solution.py:489
  39.0 2.6 %collective-permute-done.6 = f32[160,128]{1,0:T(8,128)S(1)} collective-permute-done((f32[160,128]{1,0:T(8,128)S(1)}, f32[160,128]{1,0:T(8,128)S(1)}, u32[]{:S(2)}, u32[]{:S(2)}) %collective-permute-start.6) | collective-permute-done | bytes 81952 | tf_op jit(solution)/shard_map/ppermute | solution.py:489
  41.6 0.8 %collective-permute-done.7 = f32[160,128]{1,0:T(8,128)S(1)} collective-permute-done((f32[160,128]{1,0:T(8,128)S(1)}, f32[160,128]{1,0:T(8,128)S(1)}, u32[]{:S(2)}, u32[]{:S(2)}) %collective-permute-start.7) | collective-permute-done | bytes 81952 | tf_op jit(solution)/shard_map/ppermute | solution.py:489
  42.4 0.9 %collective-permute-done.5 = f32[160,128]{1,0:T(8,128)S(1)} collective-permute-done((f32[160,128]{1,0:T(8,128)S(1)}, f32[160,128]{1,0:T(8,128)S(1)}, u32[]{:S(2)}, u32[]{:S(2)}) %collective-permute-start.5) | collective-permute-done | bytes 81952 | tf_op jit(solution)/shard_map/ppermute | solution.py:489
  43.3 0.4 collective-permute-start.10
  43.7 2.9 %collective-permute-start.9 = (f32[160,128]{1,0:T(8,128)S(1)}, f32[160,128]{1,0:T(8,128)S(1)}, u32[]{:S(2)}, u32[]{:S(2)}) collective-permute-start(f32[160,128]{1,0:T(8,128)S(1)} %add_add_fusion.1), channel_id=1, source_target_pairs={{0,4},{1,5},{2,6},{3,7},{4,0},{5,1},{6,2},{7,3},{8,12},{9,13},{10,... | collective-permute-start | bytes 245768 | tf_op jit(solution)/shard_map/ppermute | solution.py:489
  46.6 1.1 %collective-permute-start.8 = (f32[160,128]{1,0:T(8,128)S(1)}, f32[160,128]{1,0:T(8,128)S(1)}, u32[]{:S(2)}, u32[]{:S(2)}) collective-permute-start(f32[160,128]{1,0:T(8,128)S(1)} %add_add_fusion.1), channel_id=1, source_target_pairs={{0,2},{1,3},{2,0},{3,1},{4,6},{5,7},{6,4},{7,5},{8,10},{9,11},{10,... | collective-permute-start | bytes 245768 | tf_op jit(solution)/shard_map/ppermute | solution.py:489
  47.7 2.8 %collective-permute-done.10 = f32[160,128]{1,0:T(8,128)S(1)} collective-permute-done((f32[160,128]{1,0:T(8,128)S(1)}, f32[160,128]{1,0:T(8,128)S(1)}, u32[]{:S(2)}, u32[]{:S(2)}) %collective-permute-start.10) | collective-permute-done | bytes 81952 | tf_op jit(solution)/shard_map/ppermute | solution.py:489
  50.6 2.8 %collective-permute-done.9 = f32[160,128]{1,0:T(8,128)S(1)} collective-permute-done((f32[160,128]{1,0:T(8,128)S(1)}, f32[160,128]{1,0:T(8,128)S(1)}, u32[]{:S(2)}, u32[]{:S(2)}) %collective-permute-start.9) | collective-permute-done | bytes 81952 | tf_op jit(solution)/shard_map/ppermute | solution.py:489
  53.4 0.1 collective-permute-start.11
  53.5 1.3 %collective-permute-done.11.other_ref = f32[160,128]{1,0:T(8,128)S(1)} collective-permute-done((f32[160,128]{1,0:T(8,128)S(1)}, f32[160,128]{1,0:T(8,128)S(1)}, u32[]{:S(2)}, u32[]{:S(2)}) %collective-permute-start.11) | collective-permute-done | bytes 81952 | tf_op jit(solution)/shard_map/ppermute | solution.py:489
  54.8 0.8 %unpack.1 = (f32[9,64,64]{2,1,0:T(8,128)}, f32[8,64]{1,0:T(8,128)}, f32[8,64]{1,0:T(8,128)}) custom-call(f32[160,128]{1,0:T(8,128)S(1)} %add_add_fusion.mine_ref, f32[160,128]{1,0:T(8,128)S(1)} %collective-permute-done.11.other_ref), custom_call_target="tpu_custom_call" | custom-call | tf_op jit(solution)/shard_map/unpack/pallas_call | solution.py:476
  (24 shorter events, 0.2 us)
Async XLA Ops:
  0.6 11.6 %copy-start.2 = (bf16[8,32,256]{2,1,0:T(8,128)(2,1)S(1)}, bf16[8,32,256]{2,1,0:T(8,128)(2,1)}, u32[]{:S(2)}) copy-start(bf16[8,32,256]{2,1,0:T(8,128)(2,1)} %param.12) | copy-start | bytes 393220
  4.8 13.0 %copy-start.3 = (bf16[64,8]{0,1:T(8,128)(2,1)S(1)}, bf16[64,8]{0,1:T(8,128)(2,1)}, u32[]{:S(2)}) copy-start(bf16[64,8]{0,1:T(8,128)(2,1)} %param.15) | copy-start | bytes 3076
  4.9 16.8 %copy-start = (bf16[9,64,64]{2,1,0:T(8,128)(2,1)S(1)}, bf16[9,64,64]{2,1,0:T(8,128)(2,1)}, u32[]{:S(2)}) copy-start(bf16[9,64,64]{2,1,0:T(8,128)(2,1)} %kernel_ref) | copy-start | bytes 221188
  4.9 16.8 %copy-start.1 = (bf16[8,64]{1,0:T(8,128)(2,1)S(1)}, bf16[8,64]{1,0:T(8,128)(2,1)}, u32[]{:S(2)}) copy-start(bf16[8,64]{1,0:T(8,128)(2,1)} %lift_weight_ref) | copy-start | bytes 3076
  4.9 25.1 %all-to-all-start = ((bf16[32,9,8,128]{3,2,1,0:T(8,128)(2,1)}), bf16[32,9,8,128]{3,2,1,0:T(8,128)(2,1)S(1)}, u32[]{:S(2)}, u32[]{:S(2)}) async-start(bf16[32,9,8,128]{3,2,1,0:T(8,128)(2,1)} %regrid.1), calls=%async_computation | async-start | bytes 1179648 | tf_op jit(solution)/shard_map/all_to_all | solution.py:539
  12.3 5.7 %collective-permute-start = (bf16[8,256]{1,0:T(8,128)(2,1)S(1)}, bf16[8,256]{1,0:T(8,128)(2,1)S(1)}, u32[]{:S(2)}, u32[]{:S(2)}) collective-permute-start(bf16[8,256]{1,0:T(8,128)(2,1)S(1)} %get-tuple-element.49), channel_id=1, source_target_pairs={{8,16},{16,8},{9,17},{17,9},{10,18},{18,10},{11,19},{19,11},{12,20... | collective-permute-start | bytes 12296 | tf_op jit(solution)/shard_map/ppermute | solution.py:512
  13.0 6.3 %collective-permute-start.1 = (bf16[8,256]{1,0:T(8,128)(2,1)S(1)}, bf16[8,256]{1,0:T(8,128)(2,1)S(1)}, u32[]{:S(2)}, u32[]{:S(2)}) collective-permute-start(bf16[8,256]{1,0:T(8,128)(2,1)S(1)} %get-tuple-element.50), channel_id=1, source_target_pairs={{0,8},{8,0},{16,24},{24,16},{1,9},{9,1},{17,25},{25,17},{2,10},{10... | collective-permute-start | bytes 12296 | tf_op jit(solution)/shard_map/ppermute | solution.py:511
  19.5 6.5 %collective-permute-start.2 = (bf16[8,128]{1,0:T(8,128)(2,1)S(1)}, bf16[8,128]{1,0:T(8,128)(2,1)S(1)}, u32[]{:S(2)}, u32[]{:S(2)}) collective-permute-start(bf16[8,128]{1,0:T(8,128)(2,1)S(1)} %get-tuple-element.51), channel_id=1, source_target_pairs={{1,2},{2,1},{3,4},{4,3},{5,6},{6,5},{7,0},{0,7},{9,10},{10,9},{11,... | collective-permute-start | bytes 6152 | tf_op jit(solution)/shard_map/ppermute | solution.py:512
  21.6 4.3 %collective-permute-start.3 = (bf16[8,128]{1,0:T(8,128)(2,1)S(1)}, bf16[8,128]{1,0:T(8,128)(2,1)S(1)}, u32[]{:S(2)}, u32[]{:S(2)}) collective-permute-start(bf16[8,128]{1,0:T(8,128)(2,1)S(1)} %get-tuple-element.52), channel_id=1, source_target_pairs={{0,1},{1,0},{2,3},{3,2},{4,5},{5,4},{6,7},{7,6},{8,9},{9,8},{10,11... | collective-permute-start | bytes 6152 | tf_op jit(solution)/shard_map/ppermute | solution.py:511
  33.7 1.7 %collective-permute-start.4 = (f32[152,128]{1,0:T(8,128)S(1)}, f32[152,128]{1,0:T(8,128)S(1)}, u32[]{:S(2)}, u32[]{:S(2)}) collective-permute-start(f32[152,128]{1,0:T(8,128)S(1)} %slice_bitcast_fusion), channel_id=1, source_target_pairs={{0,1},{1,0},{2,3},{3,2},{4,5},{5,4},{6,7},{7,6},{8,9},{9,8},{10,11... | collective-permute-start | bytes 233480 | tf_op jit(solution)/shard_map/ppermute | solution.py:489
  35.4 6.2 %collective-permute-start.6 = (f32[160,128]{1,0:T(8,128)S(1)}, f32[160,128]{1,0:T(8,128)S(1)}, u32[]{:S(2)}, u32[]{:S(2)}) collective-permute-start(f32[160,128]{1,0:T(8,128)S(1)} %pad_maximum_fusion), channel_id=1, source_target_pairs={{0,16},{8,24},{16,0},{24,8},{1,17},{9,25},{17,1},{25,9},{2,18},{10... | collective-permute-start | bytes 245768 | tf_op jit(solution)/shard_map/ppermute | solution.py:489
  36.3 6.0 %collective-permute-start.7 = (f32[160,128]{1,0:T(8,128)S(1)}, f32[160,128]{1,0:T(8,128)S(1)}, u32[]{:S(2)}, u32[]{:S(2)}) collective-permute-start(f32[160,128]{1,0:T(8,128)S(1)} %pad_maximum_fusion), channel_id=1, source_target_pairs={{0,24},{8,16},{16,8},{24,0},{1,25},{9,17},{17,9},{25,1},{2,26},{10... | collective-permute-start | bytes 245768 | tf_op jit(solution)/shard_map/ppermute | solution.py:489
  37.8 5.5 %collective-permute-start.5 = (f32[160,128]{1,0:T(8,128)S(1)}, f32[160,128]{1,0:T(8,128)S(1)}, u32[]{:S(2)}, u32[]{:S(2)}) collective-permute-start(f32[160,128]{1,0:T(8,128)S(1)} %pad_maximum_fusion), channel_id=1, source_target_pairs={{0,8},{8,0},{16,24},{24,16},{1,9},{9,1},{17,25},{25,17},{2,10},{10... | collective-permute-start | bytes 245768 | tf_op jit(solution)/shard_map/ppermute | solution.py:489
  43.3 7.3 %collective-permute-start.10 = (f32[160,128]{1,0:T(8,128)S(1)}, f32[160,128]{1,0:T(8,128)S(1)}, u32[]{:S(2)}, u32[]{:S(2)}) collective-permute-start(f32[160,128]{1,0:T(8,128)S(1)} %add_add_fusion.1), channel_id=1, source_target_pairs={{0,6},{1,7},{2,4},{3,5},{4,2},{5,3},{6,0},{7,1},{8,14},{9,15},{10,... | collective-permute-start | bytes 245768 | tf_op jit(solution)/shard_map/ppermute | solution.py:489
  43.7 9.7 %collective-permute-start.9 = (f32[160,128]{1,0:T(8,128)S(1)}, f32[160,128]{1,0:T(8,128)S(1)}, u32[]{:S(2)}, u32[]{:S(2)}) collective-permute-start(f32[160,128]{1,0:T(8,128)S(1)} %add_add_fusion.1), channel_id=1, source_target_pairs={{0,4},{1,5},{2,6},{3,7},{4,0},{5,1},{6,2},{7,3},{8,12},{9,13},{10,... | collective-permute-start | bytes 245768 | tf_op jit(solution)/shard_map/ppermute | solution.py:489
  46.6 6.8 %collective-permute-start.8 = (f32[160,128]{1,0:T(8,128)S(1)}, f32[160,128]{1,0:T(8,128)S(1)}, u32[]{:S(2)}, u32[]{:S(2)}) collective-permute-start(f32[160,128]{1,0:T(8,128)S(1)} %add_add_fusion.1), channel_id=1, source_target_pairs={{0,2},{1,3},{2,0},{3,1},{4,6},{5,7},{6,4},{7,5},{8,10},{9,11},{10,... | collective-permute-start | bytes 245768 | tf_op jit(solution)/shard_map/ppermute | solution.py:489
  53.4 1.3 %collective-permute-start.11 = (f32[160,128]{1,0:T(8,128)S(1)}, f32[160,128]{1,0:T(8,128)S(1)}, u32[]{:S(2)}, u32[]{:S(2)}) collective-permute-start(f32[160,128]{1,0:T(8,128)S(1)} %add_add_fusion.mine_ref), channel_id=1, source_target_pairs={{0,1},{1,0},{2,3},{3,2},{4,5},{5,4},{6,7},{7,6},{8,9},{9,8},{10,11... | collective-permute-start | bytes 245768 | tf_op jit(solution)/shard_map/ppermute | solution.py:489

commit v3 on v2

--- a/solution.py
+++ b/solution.py
@@ -25,11 +25,26 @@
     return 1.0 / (1.0 + jnp.exp(-x))
 
 
-def regrid_kernel(capacity, tile_ref, row_ref, src_ref, wts_hbm, out_ref, wts_ref, count_ref, slot_ref, head_ref, sems):
+def regrid_kernel(
+    capacity,
+    tile_hbm,
+    row_hbm,
+    src_hbm,
+    wts_hbm,
+    out_ref,
+    tile_ref,
+    row_ref,
+    src_ref,
+    wts_ref,
+    count_ref,
+    slot_ref,
+    head_ref,
+    sems,
+):
     blocks, fields, width = src_ref.shape
     intersections = wts_ref.shape[1]
     devices = out_ref.shape[0]
-    chunks = sems.shape[0]
+    chunks = sems.shape[0] - 3
     chunk = blocks // chunks
     copies = [
         pltpu.make_async_copy(
@@ -37,11 +52,15 @@
         )
         for i in range(chunks)
     ]
-    for copy in copies:
+    pairs = ((tile_hbm, tile_ref), (row_hbm, row_ref), (src_hbm, src_ref))
+    first = [pltpu.make_async_copy(a, b, sems.at[chunks + i]) for i, (a, b) in enumerate(pairs)]
+    for copy in first + copies:
         copy.start()
     head_ref[...] = jnp.full_like(head_ref, -1.0)
     for d in range(devices):
         count_ref[d] = 0
+    for copy in first:
+        copy.wait()
     slot_of_lane = lax.rem(lax.broadcasted_iota(jnp.int32, (1, width), 1), capacity)
     for s in range(blocks):
         for k in range(intersections):
@@ -69,19 +88,21 @@
     blocks, fields, width = source.shape
     intersections = weights.shape[1]
     chunks = math.gcd(blocks, 4)
-    smem = pl.BlockSpec(memory_space=pltpu.SMEM)
     vmem = pl.BlockSpec(memory_space=pltpu.VMEM)
     return pl.pallas_call(
         functools.partial(regrid_kernel, capacity),
         out_shape=jax.ShapeDtypeStruct((devices, capacity + 1, fields, width), jnp.bfloat16),
-        in_specs=[smem, smem, vmem, pl.BlockSpec(memory_space=pl.ANY)],
+        in_specs=[pl.BlockSpec(memory_space=pl.ANY)] * 4,
         out_specs=vmem,
         scratch_shapes=[
+            pltpu.SMEM((intersections, blocks), jnp.int32),
+            pltpu.SMEM((intersections, blocks), jnp.int32),
+            pltpu.VMEM(source.shape, jnp.bfloat16),
             pltpu.VMEM(weights.shape, jnp.bfloat16),
             pltpu.SMEM((devices,), jnp.int32),
             pltpu.SMEM((intersections, blocks), jnp.int32),
             pltpu.VMEM((devices, width), jnp.float32),
-            pltpu.SemaphoreType.DMA((chunks,)),
+            pltpu.SemaphoreType.DMA((chunks + 3,)),
         ],
         compiler_params=pltpu.CompilerParams(vmem_limit_bytes=REGRID_VMEM),
         cost_estimate=pl.CostEstimate(
@@ -176,7 +197,6 @@
     act_ref,
     stack_ref,
     forecast_ref,
-    estimate_ref,
     halo_ref,
     hidden_ref,
     by_row_ref,
@@ -206,9 +226,7 @@
     for y in range(rows):
         increment = dot(readout, hidden_ref[y * channels : (y + 1) * channels, :])
         by_row_ref[y] = prior_ref[y].astype(jnp.float32) + increment
-    forecast = jnp.transpose(by_row_ref[...], (1, 0, 2))
-    forecast_ref[...] = forecast
-    estimate_ref[...] = forecast.astype(jnp.bfloat16)
+    forecast_ref[...] = jnp.transpose(by_row_ref[...], (1, 0, 2))
 
 
 def finish(part, prior, sides, lift, conv, readout):
@@ -221,10 +239,9 @@
             jax.ShapeDtypeStruct(part.shape, jnp.float32),
             jax.ShapeDtypeStruct((conv.shape[1], 256), jnp.bfloat16),
             jax.ShapeDtypeStruct((fields, rows, width), jnp.float32),
-            jax.ShapeDtypeStruct((fields, rows, width), jnp.bfloat16),
         ),
         in_specs=[vmem] * 6,
-        out_specs=[vmem] * 4,
+        out_specs=[vmem] * 3,
         scratch_shapes=[
             pltpu.VMEM((channels, 256), jnp.float32),
             pltpu.VMEM((rows * channels, width), jnp.bfloat16),
@@ -302,8 +319,9 @@
         for g in range(2):
             target = picked[:, g * 128 : (g + 1) * 128].astype(jnp.bfloat16)
             target = jnp.concatenate([target[b * rows : (b + 1) * rows] for b in range(per_row)], axis=1)
+            target = target.astype(jnp.float32)
             remapped_ref[f + g] = target
-            misfit_ref[f + g] = (forecast_ref[f + g] - target.astype(jnp.float32)) * norm
+            misfit_ref[f + g] = (forecast_ref[f + g] - target) * norm
     by_row = jnp.transpose(misfit_ref[...], (1, 0, 2))
     empty = jnp.zeros((fields, width), jnp.float32)
     for y in range(rows):
@@ -376,7 +394,7 @@
     return pl.pallas_call(
         functools.partial(backward_kernel, capacity, channels, norm),
         out_shape=(
-            jax.ShapeDtypeStruct((fields, rows, width), jnp.bfloat16),
+            jax.ShapeDtypeStruct((fields, rows, width), jnp.float32),
             jax.ShapeDtypeStruct((2, packed_rows, 2 * channels), jnp.float32),
             jax.ShapeDtypeStruct(((rows + 2) * channels, width), jnp.bfloat16),
             jax.ShapeDtypeStruct((3, fields, 3 * channels), jnp.float32),
@@ -405,7 +423,8 @@
 def lift_gradient_kernel(slope_ref, prior_ref, back_ref, contract_ref, moment_ref, out_ref, delta_ref):
     rows, fields, width = prior_ref.shape
     channels = contract_ref.shape[1]
-    col = lax.broadcasted_iota(jnp.int32, (channels, width), 1)
+    col = lax.broadcasted_iota(jnp.int32, (fields, width), 1)
+    inside = (col > 0) & (col < width - 1)
     delta_ref[:channels, :] = jnp.zeros((channels, width), jnp.bfloat16)
     delta_ref[(rows - 1) * channels :, :] = jnp.zeros((channels, width), jnp.bfloat16)
     for y in range(1, rows - 1):
@@ -415,14 +434,14 @@
             + pltpu.roll(parts[:channels], width - 1, 1)
             + pltpu.roll(parts[2 * channels :], 1, 1)
         )
-        inside = (col > 0) & (col < width - 1)
-        delta = jnp.where(inside, grad.astype(jnp.bfloat16).astype(jnp.float32) - grad, 0.0)
+        delta = grad.astype(jnp.bfloat16).astype(jnp.float32) - grad
         delta_ref[y * channels : (y + 1) * channels, :] = delta.astype(jnp.bfloat16)
     grad_lift = jnp.zeros((fields, channels), jnp.float32)
     batch = 4
     for first in range(0, rows, batch):
         span = range(first, first + batch)
-        states = jnp.concatenate([prior_ref[y] for y in span], axis=1)
+        states = [jnp.where(inside, prior_ref[y].astype(jnp.float32), 0.0).astype(jnp.bfloat16) for y in span]
+        states = jnp.concatenate(states, axis=1)
         deltas = jnp.concatenate([delta_ref[y * channels : (y + 1) * channels, :] for y in span], axis=1)
         grad_lift += dot_nt(states, deltas)
     for i in range(3):
@@ -553,7 +572,7 @@
     edges = jnp.stack([top, bottom])
     sides = jnp.concatenate([left, right], axis=1)
     part, lift, conv, back, contract = convolve(prior, edges, lift_weight, kernel)
-    act, stack, forecast, estimate = finish(part, prior, sides, lift, conv, readout_weights)
+    act, stack, forecast = finish(part, prior, sides, lift, conv, readout_weights)
     remapped, packed, slope, moment = backward(
         arrived, prior, edges, stack, lift, act, forecast, readout_weights, capacity, norm
     )
@@ -563,8 +582,8 @@
     part = sum_over(part, "lon", 2, lon_count)
     grad_kernel, grad_lift, grad_head = unpack(part, swap(part, "lon", 1), channels, fields)
     return (
-        remapped,
-        estimate,
+        remapped.astype(jnp.bfloat16),
+        forecast.astype(jnp.bfloat16),
         grad_lift,
         grad_kernel,
         grad_head.T,

time: 55.8 us -> 54.2 us (0.971)
  Pallas kernels: 14.9 us -> 13 us
  other arithmetic: 0.19 us -> 1.53 us
  waiting for transfers between devices: 16.3 us -> 15.1 us
    ppermute x8, waiting for transfers between devices: 11.2 us -> 9.32 us  [swap(): lax.ppermute(x, axis, [(i, i ^ bit) for i in range(lax.axis_size(axis))])]
    convert_element_type x0 -> x2, other arithmetic: none -> 1.34 us  [the longest x1 0.67 us: per_device(): forecast.astype(jnp.bfloat16)]
    pallas_call x1, Pallas kernels: 4.19 us -> 3.42 us  [regrid(): pl.pallas_call(functools.partial(regrid_kernel, capacity), out_shape=jax....]
    pallas_call x1, Pallas kernels: 2.63 us -> 1.96 us  [finish(): pl.pallas_call(finish_kernel, out_shape=(jax.ShapeDtypeStruct(part.shape,...]
    all_to_all x1, waiting for transfers between devices: 1.36 us -> 2.02 us  [per_device(): lax.all_to_all(outgoing, ('face', 'lon'), split_axis=0, concat_axis=0, ti...]
  transfers between devices with their start and end apart: 13 -> 13, of which waited for: 9 -> 8; matrix products, arithmetic and copies ran while one was open for 1% -> 4% of each run, Pallas kernels for 11% -> 10%
where the time goes in v3:
time: 54.2 us; the launch traced here: 54 us
  starting transfers between devices  22.8 us (42%)
  waiting for transfers between devices  15.1 us (28%)
  Pallas kernels  13 us (24%)
  other arithmetic  1.53 us (3%)
  between operations  0.84 us (2%)
  local copies, waits for them, and re-layouts  0.6 us (1%)
    ppermute x8, waiting for transfers between devices, swap(): lax.ppermute(x, axis, [(i, i ^ bit) for i in range(lax.axis_size(axis))])  9.32 us
    ppermute x8, starting transfers between devices, swap(): lax.ppermute(x, axis, [(i, i ^ bit) for i in range(lax.axis_size(axis))])  8.15 us
    all_to_all x1, starting transfers between devices, per_device(): lax.all_to_all(outgoing, ('face', 'lon'), split_axis=0, concat_axis=0, ti...  7.31 us
    ppermute x2, starting transfers between devices, pair_swap(): lax.ppermute(jnp.where(even, odd_sends, even_sends), axis, inner)  4.55 us
    pallas_call x1, Pallas kernels, regrid(): pl.pallas_call(functools.partial(regrid_kernel, capacity), out_shape=jax....  3.42 us
    pallas_call x1, Pallas kernels, backward(): pl.pallas_call(functools.partial(backward_kernel, capacity, channels, nor...  3.3 us
    ppermute x2, starting transfers between devices, pair_swap(): lax.ppermute(jnp.where(even, even_sends, odd_sends), axis, outer)  2.85 us
    ppermute x2, waiting for transfers between devices, pair_swap(): lax.ppermute(jnp.where(even, even_sends, odd_sends), axis, outer)  2.43 us
  transfers between devices with their start and end apart: 13, of which 8 were waited for; matrix products, arithmetic and copies ran while one was open for 4% of the time, Pallas kernels for 10%

profile of v3, /device:TPU:0, one launch (start us, length us, event | category | flops | bytes accessed | tf_op | source)
XLA Modules:
  0.0 54.0 jit_solution(16545089582223820421)
XLA Ops:
  0.6 3.4 %regrid.1 = bf16[32,9,8,128]{3,2,1,0:T(8,128)(2,1)} custom-call(s32[4,32]{1,0:T(4,128)} %bitcast.29, s32[4,32]{1,0:T(4,128)} %bitcast.30, bf16[32,8,128]{2,1,0:T(8,128)(2,1)} %src_hbm.1, bf16[32,4,128,128]{3,2,1,0:T(8,128)(2,1)} %wts_hbm.1), custom_call_target="tpu_custom_call" | custom-call | flops 33554432 | bytes 4194304 | tf_op jit(solution)/shard_map/regrid/pallas_call | solution.py:92
  4.1 7.3 %all-to-all-start = ((bf16[32,9,8,128]{3,2,1,0:T(8,128)(2,1)}), bf16[32,9,8,128]{3,2,1,0:T(8,128)(2,1)S(1)}, u32[]{:S(2)}, u32[]{:S(2)}) async-start(bf16[32,9,8,128]{3,2,1,0:T(8,128)(2,1)} %regrid.1), calls=%async_computation | async-start | bytes 1179648 | tf_op jit(solution)/shard_map/all_to_all | solution.py:558
  11.4 0.1 copy.20
  11.5 0.7 %collective-permute-start = (bf16[8,256]{1,0:T(8,128)(2,1)S(1)}, bf16[8,256]{1,0:T(8,128)(2,1)S(1)}, u32[]{:S(2)}, u32[]{:S(2)}) collective-permute-start(bf16[8,256]{1,0:T(8,128)(2,1)S(1)} %get-tuple-element.47), channel_id=1, source_target_pairs={{8,16},{16,8},{9,17},{17,9},{10,18},{18,10},{11,19},{19,11},{12,20... | collective-permute-start | bytes 12296 | tf_op jit(solution)/shard_map/ppermute | solution.py:531
  12.2 4.5 %collective-permute-start.1 = (bf16[8,256]{1,0:T(8,128)(2,1)S(1)}, bf16[8,256]{1,0:T(8,128)(2,1)S(1)}, u32[]{:S(2)}, u32[]{:S(2)}) collective-permute-start(bf16[8,256]{1,0:T(8,128)(2,1)S(1)} %get-tuple-element.48), channel_id=1, source_target_pairs={{0,8},{8,0},{16,24},{24,16},{1,9},{9,1},{17,25},{25,17},{2,10},{10... | collective-permute-start | bytes 12296 | tf_op jit(solution)/shard_map/ppermute | solution.py:530
  16.8 0.3 copy.15
  17.1 0.1 copy.17.readout_ref
  17.2 1.3 %collective-permute-done.1 = bf16[8,256]{1,0:T(8,128)(2,1)S(1)} collective-permute-done((bf16[8,256]{1,0:T(8,128)(2,1)S(1)}, bf16[8,256]{1,0:T(8,128)(2,1)S(1)}, u32[]{:S(2)}, u32[]{:S(2)}) %collective-permute-start.1) | collective-permute-done | bytes 4128 | tf_op jit(solution)/shard_map/ppermute | solution.py:530
  18.5 0.1 fusion.10
  18.6 0.1 broadcast_select_fusion.5
  18.7 2.2 %collective-permute-start.2 = (bf16[8,128]{1,0:T(8,128)(2,1)S(1)}, bf16[8,128]{1,0:T(8,128)(2,1)S(1)}, u32[]{:S(2)}, u32[]{:S(2)}) collective-permute-start(bf16[8,128]{1,0:T(8,128)(2,1)S(1)} %get-tuple-element.49), channel_id=1, source_target_pairs={{1,2},{2,1},{3,4},{4,3},{5,6},{6,5},{7,0},{0,7},{9,10},{10,9},{11,... | collective-permute-start | bytes 6152 | tf_op jit(solution)/shard_map/ppermute | solution.py:531
  20.9 1.8 %convolve.1 = (f32[2048,256]{1,0:T(8,128)S(1)}, bf16[80,8]{1,0:T(8,128)(2,1)S(1)}, bf16[192,240]{1,0:T(8,128)(2,1)S(1)}, bf16[192,192]{1,0:T(8,128)(2,1)S(1)}, bf16[3,64,192]{2,1,0:T(8,128)(2,1)S(1)}) custom-call(bf16[32,8,256]{2,1,0:T(8,128)(2,1)S(1)} %bitcast.23, bf16[2,8,256]{2,1,0:T(8,128)(2,1)S(1)} %pad_maximum_fusion.1.edge_ref, ...), custom_call_target="tpu_custom_call" | custom-call | flops 754974720 | bytes 4194304 | tf_op jit(solution)/shard_map/convolve/pallas_call | solution.py:168
  22.8 2.4 %collective-permute-done.2 = bf16[8,128]{1,0:T(8,128)(2,1)S(1)} collective-permute-done((bf16[8,128]{1,0:T(8,128)(2,1)S(1)}, bf16[8,128]{1,0:T(8,128)(2,1)S(1)}, u32[]{:S(2)}, u32[]{:S(2)}) %collective-permute-start.2) | collective-permute-done | bytes 2080 | tf_op jit(solution)/shard_map/ppermute | solution.py:531
  25.2 2.0 %finish.1 = (f32[2048,256]{1,0:T(8,128)S(1)}, bf16[240,256]{1,0:T(8,128)(2,1)S(1)}, f32[8,32,256]{2,1,0:T(8,128)S(1)}) custom-call(f32[2048,256]{1,0:T(8,128)S(1)} %get-tuple-element.29.part_ref, bf16[32,8,256]{2,1,0:T(8,128)(2,1)S(1)} %bitcast.24, bf16[8,256]{1,0:T(8,128)(2,1)S(1)} %pad_maximum_fusion.2.side_ref, ...), custom_call_target="tpu_custom_call", output_to_operand_aliasing={{0}: (0, {})} | custom-call | flops 8388608 | bytes 4194304 | tf_op jit(solution)/shard_map/finish/pallas_call | solution.py:236
  27.2 2.0 %all-to-all-done = bf16[32,9,8,128]{3,2,1,0:T(8,128)(2,1)S(1)} async-done(((bf16[32,9,8,128]{3,2,1,0:T(8,128)(2,1)}), bf16[32,9,8,128]{3,2,1,0:T(8,128)(2,1)S(1)}, u32[]{:S(2)}, u32[]{:S(2)}) %all-to-all-start) | async-done | bytes 589856 | tf_op jit(solution)/shard_map/all_to_all | solution.py:558
  29.2 3.3 %backward.1 = (f32[8,32,256]{2,1,0:T(8,128)S(1)}, f32[2,152,128]{2,1,0:T(8,128)S(1)}, bf16[2176,256]{1,0:T(8,128)(2,1)S(1)}, f32[3,8,192]{2,1,0:T(8,128)S(1)}) custom-call(bf16[32,72,128]{2,1,0:T(8,128)(2,1)S(1)} %bitcast.21, bf16[32,8,256]{2,1,0:T(8,128)(2,1)S(1)} %bitcast.25, bf16[2,8,256]{2,1,0:T(8,128)(2,1)S(1)} %pad_maximum_fusion.1.edge_ref, ...), custom_call_target="tpu_custom_call" | custom-call | flops 754974720 | bytes 4194304 | tf_op jit(solution)/shard_map/backward/pallas_call | solution.py:394
  32.6 1.7 %lift_gradient.1 = f32[8,128]{1,0:T(8,128)S(1)} custom-call(bf16[2176,256]{1,0:T(8,128)(2,1)S(1)} %get-tuple-element.38.slope_ref, bf16[32,8,256]{2,1,0:T(8,128)(2,1)S(1)} %bitcast.26, bf16[192,192]{1,0:T(8,128)(2,1)S(1)} %get-tuple-element.39.back_ref, bf16[3,64,192]{2,1,0:T(8,128)(2,1)S(1)} %get-tuple-element.40.contract_ref, ...), custom_call_target="tpu_custom_call" | custom-call | flops 603979776 | bytes 1114112 | tf_op jit(solution)/shard_map/lift_gradient/pallas_call | solution.py:460
  34.3 0.9 %collective-permute-start.6 = (f32[160,128]{1,0:T(8,128)S(1)}, f32[160,128]{1,0:T(8,128)S(1)}, u32[]{:S(2)}, u32[]{:S(2)}) collective-permute-start(f32[160,128]{1,0:T(8,128)S(1)} %pad_maximum_fusion), channel_id=1, source_target_pairs={{0,16},{8,24},{16,0},{24,8},{1,17},{9,25},{17,1},{25,9},{2,18},{10... | collective-permute-start | bytes 245768 | tf_op jit(solution)/shard_map/ppermute | solution.py:508
  35.3 1.5 %collective-permute-start.7 = (f32[160,128]{1,0:T(8,128)S(1)}, f32[160,128]{1,0:T(8,128)S(1)}, u32[]{:S(2)}, u32[]{:S(2)}) collective-permute-start(f32[160,128]{1,0:T(8,128)S(1)} %pad_maximum_fusion), channel_id=1, source_target_pairs={{0,24},{8,16},{16,8},{24,0},{1,25},{9,17},{17,9},{25,1},{2,26},{10... | collective-permute-start | bytes 245768 | tf_op jit(solution)/shard_map/ppermute | solution.py:508
  36.7 1.2 %collective-permute-start.5 = (f32[160,128]{1,0:T(8,128)S(1)}, f32[160,128]{1,0:T(8,128)S(1)}, u32[]{:S(2)}, u32[]{:S(2)}) collective-permute-start(f32[160,128]{1,0:T(8,128)S(1)} %pad_maximum_fusion), channel_id=1, source_target_pairs={{0,8},{8,0},{16,24},{24,16},{1,9},{9,1},{17,25},{25,17},{2,10},{10... | collective-permute-start | bytes 245768 | tf_op jit(solution)/shard_map/ppermute | solution.py:508
  37.9 2.6 %collective-permute-done.6 = f32[160,128]{1,0:T(8,128)S(1)} collective-permute-done((f32[160,128]{1,0:T(8,128)S(1)}, f32[160,128]{1,0:T(8,128)S(1)}, u32[]{:S(2)}, u32[]{:S(2)}) %collective-permute-start.6) | collective-permute-done | bytes 81952 | tf_op jit(solution)/shard_map/ppermute | solution.py:508
  40.5 0.8 %collective-permute-done.7 = f32[160,128]{1,0:T(8,128)S(1)} collective-permute-done((f32[160,128]{1,0:T(8,128)S(1)}, f32[160,128]{1,0:T(8,128)S(1)}, u32[]{:S(2)}, u32[]{:S(2)}) %collective-permute-start.7) | collective-permute-done | bytes 81952 | tf_op jit(solution)/shard_map/ppermute | solution.py:508
  41.3 0.9 %collective-permute-done.5 = f32[160,128]{1,0:T(8,128)S(1)} collective-permute-done((f32[160,128]{1,0:T(8,128)S(1)}, f32[160,128]{1,0:T(8,128)S(1)}, u32[]{:S(2)}, u32[]{:S(2)}) %collective-permute-start.5) | collective-permute-done | bytes 81952 | tf_op jit(solution)/shard_map/ppermute | solution.py:508
  42.2 0.4 collective-permute-start.10
  42.6 2.3 %collective-permute-start.9 = (f32[160,128]{1,0:T(8,128)S(1)}, f32[160,128]{1,0:T(8,128)S(1)}, u32[]{:S(2)}, u32[]{:S(2)}) collective-permute-start(f32[160,128]{1,0:T(8,128)S(1)} %add_add_fusion.1), channel_id=1, source_target_pairs={{0,4},{1,5},{2,6},{3,7},{4,0},{5,1},{6,2},{7,3},{8,12},{9,13},{10,... | collective-permute-start | bytes 245768 | tf_op jit(solution)/shard_map/ppermute | solution.py:508
  44.9 1.8 %collective-permute-start.8 = (f32[160,128]{1,0:T(8,128)S(1)}, f32[160,128]{1,0:T(8,128)S(1)}, u32[]{:S(2)}, u32[]{:S(2)}) collective-permute-start(f32[160,128]{1,0:T(8,128)S(1)} %add_add_fusion.1), channel_id=1, source_target_pairs={{0,2},{1,3},{2,0},{3,1},{4,6},{5,7},{6,4},{7,5},{8,10},{9,11},{10,... | collective-permute-start | bytes 245768 | tf_op jit(solution)/shard_map/ppermute | solution.py:508
  46.7 2.8 %collective-permute-done.10 = f32[160,128]{1,0:T(8,128)S(1)} collective-permute-done((f32[160,128]{1,0:T(8,128)S(1)}, f32[160,128]{1,0:T(8,128)S(1)}, u32[]{:S(2)}, u32[]{:S(2)}) %collective-permute-start.10) | collective-permute-done | bytes 81952 | tf_op jit(solution)/shard_map/ppermute | solution.py:508
  49.5 2.2 %collective-permute-done.9 = f32[160,128]{1,0:T(8,128)S(1)} collective-permute-done((f32[160,128]{1,0:T(8,128)S(1)}, f32[160,128]{1,0:T(8,128)S(1)}, u32[]{:S(2)}, u32[]{:S(2)}) %collective-permute-start.9) | collective-permute-done | bytes 81952 | tf_op jit(solution)/shard_map/ppermute | solution.py:508
  51.7 0.1 collective-permute-start.11
  51.8 0.7 %convert_element_type.10 = bf16[8,32,256]{2,1,0:T(8,128)(2,1)} convert(f32[8,32,256]{2,1,0:T(8,128)S(1)} %get-tuple-element.35.forecast_ref) | non-fusion elementwise | flops 65536 | bytes 393216 | tf_op jit(solution)/shard_map/convert_element_type | solution.py:586
  52.5 0.7 %convert_element_type.9 = bf16[8,32,256]{2,1,0:T(8,128)(2,1)} convert(f32[8,32,256]{2,1,0:T(8,128)S(1)} %get-tuple-element.36) | non-fusion elementwise | flops 65536 | bytes 393216 | tf_op jit(solution)/shard_map/convert_element_type | solution.py:585
  53.1 0.8 %unpack.1 = (f32[9,64,64]{2,1,0:T(8,128)}, f32[8,64]{1,0:T(8,128)}, f32[8,64]{1,0:T(8,128)}) custom-call(f32[160,128]{1,0:T(8,128)S(1)} %add_add_fusion.mine_ref, f32[160,128]{1,0:T(8,128)S(1)} %collective-permute-done.11.other_ref), custom_call_target="tpu_custom_call" | custom-call | tf_op jit(solution)/shard_map/unpack/pallas_call | solution.py:495
  (26 shorter events, 0.2 us)
Async XLA Ops:
  0.6 10.8 %copy-start.2 = (bf16[8,32,256]{2,1,0:T(8,128)(2,1)S(1)}, bf16[8,32,256]{2,1,0:T(8,128)(2,1)}, u32[]{:S(2)}) copy-start(bf16[8,32,256]{2,1,0:T(8,128)(2,1)} %param.12) | copy-start | bytes 393220
  4.1 13.0 %copy-start.3 = (bf16[64,8]{0,1:T(8,128)(2,1)S(1)}, bf16[64,8]{0,1:T(8,128)(2,1)}, u32[]{:S(2)}) copy-start(bf16[64,8]{0,1:T(8,128)(2,1)} %param.15) | copy-start | bytes 3076
  4.1 16.8 %copy-start = (bf16[9,64,64]{2,1,0:T(8,128)(2,1)S(1)}, bf16[9,64,64]{2,1,0:T(8,128)(2,1)}, u32[]{:S(2)}) copy-start(bf16[9,64,64]{2,1,0:T(8,128)(2,1)} %kernel_ref) | copy-start | bytes 221188
  4.1 16.8 %copy-start.1 = (bf16[8,64]{1,0:T(8,128)(2,1)S(1)}, bf16[8,64]{1,0:T(8,128)(2,1)}, u32[]{:S(2)}) copy-start(bf16[8,64]{1,0:T(8,128)(2,1)} %lift_weight_ref) | copy-start | bytes 3076
  4.1 25.1 %all-to-all-start = ((bf16[32,9,8,128]{3,2,1,0:T(8,128)(2,1)}), bf16[32,9,8,128]{3,2,1,0:T(8,128)(2,1)S(1)}, u32[]{:S(2)}, u32[]{:S(2)}) async-start(bf16[32,9,8,128]{3,2,1,0:T(8,128)(2,1)} %regrid.1), calls=%async_computation | async-start | bytes 1179648 | tf_op jit(solution)/shard_map/all_to_all | solution.py:558
  11.5 5.7 %collective-permute-start = (bf16[8,256]{1,0:T(8,128)(2,1)S(1)}, bf16[8,256]{1,0:T(8,128)(2,1)S(1)}, u32[]{:S(2)}, u32[]{:S(2)}) collective-permute-start(bf16[8,256]{1,0:T(8,128)(2,1)S(1)} %get-tuple-element.47), channel_id=1, source_target_pairs={{8,16},{16,8},{9,17},{17,9},{10,18},{18,10},{11,19},{19,11},{12,20... | collective-permute-start | bytes 12296 | tf_op jit(solution)/shard_map/ppermute | solution.py:531
  12.2 6.3 %collective-permute-start.1 = (bf16[8,256]{1,0:T(8,128)(2,1)S(1)}, bf16[8,256]{1,0:T(8,128)(2,1)S(1)}, u32[]{:S(2)}, u32[]{:S(2)}) collective-permute-start(bf16[8,256]{1,0:T(8,128)(2,1)S(1)} %get-tuple-element.48), channel_id=1, source_target_pairs={{0,8},{8,0},{16,24},{24,16},{1,9},{9,1},{17,25},{25,17},{2,10},{10... | collective-permute-start | bytes 12296 | tf_op jit(solution)/shard_map/ppermute | solution.py:530
  18.7 6.5 %collective-permute-start.2 = (bf16[8,128]{1,0:T(8,128)(2,1)S(1)}, bf16[8,128]{1,0:T(8,128)(2,1)S(1)}, u32[]{:S(2)}, u32[]{:S(2)}) collective-permute-start(bf16[8,128]{1,0:T(8,128)(2,1)S(1)} %get-tuple-element.49), channel_id=1, source_target_pairs={{1,2},{2,1},{3,4},{4,3},{5,6},{6,5},{7,0},{0,7},{9,10},{10,9},{11,... | collective-permute-start | bytes 6152 | tf_op jit(solution)/shard_map/ppermute | solution.py:531
  20.9 4.3 %collective-permute-start.3 = (bf16[8,128]{1,0:T(8,128)(2,1)S(1)}, bf16[8,128]{1,0:T(8,128)(2,1)S(1)}, u32[]{:S(2)}, u32[]{:S(2)}) collective-permute-start(bf16[8,128]{1,0:T(8,128)(2,1)S(1)} %get-tuple-element.50), channel_id=1, source_target_pairs={{0,1},{1,0},{2,3},{3,2},{4,5},{5,4},{6,7},{7,6},{8,9},{9,8},{10,11... | collective-permute-start | bytes 6152 | tf_op jit(solution)/shard_map/ppermute | solution.py:530
  32.5 1.8 %collective-permute-start.4 = (f32[152,128]{1,0:T(8,128)S(1)}, f32[152,128]{1,0:T(8,128)S(1)}, u32[]{:S(2)}, u32[]{:S(2)}) collective-permute-start(f32[152,128]{1,0:T(8,128)S(1)} %slice_bitcast_fusion), channel_id=1, source_target_pairs={{0,1},{1,0},{2,3},{3,2},{4,5},{5,4},{6,7},{7,6},{8,9},{9,8},{10,11... | collective-permute-start | bytes 233480 | tf_op jit(solution)/shard_map/ppermute | solution.py:508
  34.3 6.2 %collective-permute-start.6 = (f32[160,128]{1,0:T(8,128)S(1)}, f32[160,128]{1,0:T(8,128)S(1)}, u32[]{:S(2)}, u32[]{:S(2)}) collective-permute-start(f32[160,128]{1,0:T(8,128)S(1)} %pad_maximum_fusion), channel_id=1, source_target_pairs={{0,16},{8,24},{16,0},{24,8},{1,17},{9,25},{17,1},{25,9},{2,18},{10... | collective-permute-start | bytes 245768 | tf_op jit(solution)/shard_map/ppermute | solution.py:508
  35.3 6.0 %collective-permute-start.7 = (f32[160,128]{1,0:T(8,128)S(1)}, f32[160,128]{1,0:T(8,128)S(1)}, u32[]{:S(2)}, u32[]{:S(2)}) collective-permute-start(f32[160,128]{1,0:T(8,128)S(1)} %pad_maximum_fusion), channel_id=1, source_target_pairs={{0,24},{8,16},{16,8},{24,0},{1,25},{9,17},{17,9},{25,1},{2,26},{10... | collective-permute-start | bytes 245768 | tf_op jit(solution)/shard_map/ppermute | solution.py:508
  36.7 5.5 %collective-permute-start.5 = (f32[160,128]{1,0:T(8,128)S(1)}, f32[160,128]{1,0:T(8,128)S(1)}, u32[]{:S(2)}, u32[]{:S(2)}) collective-permute-start(f32[160,128]{1,0:T(8,128)S(1)} %pad_maximum_fusion), channel_id=1, source_target_pairs={{0,8},{8,0},{16,24},{24,16},{1,9},{9,1},{17,25},{25,17},{2,10},{10... | collective-permute-start | bytes 245768 | tf_op jit(solution)/shard_map/ppermute | solution.py:508
  42.2 7.2 %collective-permute-start.10 = (f32[160,128]{1,0:T(8,128)S(1)}, f32[160,128]{1,0:T(8,128)S(1)}, u32[]{:S(2)}, u32[]{:S(2)}) collective-permute-start(f32[160,128]{1,0:T(8,128)S(1)} %add_add_fusion.1), channel_id=1, source_target_pairs={{0,6},{1,7},{2,4},{3,5},{4,2},{5,3},{6,0},{7,1},{8,14},{9,15},{10,... | collective-permute-start | bytes 245768 | tf_op jit(solution)/shard_map/ppermute | solution.py:508
  42.6 9.0 %collective-permute-start.9 = (f32[160,128]{1,0:T(8,128)S(1)}, f32[160,128]{1,0:T(8,128)S(1)}, u32[]{:S(2)}, u32[]{:S(2)}) collective-permute-start(f32[160,128]{1,0:T(8,128)S(1)} %add_add_fusion.1), channel_id=1, source_target_pairs={{0,4},{1,5},{2,6},{3,7},{4,0},{5,1},{6,2},{7,3},{8,12},{9,13},{10,... | collective-permute-start | bytes 245768 | tf_op jit(solution)/shard_map/ppermute | solution.py:508
  44.9 6.8 %collective-permute-start.8 = (f32[160,128]{1,0:T(8,128)S(1)}, f32[160,128]{1,0:T(8,128)S(1)}, u32[]{:S(2)}, u32[]{:S(2)}) collective-permute-start(f32[160,128]{1,0:T(8,128)S(1)} %add_add_fusion.1), channel_id=1, source_target_pairs={{0,2},{1,3},{2,0},{3,1},{4,6},{5,7},{6,4},{7,5},{8,10},{9,11},{10,... | collective-permute-start | bytes 245768 | tf_op jit(solution)/shard_map/ppermute | solution.py:508
  51.7 1.4 %collective-permute-start.11 = (f32[160,128]{1,0:T(8,128)S(1)}, f32[160,128]{1,0:T(8,128)S(1)}, u32[]{:S(2)}, u32[]{:S(2)}) collective-permute-start(f32[160,128]{1,0:T(8,128)S(1)} %add_add_fusion.mine_ref), channel_id=1, source_target_pairs={{0,1},{1,0},{2,3},{3,2},{4,5},{5,4},{6,7},{7,6},{8,9},{9,8},{10,11... | collective-permute-start | bytes 245768 | tf_op jit(solution)/shard_map/ppermute | solution.py:508

commit v4 on v3

--- a/solution.py
+++ b/solution.py
@@ -376,20 +376,19 @@
     packed = [t[:, : 2 * channels] for t in taps]
     packed.append(jnp.concatenate(last[:2], axis=1))
     packed.append(jnp.concatenate([last[2][:half], last[2][half:]], axis=1))
-    packed.append(jnp.concatenate([grad_head, jnp.zeros_like(grad_head)], axis=1))
-    packed.append(jnp.zeros((8, 2 * channels), jnp.float32))
     packed = jnp.concatenate(packed, axis=0)
     cut = packed.shape[0] // 2
+    head = jnp.concatenate([grad_head, jnp.zeros_like(grad_head)], axis=1)
     odd = lax.rem(lax.axis_index("lon"), 2)
-    packed_ref[odd] = packed[:cut]
-    packed_ref[1 - odd] = packed[cut:]
+    packed_ref[odd] = jnp.concatenate([packed[:cut], head], axis=0)
+    packed_ref[1 - odd] = jnp.concatenate([packed[cut:], jnp.zeros_like(head)], axis=0)
 
 
 def backward(arrived, prior, edges, stack, lift, act, forecast, readout, capacity, norm):
     fields, rows, width = forecast.shape
     channels = readout.shape[0]
     pitch = lift.shape[0]
-    packed_rows = (3 * channels + channels + channels // 2 + fields + 8) // 2
+    packed_rows = (3 * channels + channels + channels // 2) // 2 + fields
     vmem = pl.BlockSpec(memory_space=pltpu.VMEM)
     return pl.pallas_call(
         functools.partial(backward_kernel, capacity, channels, norm),
@@ -436,30 +435,33 @@
         )
         delta = grad.astype(jnp.bfloat16).astype(jnp.float32) - grad
         delta_ref[y * channels : (y + 1) * channels, :] = delta.astype(jnp.bfloat16)
-    grad_lift = jnp.zeros((fields, channels), jnp.float32)
+    crossed = jnp.zeros((channels, fields), jnp.float32)
     batch = 4
     for first in range(0, rows, batch):
         span = range(first, first + batch)
         states = [jnp.where(inside, prior_ref[y].astype(jnp.float32), 0.0).astype(jnp.bfloat16) for y in span]
         states = jnp.concatenate(states, axis=1)
         deltas = jnp.concatenate([delta_ref[y * channels : (y + 1) * channels, :] for y in span], axis=1)
-        grad_lift += dot_nt(states, deltas)
+        crossed += dot_nt(deltas, states)
+    grad_lift = crossed.T
     for i in range(3):
-        rest = moment_ref[i]
+        rest, pieces = moment_ref[i], []
         for _ in range(3):
-            piece = rest.astype(jnp.bfloat16)
-            rest = rest - piece.astype(jnp.float32)
-            grad_lift += dot_nt(piece, contract_ref[i])
-    out_ref[...] = jnp.concatenate([grad_lift, jnp.zeros_like(grad_lift)], axis=1)
-
-
-def lift_gradient(slope, prior, back, contract, moment):
+            pieces.append(rest.astype(jnp.bfloat16).astype(jnp.float32))
+            rest = rest - pieces[-1]
+        part = dot_nt(jnp.concatenate(pieces, axis=0).astype(jnp.bfloat16), contract_ref[i])
+        grad_lift += part[:fields] + part[fields : 2 * fields] + part[2 * fields :]
+    out_ref[...] = jnp.zeros_like(out_ref)
+    out_ref[-fields:, channels:] = grad_lift
+
+
+def lift_gradient(slope, prior, back, contract, moment, packed_rows):
     rows, fields, width = prior.shape
     channels = contract.shape[1]
     vmem = pl.BlockSpec(memory_space=pltpu.VMEM)
     return pl.pallas_call(
         lift_gradient_kernel,
-        out_shape=jax.ShapeDtypeStruct((fields, 2 * channels), jnp.float32),
+        out_shape=jax.ShapeDtypeStruct((packed_rows, 2 * channels), jnp.float32),
         in_specs=[vmem] * 5,
         out_specs=vmem,
         scratch_shapes=[pltpu.VMEM((rows * channels, width), jnp.bfloat16)],
@@ -474,7 +476,9 @@
 def unpack_kernel(channels, mine_ref, other_ref, kernel_ref, lift_ref, head_ref):
     odd = lax.rem(lax.axis_index("lon"), 2) == 1
     fields = lift_ref.shape[0]
-    lift_ref[...] = (mine_ref[-fields:, :] + other_ref[-fields:, :])[:, :channels]
+    mine, other = mine_ref[-fields:, :], other_ref[-fields:, :]
+    lift_ref[...] = (mine + other)[:, channels:]
+    head_ref[...] = jnp.where(odd, other, mine)[:, :channels]
     mine, other = mine_ref[:-fields, :], other_ref[:-fields, :]
     packed = jnp.concatenate([jnp.where(odd, other, mine), jnp.where(odd, mine, other)], axis=0)
     half = channels // 2
@@ -488,7 +492,6 @@
     block = packed[4 * channels : 4 * channels + half]
     kernel_ref[8, :half] = block[:, :channels]
     kernel_ref[8, half:] = block[:, channels:]
-    head_ref[...] = packed[4 * channels + half : 4 * channels + half + fields, :channels]
 
 
 def unpack(mine, other, channels, fields):
@@ -576,8 +579,8 @@
     remapped, packed, slope, moment = backward(
         arrived, prior, edges, stack, lift, act, forecast, readout_weights, capacity, norm
     )
-    part = packed[0] + swap(packed[1], "lon", 1)
-    part = jnp.concatenate([part, lift_gradient(slope, prior, back, contract, moment)])
+    lift_part = lift_gradient(slope, prior, back, contract, moment, packed.shape[1])
+    part = packed[0] + swap(packed[1], "lon", 1) + lift_part
     part = sum_over(part, "face", 1, face_count)
     part = sum_over(part, "lon", 2, lon_count)
     grad_kernel, grad_lift, grad_head = unpack(part, swap(part, "lon", 1), channels, fields)

time: 54.2 us -> 53.6 us (0.989)
  transfers between devices with their start and end apart: 13 -> 13, of which waited for: 8 -> 7; matrix products, arithmetic and copies ran while one was open for 4% -> 4% of each run, Pallas kernels for 10% -> 10%
where the time goes in v4:
time: 53.6 us; the launch traced here: 53.3 us
  starting transfers between devices  22.8 us (43%)
  waiting for transfers between devices  14.6 us (27%)
  Pallas kernels  13 us (24%)
  other arithmetic  1.51 us (3%)
  between operations  0.84 us (2%)
  local copies, waits for them, and re-layouts  0.6 us (1%)
    ppermute x8, waiting for transfers between devices, swap(): lax.ppermute(x, axis, [(i, i ^ bit) for i in range(lax.axis_size(axis))])  8.78 us
    ppermute x8, starting transfers between devices, swap(): lax.ppermute(x, axis, [(i, i ^ bit) for i in range(lax.axis_size(axis))])  8.15 us
    all_to_all x1, starting transfers between devices, per_device(): lax.all_to_all(outgoing, ('face', 'lon'), split_axis=0, concat_axis=0, ti...  7.3 us
    ppermute x2, starting transfers between devices, pair_swap(): lax.ppermute(jnp.where(even, odd_sends, even_sends), axis, inner)  4.55 us
    pallas_call x1, Pallas kernels, regrid(): pl.pallas_call(functools.partial(regrid_kernel, capacity), out_shape=jax....  3.42 us
    pallas_call x1, Pallas kernels, backward(): pl.pallas_call(functools.partial(backward_kernel, capacity, channels, nor...  3.28 us
    ppermute x2, starting transfers between devices, pair_swap(): lax.ppermute(jnp.where(even, even_sends, odd_sends), axis, outer)  2.85 us
    ppermute x2, waiting for transfers between devices, pair_swap(): lax.ppermute(jnp.where(even, even_sends, odd_sends), axis, outer)  2.43 us
  transfers between devices with their start and end apart: 13, of which 7 were waited for; matrix products, arithmetic and copies ran while one was open for 4% of the time, Pallas kernels for 10%

profile of v4, /device:TPU:0, one launch (start us, length us, event | category | flops | bytes accessed | tf_op | source)
XLA Modules:
  0.0 53.3 jit_solution(11274237051389219604)
XLA Ops:
  0.6 3.4 %regrid.1 = bf16[32,9,8,128]{3,2,1,0:T(8,128)(2,1)} custom-call(s32[4,32]{1,0:T(4,128)} %bitcast.31, s32[4,32]{1,0:T(4,128)} %bitcast.32, bf16[32,8,128]{2,1,0:T(8,128)(2,1)} %src_hbm.1, bf16[32,4,128,128]{3,2,1,0:T(8,128)(2,1)} %wts_hbm.1), custom_call_target="tpu_custom_call" | custom-call | flops 33554432 | bytes 4194304 | tf_op jit(solution)/shard_map/regrid/pallas_call | solution.py:92
  4.1 7.3 %all-to-all-start = ((bf16[32,9,8,128]{3,2,1,0:T(8,128)(2,1)}), bf16[32,9,8,128]{3,2,1,0:T(8,128)(2,1)S(1)}, u32[]{:S(2)}, u32[]{:S(2)}) async-start(bf16[32,9,8,128]{3,2,1,0:T(8,128)(2,1)} %regrid.1), calls=%async_computation | async-start | bytes 1179648 | tf_op jit(solution)/shard_map/all_to_all | solution.py:561
  11.4 0.1 copy.20
  11.5 0.7 %collective-permute-start = (bf16[8,256]{1,0:T(8,128)(2,1)S(1)}, bf16[8,256]{1,0:T(8,128)(2,1)S(1)}, u32[]{:S(2)}, u32[]{:S(2)}) collective-permute-start(bf16[8,256]{1,0:T(8,128)(2,1)S(1)} %get-tuple-element.47), channel_id=1, source_target_pairs={{8,16},{16,8},{9,17},{17,9},{10,18},{18,10},{11,19},{19,11},{12,20... | collective-permute-start | bytes 12296 | tf_op jit(solution)/shard_map/ppermute | solution.py:534
  12.2 4.5 %collective-permute-start.1 = (bf16[8,256]{1,0:T(8,128)(2,1)S(1)}, bf16[8,256]{1,0:T(8,128)(2,1)S(1)}, u32[]{:S(2)}, u32[]{:S(2)}) collective-permute-start(bf16[8,256]{1,0:T(8,128)(2,1)S(1)} %get-tuple-element.48), channel_id=1, source_target_pairs={{0,8},{8,0},{16,24},{24,16},{1,9},{9,1},{17,25},{25,17},{2,10},{10... | collective-permute-start | bytes 12296 | tf_op jit(solution)/shard_map/ppermute | solution.py:533
  16.8 0.3 copy.15
  17.1 0.1 copy.17.readout_ref
  17.2 1.3 %collective-permute-done.1 = bf16[8,256]{1,0:T(8,128)(2,1)S(1)} collective-permute-done((bf16[8,256]{1,0:T(8,128)(2,1)S(1)}, bf16[8,256]{1,0:T(8,128)(2,1)S(1)}, u32[]{:S(2)}, u32[]{:S(2)}) %collective-permute-start.1) | collective-permute-done | bytes 4128 | tf_op jit(solution)/shard_map/ppermute | solution.py:533
  18.5 0.1 fusion.11
  18.6 0.1 broadcast_select_fusion.5
  18.7 2.2 %collective-permute-start.2 = (bf16[8,128]{1,0:T(8,128)(2,1)S(1)}, bf16[8,128]{1,0:T(8,128)(2,1)S(1)}, u32[]{:S(2)}, u32[]{:S(2)}) collective-permute-start(bf16[8,128]{1,0:T(8,128)(2,1)S(1)} %get-tuple-element.49), channel_id=1, source_target_pairs={{1,2},{2,1},{3,4},{4,3},{5,6},{6,5},{7,0},{0,7},{9,10},{10,9},{11,... | collective-permute-start | bytes 6152 | tf_op jit(solution)/shard_map/ppermute | solution.py:534
  20.9 1.8 %convolve.1 = (f32[2048,256]{1,0:T(8,128)S(1)}, bf16[80,8]{1,0:T(8,128)(2,1)S(1)}, bf16[192,240]{1,0:T(8,128)(2,1)S(1)}, bf16[192,192]{1,0:T(8,128)(2,1)S(1)}, bf16[3,64,192]{2,1,0:T(8,128)(2,1)S(1)}) custom-call(bf16[32,8,256]{2,1,0:T(8,128)(2,1)S(1)} %bitcast.25, bf16[2,8,256]{2,1,0:T(8,128)(2,1)S(1)} %pad_maximum_fusion.edge_ref, ...), custom_call_target="tpu_custom_call" | custom-call | flops 754974720 | bytes 4194304 | tf_op jit(solution)/shard_map/convolve/pallas_call | solution.py:168
  22.8 2.4 %collective-permute-done.2 = bf16[8,128]{1,0:T(8,128)(2,1)S(1)} collective-permute-done((bf16[8,128]{1,0:T(8,128)(2,1)S(1)}, bf16[8,128]{1,0:T(8,128)(2,1)S(1)}, u32[]{:S(2)}, u32[]{:S(2)}) %collective-permute-start.2) | collective-permute-done | bytes 2080 | tf_op jit(solution)/shard_map/ppermute | solution.py:534
  25.2 2.0 %finish.1 = (f32[2048,256]{1,0:T(8,128)S(1)}, bf16[240,256]{1,0:T(8,128)(2,1)S(1)}, f32[8,32,256]{2,1,0:T(8,128)S(1)}) custom-call(f32[2048,256]{1,0:T(8,128)S(1)} %get-tuple-element.29.part_ref, bf16[32,8,256]{2,1,0:T(8,128)(2,1)S(1)} %bitcast.26, bf16[8,256]{1,0:T(8,128)(2,1)S(1)} %pad_maximum_fusion.1.side_ref, ...), custom_call_target="tpu_custom_call", output_to_operand_aliasing={{0}: (0, {})} | custom-call | flops 8388608 | bytes 4194304 | tf_op jit(solution)/shard_map/finish/pallas_call | solution.py:236
  27.2 2.0 %all-to-all-done = bf16[32,9,8,128]{3,2,1,0:T(8,128)(2,1)S(1)} async-done(((bf16[32,9,8,128]{3,2,1,0:T(8,128)(2,1)}), bf16[32,9,8,128]{3,2,1,0:T(8,128)(2,1)S(1)}, u32[]{:S(2)}, u32[]{:S(2)}) %all-to-all-start) | async-done | bytes 589856 | tf_op jit(solution)/shard_map/all_to_all | solution.py:561
  29.2 3.3 %backward.1 = (f32[8,32,256]{2,1,0:T(8,128)S(1)}, f32[2,152,128]{2,1,0:T(8,128)S(1)}, bf16[2176,256]{1,0:T(8,128)(2,1)S(1)}, f32[3,8,192]{2,1,0:T(8,128)S(1)}) custom-call(bf16[32,72,128]{2,1,0:T(8,128)(2,1)S(1)} %bitcast.23, bf16[32,8,256]{2,1,0:T(8,128)(2,1)S(1)} %bitcast.27, bf16[2,8,256]{2,1,0:T(8,128)(2,1)S(1)} %pad_maximum_fusion.edge_ref, ...), custom_call_target="tpu_custom_call" | custom-call | flops 754974720 | bytes 4194304 | tf_op jit(solution)/shard_map/backward/pallas_call | solution.py:393
  32.5 0.1 collective-permute-start.4
  32.6 1.6 %lift_gradient.1 = f32[152,128]{1,0:T(8,128)S(1)} custom-call(bf16[2176,256]{1,0:T(8,128)(2,1)S(1)} %get-tuple-element.38.slope_ref, bf16[32,8,256]{2,1,0:T(8,128)(2,1)S(1)} %bitcast.28, bf16[192,192]{1,0:T(8,128)(2,1)S(1)} %get-tuple-element.39.back_ref, bf16[3,64,192]{2,1,0:T(8,128)(2,1)S(1)} %get-tuple-element.40.contract_ref, ...), custom_call_target="tpu_custom_call" | custom-call | flops 603979776 | bytes 1114112 | tf_op jit(solution)/shard_map/lift_gradient/pallas_call | solution.py:462
  34.2 0.9 %collective-permute-start.7 = (f32[152,128]{1,0:T(8,128)S(1)}, f32[152,128]{1,0:T(8,128)S(1)}, u32[]{:S(2)}, u32[]{:S(2)}) collective-permute-start(f32[152,128]{1,0:T(8,128)S(1)} %fusion), channel_id=1, source_target_pairs={{0,24},{8,16},{16,8},{24,0},{1,25},{9,17},{17,9},{25,1},{2,26},{10... | collective-permute-start | bytes 233480 | tf_op jit(solution)/shard_map/ppermute | solution.py:511
  35.1 1.5 %collective-permute-start.6 = (f32[152,128]{1,0:T(8,128)S(1)}, f32[152,128]{1,0:T(8,128)S(1)}, u32[]{:S(2)}, u32[]{:S(2)}) collective-permute-start(f32[152,128]{1,0:T(8,128)S(1)} %fusion), channel_id=1, source_target_pairs={{0,16},{8,24},{16,0},{24,8},{1,17},{9,25},{17,1},{25,9},{2,18},{10... | collective-permute-start | bytes 233480 | tf_op jit(solution)/shard_map/ppermute | solution.py:511
  36.6 1.2 %collective-permute-start.5 = (f32[152,128]{1,0:T(8,128)S(1)}, f32[152,128]{1,0:T(8,128)S(1)}, u32[]{:S(2)}, u32[]{:S(2)}) collective-permute-start(f32[152,128]{1,0:T(8,128)S(1)} %fusion), channel_id=1, source_target_pairs={{0,8},{8,0},{16,24},{24,16},{1,9},{9,1},{17,25},{25,17},{2,10},{10... | collective-permute-start | bytes 233480 | tf_op jit(solution)/shard_map/ppermute | solution.py:511
  37.8 2.6 %collective-permute-done.7 = f32[152,128]{1,0:T(8,128)S(1)} collective-permute-done((f32[152,128]{1,0:T(8,128)S(1)}, f32[152,128]{1,0:T(8,128)S(1)}, u32[]{:S(2)}, u32[]{:S(2)}) %collective-permute-start.7) | collective-permute-done | bytes 77856 | tf_op jit(solution)/shard_map/ppermute | solution.py:511
  40.4 0.6 %collective-permute-done.6 = f32[152,128]{1,0:T(8,128)S(1)} collective-permute-done((f32[152,128]{1,0:T(8,128)S(1)}, f32[152,128]{1,0:T(8,128)S(1)}, u32[]{:S(2)}, u32[]{:S(2)}) %collective-permute-start.6) | collective-permute-done | bytes 77856 | tf_op jit(solution)/shard_map/ppermute | solution.py:511
  41.0 1.1 %collective-permute-start.10 = (f32[152,128]{1,0:T(8,128)S(1)}, f32[152,128]{1,0:T(8,128)S(1)}, u32[]{:S(2)}, u32[]{:S(2)}) collective-permute-start(f32[152,128]{1,0:T(8,128)S(1)} %add_add_fusion.1), channel_id=1, source_target_pairs={{0,6},{1,7},{2,4},{3,5},{4,2},{5,3},{6,0},{7,1},{8,14},{9,15},{10,... | collective-permute-start | bytes 233480 | tf_op jit(solution)/shard_map/ppermute | solution.py:511
  42.2 2.3 %collective-permute-start.9 = (f32[152,128]{1,0:T(8,128)S(1)}, f32[152,128]{1,0:T(8,128)S(1)}, u32[]{:S(2)}, u32[]{:S(2)}) collective-permute-start(f32[152,128]{1,0:T(8,128)S(1)} %add_add_fusion.1), channel_id=1, source_target_pairs={{0,4},{1,5},{2,6},{3,7},{4,0},{5,1},{6,2},{7,3},{8,12},{9,13},{10,... | collective-permute-start | bytes 233480 | tf_op jit(solution)/shard_map/ppermute | solution.py:511
  44.5 1.0 %collective-permute-start.8 = (f32[152,128]{1,0:T(8,128)S(1)}, f32[152,128]{1,0:T(8,128)S(1)}, u32[]{:S(2)}, u32[]{:S(2)}) collective-permute-start(f32[152,128]{1,0:T(8,128)S(1)} %add_add_fusion.1), channel_id=1, source_target_pairs={{0,2},{1,3},{2,0},{3,1},{4,6},{5,7},{6,4},{7,5},{8,10},{9,11},{10,... | collective-permute-start | bytes 233480 | tf_op jit(solution)/shard_map/ppermute | solution.py:511
  45.5 2.6 %collective-permute-done.10 = f32[152,128]{1,0:T(8,128)S(1)} collective-permute-done((f32[152,128]{1,0:T(8,128)S(1)}, f32[152,128]{1,0:T(8,128)S(1)}, u32[]{:S(2)}, u32[]{:S(2)}) %collective-permute-start.10) | collective-permute-done | bytes 77856 | tf_op jit(solution)/shard_map/ppermute | solution.py:511
  48.1 2.9 %collective-permute-done.9 = f32[152,128]{1,0:T(8,128)S(1)} collective-permute-done((f32[152,128]{1,0:T(8,128)S(1)}, f32[152,128]{1,0:T(8,128)S(1)}, u32[]{:S(2)}, u32[]{:S(2)}) %collective-permute-start.9) | collective-permute-done | bytes 77856 | tf_op jit(solution)/shard_map/ppermute | solution.py:511
  51.1 0.1 collective-permute-start.11
  51.1 0.7 %convert_element_type.10 = bf16[8,32,256]{2,1,0:T(8,128)(2,1)} convert(f32[8,32,256]{2,1,0:T(8,128)S(1)} %get-tuple-element.35.forecast_ref) | non-fusion elementwise | flops 65536 | bytes 393216 | tf_op jit(solution)/shard_map/convert_element_type | solution.py:589
  51.8 0.7 %convert_element_type.9 = bf16[8,32,256]{2,1,0:T(8,128)(2,1)} convert(f32[8,32,256]{2,1,0:T(8,128)S(1)} %get-tuple-element.36) | non-fusion elementwise | flops 65536 | bytes 393216 | tf_op jit(solution)/shard_map/convert_element_type | solution.py:588
  52.5 0.8 %unpack.1 = (f32[9,64,64]{2,1,0:T(8,128)}, f32[8,64]{1,0:T(8,128)}, f32[8,64]{1,0:T(8,128)}) custom-call(f32[152,128]{1,0:T(8,128)S(1)} %add_add_fusion.mine_ref, f32[152,128]{1,0:T(8,128)S(1)} %collective-permute-done.11.other_ref), custom_call_target="tpu_custom_call" | custom-call | tf_op jit(solution)/shard_map/unpack/pallas_call | solution.py:498
  (25 shorter events, 0.2 us)
Async XLA Ops:
  0.6 10.8 %copy-start.2 = (bf16[8,32,256]{2,1,0:T(8,128)(2,1)S(1)}, bf16[8,32,256]{2,1,0:T(8,128)(2,1)}, u32[]{:S(2)}) copy-start(bf16[8,32,256]{2,1,0:T(8,128)(2,1)} %param.12) | copy-start | bytes 393220
  4.1 13.0 %copy-start.3 = (bf16[64,8]{0,1:T(8,128)(2,1)S(1)}, bf16[64,8]{0,1:T(8,128)(2,1)}, u32[]{:S(2)}) copy-start(bf16[64,8]{0,1:T(8,128)(2,1)} %param.15) | copy-start | bytes 3076
  4.1 16.8 %copy-start = (bf16[9,64,64]{2,1,0:T(8,128)(2,1)S(1)}, bf16[9,64,64]{2,1,0:T(8,128)(2,1)}, u32[]{:S(2)}) copy-start(bf16[9,64,64]{2,1,0:T(8,128)(2,1)} %kernel_ref) | copy-start | bytes 221188
  4.1 16.8 %copy-start.1 = (bf16[8,64]{1,0:T(8,128)(2,1)S(1)}, bf16[8,64]{1,0:T(8,128)(2,1)}, u32[]{:S(2)}) copy-start(bf16[8,64]{1,0:T(8,128)(2,1)} %lift_weight_ref) | copy-start | bytes 3076
  4.1 25.1 %all-to-all-start = ((bf16[32,9,8,128]{3,2,1,0:T(8,128)(2,1)}), bf16[32,9,8,128]{3,2,1,0:T(8,128)(2,1)S(1)}, u32[]{:S(2)}, u32[]{:S(2)}) async-start(bf16[32,9,8,128]{3,2,1,0:T(8,128)(2,1)} %regrid.1), calls=%async_computation | async-start | bytes 1179648 | tf_op jit(solution)/shard_map/all_to_all | solution.py:561
  11.5 5.7 %collective-permute-start = (bf16[8,256]{1,0:T(8,128)(2,1)S(1)}, bf16[8,256]{1,0:T(8,128)(2,1)S(1)}, u32[]{:S(2)}, u32[]{:S(2)}) collective-permute-start(bf16[8,256]{1,0:T(8,128)(2,1)S(1)} %get-tuple-element.47), channel_id=1, source_target_pairs={{8,16},{16,8},{9,17},{17,9},{10,18},{18,10},{11,19},{19,11},{12,20... | collective-permute-start | bytes 12296 | tf_op jit(solution)/shard_map/ppermute | solution.py:534
  12.2 6.3 %collective-permute-start.1 = (bf16[8,256]{1,0:T(8,128)(2,1)S(1)}, bf16[8,256]{1,0:T(8,128)(2,1)S(1)}, u32[]{:S(2)}, u32[]{:S(2)}) collective-permute-start(bf16[8,256]{1,0:T(8,128)(2,1)S(1)} %get-tuple-element.48), channel_id=1, source_target_pairs={{0,8},{8,0},{16,24},{24,16},{1,9},{9,1},{17,25},{25,17},{2,10},{10... | collective-permute-start | bytes 12296 | tf_op jit(solution)/shard_map/ppermute | solution.py:533
  18.7 6.5 %collective-permute-start.2 = (bf16[8,128]{1,0:T(8,128)(2,1)S(1)}, bf16[8,128]{1,0:T(8,128)(2,1)S(1)}, u32[]{:S(2)}, u32[]{:S(2)}) collective-permute-start(bf16[8,128]{1,0:T(8,128)(2,1)S(1)} %get-tuple-element.49), channel_id=1, source_target_pairs={{1,2},{2,1},{3,4},{4,3},{5,6},{6,5},{7,0},{0,7},{9,10},{10,9},{11,... | collective-permute-start | bytes 6152 | tf_op jit(solution)/shard_map/ppermute | solution.py:534
  20.9 4.3 %collective-permute-start.3 = (bf16[8,128]{1,0:T(8,128)(2,1)S(1)}, bf16[8,128]{1,0:T(8,128)(2,1)S(1)}, u32[]{:S(2)}, u32[]{:S(2)}) collective-permute-start(bf16[8,128]{1,0:T(8,128)(2,1)S(1)} %get-tuple-element.50), channel_id=1, source_target_pairs={{0,1},{1,0},{2,3},{3,2},{4,5},{5,4},{6,7},{7,6},{8,9},{9,8},{10,11... | collective-permute-start | bytes 6152 | tf_op jit(solution)/shard_map/ppermute | solution.py:533
  32.5 1.7 %collective-permute-start.4 = (f32[152,128]{1,0:T(8,128)S(1)}, f32[152,128]{1,0:T(8,128)S(1)}, u32[]{:S(2)}, u32[]{:S(2)}) collective-permute-start(f32[152,128]{1,0:T(8,128)S(1)} %slice_bitcast_fusion), channel_id=1, source_target_pairs={{0,1},{1,0},{2,3},{3,2},{4,5},{5,4},{6,7},{7,6},{8,9},{9,8},{10,11... | collective-permute-start | bytes 233480 | tf_op jit(solution)/shard_map/ppermute | solution.py:511
  34.2 6.2 %collective-permute-start.7 = (f32[152,128]{1,0:T(8,128)S(1)}, f32[152,128]{1,0:T(8,128)S(1)}, u32[]{:S(2)}, u32[]{:S(2)}) collective-permute-start(f32[152,128]{1,0:T(8,128)S(1)} %fusion), channel_id=1, source_target_pairs={{0,24},{8,16},{16,8},{24,0},{1,25},{9,17},{17,9},{25,1},{2,26},{10... | collective-permute-start | bytes 233480 | tf_op jit(solution)/shard_map/ppermute | solution.py:511
  35.1 5.9 %collective-permute-start.6 = (f32[152,128]{1,0:T(8,128)S(1)}, f32[152,128]{1,0:T(8,128)S(1)}, u32[]{:S(2)}, u32[]{:S(2)}) collective-permute-start(f32[152,128]{1,0:T(8,128)S(1)} %fusion), channel_id=1, source_target_pairs={{0,16},{8,24},{16,0},{24,8},{1,17},{9,25},{17,1},{25,9},{2,18},{10... | collective-permute-start | bytes 233480 | tf_op jit(solution)/shard_map/ppermute | solution.py:511
  36.6 4.4 %collective-permute-start.5 = (f32[152,128]{1,0:T(8,128)S(1)}, f32[152,128]{1,0:T(8,128)S(1)}, u32[]{:S(2)}, u32[]{:S(2)}) collective-permute-start(f32[152,128]{1,0:T(8,128)S(1)} %fusion), channel_id=1, source_target_pairs={{0,8},{8,0},{16,24},{24,16},{1,9},{9,1},{17,25},{25,17},{2,10},{10... | collective-permute-start | bytes 233480 | tf_op jit(solution)/shard_map/ppermute | solution.py:511
  41.0 7.1 %collective-permute-start.10 = (f32[152,128]{1,0:T(8,128)S(1)}, f32[152,128]{1,0:T(8,128)S(1)}, u32[]{:S(2)}, u32[]{:S(2)}) collective-permute-start(f32[152,128]{1,0:T(8,128)S(1)} %add_add_fusion.1), channel_id=1, source_target_pairs={{0,6},{1,7},{2,4},{3,5},{4,2},{5,3},{6,0},{7,1},{8,14},{9,15},{10,... | collective-permute-start | bytes 233480 | tf_op jit(solution)/shard_map/ppermute | solution.py:511
  42.2 8.9 %collective-permute-start.9 = (f32[152,128]{1,0:T(8,128)S(1)}, f32[152,128]{1,0:T(8,128)S(1)}, u32[]{:S(2)}, u32[]{:S(2)}) collective-permute-start(f32[152,128]{1,0:T(8,128)S(1)} %add_add_fusion.1), channel_id=1, source_target_pairs={{0,4},{1,5},{2,6},{3,7},{4,0},{5,1},{6,2},{7,3},{8,12},{9,13},{10,... | collective-permute-start | bytes 233480 | tf_op jit(solution)/shard_map/ppermute | solution.py:511
  44.5 6.5 %collective-permute-start.8 = (f32[152,128]{1,0:T(8,128)S(1)}, f32[152,128]{1,0:T(8,128)S(1)}, u32[]{:S(2)}, u32[]{:S(2)}) collective-permute-start(f32[152,128]{1,0:T(8,128)S(1)} %add_add_fusion.1), channel_id=1, source_target_pairs={{0,2},{1,3},{2,0},{3,1},{4,6},{5,7},{6,4},{7,5},{8,10},{9,11},{10,... | collective-permute-start | bytes 233480 | tf_op jit(solution)/shard_map/ppermute | solution.py:511
  51.1 1.4 %collective-permute-start.11 = (f32[152,128]{1,0:T(8,128)S(1)}, f32[152,128]{1,0:T(8,128)S(1)}, u32[]{:S(2)}, u32[]{:S(2)}) collective-permute-start(f32[152,128]{1,0:T(8,128)S(1)} %add_add_fusion.mine_ref), channel_id=1, source_target_pairs={{0,1},{1,0},{2,3},{3,2},{4,5},{5,4},{6,7},{7,6},{8,9},{9,8},{10,11... | collective-permute-start | bytes 233480 | tf_op jit(solution)/shard_map/ppermute | solution.py:511

commit v5 on v4

--- a/solution.py
+++ b/solution.py
@@ -582,11 +582,14 @@
     lift_part = lift_gradient(slope, prior, back, contract, moment, packed.shape[1])
     part = packed[0] + swap(packed[1], "lon", 1) + lift_part
     part = sum_over(part, "face", 1, face_count)
+    part, remapped, estimate = lax.optimization_barrier(
+        (part, remapped.astype(jnp.bfloat16), forecast.astype(jnp.bfloat16))
+    )
     part = sum_over(part, "lon", 2, lon_count)
     grad_kernel, grad_lift, grad_head = unpack(part, swap(part, "lon", 1), channels, fields)
     return (
-        remapped.astype(jnp.bfloat16),
-        forecast.astype(jnp.bfloat16),
+        remapped,
+        estimate,
         grad_lift,
         grad_kernel,
         grad_head.T,

time: 53.6 us -> 53.4 us (level)
  transfers between devices with their start and end apart: 13 -> 13, of which waited for: 7 -> 8; matrix products, arithmetic and copies ran while one was open for 4% -> 4% of each run, Pallas kernels for 10% -> 10%
where the time goes in v5:
time: 53.4 us; the launch traced here: 53.2 us
  starting transfers between devices  22.8 us (43%)
  waiting for transfers between devices  14.5 us (27%)
  Pallas kernels  13 us (24%)
  other arithmetic  1.51 us (3%)
  between operations  0.83 us (2%)
  local copies, waits for them, and re-layouts  0.6 us (1%)
    ppermute x8, waiting for transfers between devices, swap(): lax.ppermute(x, axis, [(i, i ^ bit) for i in range(lax.axis_size(axis))])  8.69 us
    ppermute x8, starting transfers between devices, swap(): lax.ppermute(x, axis, [(i, i ^ bit) for i in range(lax.axis_size(axis))])  8.15 us
    all_to_all x1, starting transfers between devices, per_device(): lax.all_to_all(outgoing, ('face', 'lon'), split_axis=0, concat_axis=0, ti...  7.3 us
    ppermute x2, starting transfers between devices, pair_swap(): lax.ppermute(jnp.where(even, odd_sends, even_sends), axis, inner)  4.55 us
    pallas_call x1, Pallas kernels, regrid(): pl.pallas_call(functools.partial(regrid_kernel, capacity), out_shape=jax....  3.42 us
    pallas_call x1, Pallas kernels, backward(): pl.pallas_call(functools.partial(backward_kernel, capacity, channels, nor...  3.28 us
    ppermute x2, starting transfers between devices, pair_swap(): lax.ppermute(jnp.where(even, even_sends, odd_sends), axis, outer)  2.85 us
    ppermute x2, waiting for transfers between devices, pair_swap(): lax.ppermute(jnp.where(even, even_sends, odd_sends), axis, outer)  2.43 us
  transfers between devices with their start and end apart: 13, of which 8 were waited for; matrix products, arithmetic and copies ran while one was open for 4% of the time, Pallas kernels for 10%

profile of v5, /device:TPU:0, one launch (start us, length us, event | category | flops | bytes accessed | tf_op | source)
XLA Modules:
  0.0 53.2 jit_solution(881036387290071803)
XLA Ops:
  0.6 3.4 %regrid.1 = bf16[32,9,8,128]{3,2,1,0:T(8,128)(2,1)} custom-call(s32[4,32]{1,0:T(4,128)} %bitcast.31, s32[4,32]{1,0:T(4,128)} %bitcast.32, bf16[32,8,128]{2,1,0:T(8,128)(2,1)} %src_hbm.1, bf16[32,4,128,128]{3,2,1,0:T(8,128)(2,1)} %wts_hbm.1), custom_call_target="tpu_custom_call" | custom-call | flops 33554432 | bytes 4194304 | tf_op jit(solution)/shard_map/regrid/pallas_call | solution.py:92
  4.1 7.3 %all-to-all-start = ((bf16[32,9,8,128]{3,2,1,0:T(8,128)(2,1)}), bf16[32,9,8,128]{3,2,1,0:T(8,128)(2,1)S(1)}, u32[]{:S(2)}, u32[]{:S(2)}) async-start(bf16[32,9,8,128]{3,2,1,0:T(8,128)(2,1)} %regrid.1), calls=%async_computation | async-start | bytes 1179648 | tf_op jit(solution)/shard_map/all_to_all | solution.py:561
  11.4 0.1 copy.20
  11.5 0.7 %collective-permute-start = (bf16[8,256]{1,0:T(8,128)(2,1)S(1)}, bf16[8,256]{1,0:T(8,128)(2,1)S(1)}, u32[]{:S(2)}, u32[]{:S(2)}) collective-permute-start(bf16[8,256]{1,0:T(8,128)(2,1)S(1)} %get-tuple-element.53), channel_id=1, source_target_pairs={{8,16},{16,8},{9,17},{17,9},{10,18},{18,10},{11,19},{19,11},{12,20... | collective-permute-start | bytes 12296 | tf_op jit(solution)/shard_map/ppermute | solution.py:534
  12.2 4.5 %collective-permute-start.1 = (bf16[8,256]{1,0:T(8,128)(2,1)S(1)}, bf16[8,256]{1,0:T(8,128)(2,1)S(1)}, u32[]{:S(2)}, u32[]{:S(2)}) collective-permute-start(bf16[8,256]{1,0:T(8,128)(2,1)S(1)} %get-tuple-element.54), channel_id=1, source_target_pairs={{0,8},{8,0},{16,24},{24,16},{1,9},{9,1},{17,25},{25,17},{2,10},{10... | collective-permute-start | bytes 12296 | tf_op jit(solution)/shard_map/ppermute | solution.py:533
  16.8 0.3 copy.15
  17.1 0.1 copy.17.readout_ref
  17.2 1.3 %collective-permute-done.1 = bf16[8,256]{1,0:T(8,128)(2,1)S(1)} collective-permute-done((bf16[8,256]{1,0:T(8,128)(2,1)S(1)}, bf16[8,256]{1,0:T(8,128)(2,1)S(1)}, u32[]{:S(2)}, u32[]{:S(2)}) %collective-permute-start.1) | collective-permute-done | bytes 4128 | tf_op jit(solution)/shard_map/ppermute | solution.py:533
  18.5 0.1 fusion.11
  18.6 0.1 broadcast_select_fusion.5
  18.7 2.2 %collective-permute-start.2 = (bf16[8,128]{1,0:T(8,128)(2,1)S(1)}, bf16[8,128]{1,0:T(8,128)(2,1)S(1)}, u32[]{:S(2)}, u32[]{:S(2)}) collective-permute-start(bf16[8,128]{1,0:T(8,128)(2,1)S(1)} %get-tuple-element.55), channel_id=1, source_target_pairs={{1,2},{2,1},{3,4},{4,3},{5,6},{6,5},{7,0},{0,7},{9,10},{10,9},{11,... | collective-permute-start | bytes 6152 | tf_op jit(solution)/shard_map/ppermute | solution.py:534
  20.9 1.8 %convolve.1 = (f32[2048,256]{1,0:T(8,128)S(1)}, bf16[80,8]{1,0:T(8,128)(2,1)S(1)}, bf16[192,240]{1,0:T(8,128)(2,1)S(1)}, bf16[192,192]{1,0:T(8,128)(2,1)S(1)}, bf16[3,64,192]{2,1,0:T(8,128)(2,1)S(1)}) custom-call(bf16[32,8,256]{2,1,0:T(8,128)(2,1)S(1)} %bitcast.25, bf16[2,8,256]{2,1,0:T(8,128)(2,1)S(1)} %pad_maximum_fusion.edge_ref, ...), custom_call_target="tpu_custom_call" | custom-call | flops 754974720 | bytes 4194304 | tf_op jit(solution)/shard_map/convolve/pallas_call | solution.py:168
  22.8 2.4 %collective-permute-done.2 = bf16[8,128]{1,0:T(8,128)(2,1)S(1)} collective-permute-done((bf16[8,128]{1,0:T(8,128)(2,1)S(1)}, bf16[8,128]{1,0:T(8,128)(2,1)S(1)}, u32[]{:S(2)}, u32[]{:S(2)}) %collective-permute-start.2) | collective-permute-done | bytes 2080 | tf_op jit(solution)/shard_map/ppermute | solution.py:534
  25.2 2.0 %finish.1 = (f32[2048,256]{1,0:T(8,128)S(1)}, bf16[240,256]{1,0:T(8,128)(2,1)S(1)}, f32[8,32,256]{2,1,0:T(8,128)S(1)}) custom-call(f32[2048,256]{1,0:T(8,128)S(1)} %get-tuple-element.32.part_ref, bf16[32,8,256]{2,1,0:T(8,128)(2,1)S(1)} %bitcast.26, bf16[8,256]{1,0:T(8,128)(2,1)S(1)} %pad_maximum_fusion.1.side_ref, ...), custom_call_target="tpu_custom_call", output_to_operand_aliasing={{0}: (0, {})} | custom-call | flops 8388608 | bytes 4194304 | tf_op jit(solution)/shard_map/finish/pallas_call | solution.py:236
  27.2 2.0 %all-to-all-done = bf16[32,9,8,128]{3,2,1,0:T(8,128)(2,1)S(1)} async-done(((bf16[32,9,8,128]{3,2,1,0:T(8,128)(2,1)}), bf16[32,9,8,128]{3,2,1,0:T(8,128)(2,1)S(1)}, u32[]{:S(2)}, u32[]{:S(2)}) %all-to-all-start) | async-done | bytes 589856 | tf_op jit(solution)/shard_map/all_to_all | solution.py:561
  29.2 3.3 %backward.1 = (f32[8,32,256]{2,1,0:T(8,128)S(1)}, f32[2,152,128]{2,1,0:T(8,128)S(1)}, bf16[2176,256]{1,0:T(8,128)(2,1)S(1)}, f32[3,8,192]{2,1,0:T(8,128)S(1)}) custom-call(bf16[32,72,128]{2,1,0:T(8,128)(2,1)S(1)} %bitcast.23, bf16[32,8,256]{2,1,0:T(8,128)(2,1)S(1)} %bitcast.27, bf16[2,8,256]{2,1,0:T(8,128)(2,1)S(1)} %pad_maximum_fusion.edge_ref, ...), custom_call_target="tpu_custom_call" | custom-call | flops 754974720 | bytes 4194304 | tf_op jit(solution)/shard_map/backward/pallas_call | solution.py:393
  32.5 0.1 collective-permute-start.4
  32.6 1.6 %lift_gradient.1 = f32[152,128]{1,0:T(8,128)S(1)} custom-call(bf16[2176,256]{1,0:T(8,128)(2,1)S(1)} %get-tuple-element.40.slope_ref, bf16[32,8,256]{2,1,0:T(8,128)(2,1)S(1)} %bitcast.28, bf16[192,192]{1,0:T(8,128)(2,1)S(1)} %get-tuple-element.41.back_ref, bf16[3,64,192]{2,1,0:T(8,128)(2,1)S(1)} %get-tuple-element.42.contract_ref, ...), custom_call_target="tpu_custom_call" | custom-call | flops 603979776 | bytes 1114112 | tf_op jit(solution)/shard_map/lift_gradient/pallas_call | solution.py:462
  34.2 0.9 %collective-permute-start.7 = (f32[152,128]{1,0:T(8,128)S(1)}, f32[152,128]{1,0:T(8,128)S(1)}, u32[]{:S(2)}, u32[]{:S(2)}) collective-permute-start(f32[152,128]{1,0:T(8,128)S(1)} %fusion), channel_id=1, source_target_pairs={{0,24},{8,16},{16,8},{24,0},{1,25},{9,17},{17,9},{25,1},{2,26},{10... | collective-permute-start | bytes 233480 | tf_op jit(solution)/shard_map/ppermute | solution.py:511
  35.1 1.5 %collective-permute-start.6 = (f32[152,128]{1,0:T(8,128)S(1)}, f32[152,128]{1,0:T(8,128)S(1)}, u32[]{:S(2)}, u32[]{:S(2)}) collective-permute-start(f32[152,128]{1,0:T(8,128)S(1)} %fusion), channel_id=1, source_target_pairs={{0,16},{8,24},{16,0},{24,8},{1,17},{9,25},{17,1},{25,9},{2,18},{10... | collective-permute-start | bytes 233480 | tf_op jit(solution)/shard_map/ppermute | solution.py:511
  36.6 1.2 %collective-permute-start.5 = (f32[152,128]{1,0:T(8,128)S(1)}, f32[152,128]{1,0:T(8,128)S(1)}, u32[]{:S(2)}, u32[]{:S(2)}) collective-permute-start(f32[152,128]{1,0:T(8,128)S(1)} %fusion), channel_id=1, source_target_pairs={{0,8},{8,0},{16,24},{24,16},{1,9},{9,1},{17,25},{25,17},{2,10},{10... | collective-permute-start | bytes 233480 | tf_op jit(solution)/shard_map/ppermute | solution.py:511
  37.8 0.7 %convert_element_type.10 = bf16[8,32,256]{2,1,0:T(8,128)(2,1)} convert(f32[8,32,256]{2,1,0:T(8,128)S(1)} %get-tuple-element.38.forecast_ref) | non-fusion elementwise | flops 65536 | bytes 393216 | tf_op jit(solution)/shard_map/convert_element_type | solution.py:586
  38.5 0.7 %convert_element_type.9 = bf16[8,32,256]{2,1,0:T(8,128)(2,1)} convert(f32[8,32,256]{2,1,0:T(8,128)S(1)} %get-tuple-element.44) | non-fusion elementwise | flops 65536 | bytes 393216 | tf_op jit(solution)/shard_map/convert_element_type | solution.py:586
  39.1 1.3 %collective-permute-done.7 = f32[152,128]{1,0:T(8,128)S(1)} collective-permute-done((f32[152,128]{1,0:T(8,128)S(1)}, f32[152,128]{1,0:T(8,128)S(1)}, u32[]{:S(2)}, u32[]{:S(2)}) %collective-permute-start.7) | collective-permute-done | bytes 77856 | tf_op jit(solution)/shard_map/ppermute | solution.py:511
  40.4 0.6 %collective-permute-done.6 = f32[152,128]{1,0:T(8,128)S(1)} collective-permute-done((f32[152,128]{1,0:T(8,128)S(1)}, f32[152,128]{1,0:T(8,128)S(1)}, u32[]{:S(2)}, u32[]{:S(2)}) %collective-permute-start.6) | collective-permute-done | bytes 77856 | tf_op jit(solution)/shard_map/ppermute | solution.py:511
  41.0 1.1 %collective-permute-start.10 = (f32[152,128]{1,0:T(8,128)S(1)}, f32[152,128]{1,0:T(8,128)S(1)}, u32[]{:S(2)}, u32[]{:S(2)}) collective-permute-start(f32[152,128]{1,0:T(8,128)S(1)} %add_add_fusion.1), channel_id=1, source_target_pairs={{0,6},{1,7},{2,4},{3,5},{4,2},{5,3},{6,0},{7,1},{8,14},{9,15},{10,... | collective-permute-start | bytes 233480 | tf_op jit(solution)/shard_map/ppermute | solution.py:511
  42.2 2.3 %collective-permute-start.9 = (f32[152,128]{1,0:T(8,128)S(1)}, f32[152,128]{1,0:T(8,128)S(1)}, u32[]{:S(2)}, u32[]{:S(2)}) collective-permute-start(f32[152,128]{1,0:T(8,128)S(1)} %add_add_fusion.1), channel_id=1, source_target_pairs={{0,4},{1,5},{2,6},{3,7},{4,0},{5,1},{6,2},{7,3},{8,12},{9,13},{10,... | collective-permute-start | bytes 233480 | tf_op jit(solution)/shard_map/ppermute | solution.py:511
  44.5 1.0 %collective-permute-start.8 = (f32[152,128]{1,0:T(8,128)S(1)}, f32[152,128]{1,0:T(8,128)S(1)}, u32[]{:S(2)}, u32[]{:S(2)}) collective-permute-start(f32[152,128]{1,0:T(8,128)S(1)} %add_add_fusion.1), channel_id=1, source_target_pairs={{0,2},{1,3},{2,0},{3,1},{4,6},{5,7},{6,4},{7,5},{8,10},{9,11},{10,... | collective-permute-start | bytes 233480 | tf_op jit(solution)/shard_map/ppermute | solution.py:511
  45.5 2.6 %collective-permute-done.10 = f32[152,128]{1,0:T(8,128)S(1)} collective-permute-done((f32[152,128]{1,0:T(8,128)S(1)}, f32[152,128]{1,0:T(8,128)S(1)}, u32[]{:S(2)}, u32[]{:S(2)}) %collective-permute-start.10) | collective-permute-done | bytes 77856 | tf_op jit(solution)/shard_map/ppermute | solution.py:511
  48.1 2.9 %collective-permute-done.9 = f32[152,128]{1,0:T(8,128)S(1)} collective-permute-done((f32[152,128]{1,0:T(8,128)S(1)}, f32[152,128]{1,0:T(8,128)S(1)}, u32[]{:S(2)}, u32[]{:S(2)}) %collective-permute-start.9) | collective-permute-done | bytes 77856 | tf_op jit(solution)/shard_map/ppermute | solution.py:511
  51.2 1.3 %collective-permute-done.11.other_ref = f32[152,128]{1,0:T(8,128)S(1)} collective-permute-done((f32[152,128]{1,0:T(8,128)S(1)}, f32[152,128]{1,0:T(8,128)S(1)}, u32[]{:S(2)}, u32[]{:S(2)}) %collective-permute-start.11) | collective-permute-done | bytes 77856 | tf_op jit(solution)/shard_map/ppermute | solution.py:511
  52.4 0.8 %unpack.1 = (f32[9,64,64]{2,1,0:T(8,128)}, f32[8,64]{1,0:T(8,128)}, f32[8,64]{1,0:T(8,128)}) custom-call(f32[152,128]{1,0:T(8,128)S(1)} %add_add_fusion.mine_ref, f32[152,128]{1,0:T(8,128)S(1)} %collective-permute-done.11.other_ref), custom_call_target="tpu_custom_call" | custom-call | tf_op jit(solution)/shard_map/unpack/pallas_call | solution.py:498
  (25 shorter events, 0.2 us)
Async XLA Ops:
  0.6 10.8 %copy-start.2 = (bf16[8,32,256]{2,1,0:T(8,128)(2,1)S(1)}, bf16[8,32,256]{2,1,0:T(8,128)(2,1)}, u32[]{:S(2)}) copy-start(bf16[8,32,256]{2,1,0:T(8,128)(2,1)} %param.12) | copy-start | bytes 393220
  4.1 13.0 %copy-start.3 = (bf16[64,8]{0,1:T(8,128)(2,1)S(1)}, bf16[64,8]{0,1:T(8,128)(2,1)}, u32[]{:S(2)}) copy-start(bf16[64,8]{0,1:T(8,128)(2,1)} %param.15) | copy-start | bytes 3076
  4.1 16.8 %copy-start = (bf16[9,64,64]{2,1,0:T(8,128)(2,1)S(1)}, bf16[9,64,64]{2,1,0:T(8,128)(2,1)}, u32[]{:S(2)}) copy-start(bf16[9,64,64]{2,1,0:T(8,128)(2,1)} %kernel_ref) | copy-start | bytes 221188
  4.1 16.8 %copy-start.1 = (bf16[8,64]{1,0:T(8,128)(2,1)S(1)}, bf16[8,64]{1,0:T(8,128)(2,1)}, u32[]{:S(2)}) copy-start(bf16[8,64]{1,0:T(8,128)(2,1)} %lift_weight_ref) | copy-start | bytes 3076
  4.1 25.1 %all-to-all-start = ((bf16[32,9,8,128]{3,2,1,0:T(8,128)(2,1)}), bf16[32,9,8,128]{3,2,1,0:T(8,128)(2,1)S(1)}, u32[]{:S(2)}, u32[]{:S(2)}) async-start(bf16[32,9,8,128]{3,2,1,0:T(8,128)(2,1)} %regrid.1), calls=%async_computation | async-start | bytes 1179648 | tf_op jit(solution)/shard_map/all_to_all | solution.py:561
  11.5 5.7 %collective-permute-start = (bf16[8,256]{1,0:T(8,128)(2,1)S(1)}, bf16[8,256]{1,0:T(8,128)(2,1)S(1)}, u32[]{:S(2)}, u32[]{:S(2)}) collective-permute-start(bf16[8,256]{1,0:T(8,128)(2,1)S(1)} %get-tuple-element.53), channel_id=1, source_target_pairs={{8,16},{16,8},{9,17},{17,9},{10,18},{18,10},{11,19},{19,11},{12,20... | collective-permute-start | bytes 12296 | tf_op jit(solution)/shard_map/ppermute | solution.py:534
  12.2 6.3 %collective-permute-start.1 = (bf16[8,256]{1,0:T(8,128)(2,1)S(1)}, bf16[8,256]{1,0:T(8,128)(2,1)S(1)}, u32[]{:S(2)}, u32[]{:S(2)}) collective-permute-start(bf16[8,256]{1,0:T(8,128)(2,1)S(1)} %get-tuple-element.54), channel_id=1, source_target_pairs={{0,8},{8,0},{16,24},{24,16},{1,9},{9,1},{17,25},{25,17},{2,10},{10... | collective-permute-start | bytes 12296 | tf_op jit(solution)/shard_map/ppermute | solution.py:533
  18.7 6.5 %collective-permute-start.2 = (bf16[8,128]{1,0:T(8,128)(2,1)S(1)}, bf16[8,128]{1,0:T(8,128)(2,1)S(1)}, u32[]{:S(2)}, u32[]{:S(2)}) collective-permute-start(bf16[8,128]{1,0:T(8,128)(2,1)S(1)} %get-tuple-element.55), channel_id=1, source_target_pairs={{1,2},{2,1},{3,4},{4,3},{5,6},{6,5},{7,0},{0,7},{9,10},{10,9},{11,... | collective-permute-start | bytes 6152 | tf_op jit(solution)/shard_map/ppermute | solution.py:534
  20.9 4.3 %collective-permute-start.3 = (bf16[8,128]{1,0:T(8,128)(2,1)S(1)}, bf16[8,128]{1,0:T(8,128)(2,1)S(1)}, u32[]{:S(2)}, u32[]{:S(2)}) collective-permute-start(bf16[8,128]{1,0:T(8,128)(2,1)S(1)} %get-tuple-element.56), channel_id=1, source_target_pairs={{0,1},{1,0},{2,3},{3,2},{4,5},{5,4},{6,7},{7,6},{8,9},{9,8},{10,11... | collective-permute-start | bytes 6152 | tf_op jit(solution)/shard_map/ppermute | solution.py:533
  32.5 1.7 %collective-permute-start.4 = (f32[152,128]{1,0:T(8,128)S(1)}, f32[152,128]{1,0:T(8,128)S(1)}, u32[]{:S(2)}, u32[]{:S(2)}) collective-permute-start(f32[152,128]{1,0:T(8,128)S(1)} %slice_bitcast_fusion), channel_id=1, source_target_pairs={{0,1},{1,0},{2,3},{3,2},{4,5},{5,4},{6,7},{7,6},{8,9},{9,8},{10,11... | collective-permute-start | bytes 233480 | tf_op jit(solution)/shard_map/ppermute | solution.py:511
  34.2 6.2 %collective-permute-start.7 = (f32[152,128]{1,0:T(8,128)S(1)}, f32[152,128]{1,0:T(8,128)S(1)}, u32[]{:S(2)}, u32[]{:S(2)}) collective-permute-start(f32[152,128]{1,0:T(8,128)S(1)} %fusion), channel_id=1, source_target_pairs={{0,24},{8,16},{16,8},{24,0},{1,25},{9,17},{17,9},{25,1},{2,26},{10... | collective-permute-start | bytes 233480 | tf_op jit(solution)/shard_map/ppermute | solution.py:511
  35.1 5.9 %collective-permute-start.6 = (f32[152,128]{1,0:T(8,128)S(1)}, f32[152,128]{1,0:T(8,128)S(1)}, u32[]{:S(2)}, u32[]{:S(2)}) collective-permute-start(f32[152,128]{1,0:T(8,128)S(1)} %fusion), channel_id=1, source_target_pairs={{0,16},{8,24},{16,0},{24,8},{1,17},{9,25},{17,1},{25,9},{2,18},{10... | collective-permute-start | bytes 233480 | tf_op jit(solution)/shard_map/ppermute | solution.py:511
  36.6 4.4 %collective-permute-start.5 = (f32[152,128]{1,0:T(8,128)S(1)}, f32[152,128]{1,0:T(8,128)S(1)}, u32[]{:S(2)}, u32[]{:S(2)}) collective-permute-start(f32[152,128]{1,0:T(8,128)S(1)} %fusion), channel_id=1, source_target_pairs={{0,8},{8,0},{16,24},{24,16},{1,9},{9,1},{17,25},{25,17},{2,10},{10... | collective-permute-start | bytes 233480 | tf_op jit(solution)/shard_map/ppermute | solution.py:511
  41.0 7.1 %collective-permute-start.10 = (f32[152,128]{1,0:T(8,128)S(1)}, f32[152,128]{1,0:T(8,128)S(1)}, u32[]{:S(2)}, u32[]{:S(2)}) collective-permute-start(f32[152,128]{1,0:T(8,128)S(1)} %add_add_fusion.1), channel_id=1, source_target_pairs={{0,6},{1,7},{2,4},{3,5},{4,2},{5,3},{6,0},{7,1},{8,14},{9,15},{10,... | collective-permute-start | bytes 233480 | tf_op jit(solution)/shard_map/ppermute | solution.py:511
  42.2 8.9 %collective-permute-start.9 = (f32[152,128]{1,0:T(8,128)S(1)}, f32[152,128]{1,0:T(8,128)S(1)}, u32[]{:S(2)}, u32[]{:S(2)}) collective-permute-start(f32[152,128]{1,0:T(8,128)S(1)} %add_add_fusion.1), channel_id=1, source_target_pairs={{0,4},{1,5},{2,6},{3,7},{4,0},{5,1},{6,2},{7,3},{8,12},{9,13},{10,... | collective-permute-start | bytes 233480 | tf_op jit(solution)/shard_map/ppermute | solution.py:511
  44.5 6.5 %collective-permute-start.8 = (f32[152,128]{1,0:T(8,128)S(1)}, f32[152,128]{1,0:T(8,128)S(1)}, u32[]{:S(2)}, u32[]{:S(2)}) collective-permute-start(f32[152,128]{1,0:T(8,128)S(1)} %add_add_fusion.1), channel_id=1, source_target_pairs={{0,2},{1,3},{2,0},{3,1},{4,6},{5,7},{6,4},{7,5},{8,10},{9,11},{10,... | collective-permute-start | bytes 233480 | tf_op jit(solution)/shard_map/ppermute | solution.py:511
  51.1 1.3 %collective-permute-start.11 = (f32[152,128]{1,0:T(8,128)S(1)}, f32[152,128]{1,0:T(8,128)S(1)}, u32[]{:S(2)}, u32[]{:S(2)}) collective-permute-start(f32[152,128]{1,0:T(8,128)S(1)} %add_add_fusion.mine_ref), channel_id=1, source_target_pairs={{0,1},{1,0},{2,3},{3,2},{4,5},{5,4},{6,7},{7,6},{8,9},{9,8},{10,11... | collective-permute-start | bytes 233480 | tf_op jit(solution)/shard_map/ppermute | solution.py:511

commit v6 on v5

--- a/solution.py
+++ b/solution.py
@@ -125,12 +125,18 @@
     edge_ref,
     lift_weight_ref,
     kernel_ref,
+    readout_ref,
     act_ref,
+    forecast_ref,
+    ends_ref,
     lift_ref,
     conv_ref,
     back_ref,
     contract_ref,
+    turned_ref,
     feat_ref,
+    hidden_ref,
+    by_row_ref,
 ):
     rows, fields, width = prior_ref.shape
     channels = kernel_ref.shape[1]
@@ -150,17 +156,30 @@
     )
     lift = jnp.concatenate([lift_weight_ref[...].astype(jnp.float32), jnp.where(same, 1.0, 0.0)], axis=1)
     lift_ref[...] = lift.T.astype(jnp.bfloat16)
+    turned_ref[...] = readout_ref[...].astype(jnp.float32).T.astype(jnp.bfloat16)
 
     lift_rows(prior_ref, edge_ref, lift_ref[...], feat_ref)
-    lane = lax.broadcasted_iota(jnp.int32, (channels, width), 1)
+    col = lax.broadcasted_iota(jnp.int32, (channels, width), 1)
+    lane = lax.broadcasted_iota(jnp.int32, (channels, 128), 1)
+    ends_left = ends_right = jnp.zeros((channels, 128), jnp.float32)
     for y in range(rows):
         parts = dot(conv_ref[...], feat_ref[y * pitch : (y + 3) * pitch, :])
-        left = jnp.where(lane == 0, 0.0, pltpu.roll(parts[:channels], 1, 1))
-        right = jnp.where(lane == width - 1, 0.0, pltpu.roll(parts[2 * channels :], width - 1, 1))
-        act_ref[y * channels : (y + 1) * channels, :] = parts[channels : 2 * channels] + left + right
-
-
-def convolve(prior, edges, lift_weight, kernel):
+        left = jnp.where(col == 0, 0.0, pltpu.roll(parts[:channels], 1, 1))
+        right = jnp.where(col == width - 1, 0.0, pltpu.roll(parts[2 * channels :], width - 1, 1))
+        act = parts[channels : 2 * channels] + left + right
+        act_ref[y * channels : (y + 1) * channels, :] = act
+        hidden_ref[y * channels : (y + 1) * channels, :] = (act * sigmoid(act)).astype(jnp.bfloat16)
+        ends_left += pltpu.roll(jnp.where(lane == 0, act[:, :128], 0.0), y, 1)
+        ends_right += pltpu.roll(jnp.where(lane == 127, act[:, -128:], 0.0), y + 1, 1)
+    ends_ref[:, :128] = ends_left
+    ends_ref[:, 128:] = ends_right
+    for y in range(rows):
+        increment = dot(turned_ref[...], hidden_ref[y * channels : (y + 1) * channels, :])
+        by_row_ref[y] = prior_ref[y].astype(jnp.float32) + increment
+    forecast_ref[...] = jnp.transpose(by_row_ref[...], (1, 0, 2))
+
+
+def convolve(prior, edges, lift_weight, kernel, readout):
     rows, fields, width = prior.shape
     channels = kernel.shape[1]
     pitch = channels + 16
@@ -169,93 +188,94 @@
         convolve_kernel,
         out_shape=(
             jax.ShapeDtypeStruct((rows * channels, width), jnp.float32),
+            jax.ShapeDtypeStruct((fields, rows, width), jnp.float32),
+            jax.ShapeDtypeStruct((channels, 256), jnp.float32),
             jax.ShapeDtypeStruct((pitch, fields), jnp.bfloat16),
             jax.ShapeDtypeStruct((3 * channels, 3 * pitch), jnp.bfloat16),
             jax.ShapeDtypeStruct((3 * channels, 3 * channels), jnp.bfloat16),
             jax.ShapeDtypeStruct((3, channels, 3 * channels), jnp.bfloat16),
-        ),
-        in_specs=[vmem] * 4,
-        out_specs=[vmem] * 5,
-        scratch_shapes=[pltpu.VMEM(((rows + 2) * pitch, width), jnp.bfloat16)],
+            jax.ShapeDtypeStruct((fields, channels), jnp.bfloat16),
+        ),
+        in_specs=[vmem] * 5,
+        out_specs=[vmem] * 8,
+        scratch_shapes=[
+            pltpu.VMEM(((rows + 2) * pitch, width), jnp.bfloat16),
+            pltpu.VMEM((rows * channels, width), jnp.bfloat16),
+            pltpu.VMEM((rows, fields, width), jnp.float32),
+        ],
         compiler_params=pltpu.CompilerParams(vmem_limit_bytes=VMEM_LIMIT),
         cost_estimate=pl.CostEstimate(
             flops=2 * rows * width * 3 * channels * 3 * pitch,
             bytes_accessed=rows * width * channels * 8,
-            transcendentals=0,
+            transcendentals=rows * width * channels * 2,
         ),
         name="convolve",
-    )(prior, edges, lift_weight, kernel)
+    )(prior, edges, lift_weight, kernel, readout)
 
 
 def finish_kernel(
-    part_ref,
-    prior_ref,
+    old_act_ref,
+    old_forecast_ref,
+    ends_ref,
+    own_ref,
     side_ref,
     lift_ref,
     conv_ref,
-    readout_ref,
+    turned_ref,
     act_ref,
+    forecast_ref,
     stack_ref,
-    forecast_ref,
-    halo_ref,
-    hidden_ref,
-    by_row_ref,
 ):
-    rows, fields, width = prior_ref.shape
-    channels = readout_ref.shape[0]
+    fields, rows, width = forecast_ref.shape
+    channels = ends_ref.shape[0]
     side = dot(lift_ref[...], side_ref[...])
     shifted = [side] + [pltpu.roll(side, 256 - i, 1) for i in (1, 2)]
     stack = jnp.concatenate(shifted, axis=0).astype(jnp.bfloat16)
     stack_ref[...] = stack
-    halo_ref[:, :128] = dot(conv_ref[:channels, :], stack[:, :128])
-    halo_ref[:, 128:] = dot(conv_ref[2 * channels :, :], stack[:, 128:])
-    readout = readout_ref[...].astype(jnp.float32).T.astype(jnp.bfloat16)
+    left = ends_ref[:, :128] + dot(conv_ref[:channels, :], stack[:, :128])
+    right = ends_ref[:, 128:] + dot(conv_ref[2 * channels :, :], stack[:, 128:])
+    hidden = jnp.concatenate([(act * sigmoid(act)).astype(jnp.bfloat16) for act in (left, right)], axis=1)
+    forecast = pltpu.roll(own_ref[...].astype(jnp.float32), 255, 1) + dot(turned_ref[...], hidden)
+
     lane = lax.broadcasted_iota(jnp.int32, (channels, 128), 1)
-    spread = [jnp.zeros((channels, 128), jnp.float32)] * (width // 128 - 1)
     for y in range(rows):
         here = slice(y * channels, (y + 1) * channels)
-        from_left = jnp.where(lane == 0, pltpu.roll(halo_ref[:, :128], (128 - y) % 128, 1), 0.0)
-        from_right = jnp.where(lane == 127, pltpu.roll(halo_ref[:, 128:], 127 - y, 1), 0.0)
-        act = (
-            part_ref[here, :]
-            + jnp.concatenate([from_left] + spread, axis=1)
-            + jnp.concatenate(spread + [from_right], axis=1)
+        from_left = pltpu.roll(left, (128 - y) % 128, 1)
+        from_right = pltpu.roll(right, 127 - y, 1)
+        if width == 128:
+            act = jnp.where(lane == 0, from_left, jnp.where(lane == 127, from_right, old_act_ref[here, :]))
+            act_ref[here, :] = act
+        else:
+            act_ref[here, :128] = jnp.where(lane == 0, from_left, old_act_ref[here, :128])
+            act_ref[here, -128:] = jnp.where(lane == 127, from_right, old_act_ref[here, -128:])
+            if width > 256:
+                act_ref[here, 128:-128] = old_act_ref[here, 128:-128]
+    col = lax.broadcasted_iota(jnp.int32, (rows, width), 1)
+    by_row = forecast.T
+    for f in range(fields):
+        from_left = jnp.broadcast_to(by_row[:rows, f : f + 1], (rows, width))
+        from_right = jnp.broadcast_to(by_row[128 : 128 + rows, f : f + 1], (rows, width))
+        forecast_ref[f] = jnp.where(
+            col == 0, from_left, jnp.where(col == width - 1, from_right, old_forecast_ref[f])
         )
-        act_ref[here, :] = act
-        hidden_ref[here, :] = (act * sigmoid(act)).astype(jnp.bfloat16)
-    for y in range(rows):
-        increment = dot(readout, hidden_ref[y * channels : (y + 1) * channels, :])
-        by_row_ref[y] = prior_ref[y].astype(jnp.float32) + increment
-    forecast_ref[...] = jnp.transpose(by_row_ref[...], (1, 0, 2))
-
-
-def finish(part, prior, sides, lift, conv, readout):
-    rows, fields, width = prior.shape
-    channels = readout.shape[0]
+
+
+def finish(act, forecast, ends, own, sides, lift, conv, turned):
     vmem = pl.BlockSpec(memory_space=pltpu.VMEM)
     return pl.pallas_call(
         finish_kernel,
         out_shape=(
-            jax.ShapeDtypeStruct(part.shape, jnp.float32),
+            jax.ShapeDtypeStruct(act.shape, jnp.float32),
+            jax.ShapeDtypeStruct(forecast.shape, jnp.float32),
             jax.ShapeDtypeStruct((conv.shape[1], 256), jnp.bfloat16),
-            jax.ShapeDtypeStruct((fields, rows, width), jnp.float32),
-        ),
-        in_specs=[vmem] * 6,
+        ),
+        in_specs=[vmem] * 8,
         out_specs=[vmem] * 3,
-        scratch_shapes=[
-            pltpu.VMEM((channels, 256), jnp.float32),
-            pltpu.VMEM((rows * channels, width), jnp.bfloat16),
-            pltpu.VMEM((rows, fields, width), jnp.float32),
-        ],
-        input_output_aliases={0: 0},
+        input_output_aliases={0: 0, 1: 1},
         compiler_params=pltpu.CompilerParams(vmem_limit_bytes=VMEM_LIMIT),
-        cost_estimate=pl.CostEstimate(
-            flops=2 * rows * width * channels * fields,
-            bytes_accessed=rows * width * channels * 8,
-            transcendentals=rows * width * channels * 2,
-        ),
+        cost_estimate=pl.CostEstimate(flops=2 * act.size, bytes_accessed=8 * act.size, transcendentals=0),
         name="finish",
-    )(part, prior, sides, lift, conv, readout)
+    )(act, forecast, ends, own, sides, lift, conv, turned)
 
 
 def backward_kernel(
@@ -574,8 +594,11 @@
 
     edges = jnp.stack([top, bottom])
     sides = jnp.concatenate([left, right], axis=1)
-    part, lift, conv, back, contract = convolve(prior, edges, lift_weight, kernel)
-    act, stack, forecast = finish(part, prior, sides, lift, conv, readout_weights)
+    act, forecast, ends, lift, conv, back, contract, turned = convolve(
+        prior, edges, lift_weight, kernel, readout_weights
+    )
+    own = jnp.concatenate(columns, axis=1)
+    act, forecast, stack = finish(act, forecast, ends, own, sides, lift, conv, turned)
     remapped, packed, slope, moment = backward(
         arrived, prior, edges, stack, lift, act, forecast, readout_weights, capacity, norm
     )

time: 53.4 us -> 52.9 us (level)
  waiting for transfers between devices: 14.5 us -> 11 us
  starting transfers between devices: 22.8 us -> 24.4 us
  Pallas kernels: 13 us -> 13.7 us
  local copies, waits for them, and re-layouts: 0.6 us -> 1.24 us
    ppermute x2, waiting for transfers between devices: 2.43 us -> 0.01 us  [pair_swap(): lax.ppermute(jnp.where(even, even_sends, odd_sends), axis, outer)]
    ppermute x2, starting transfers between devices: 2.85 us -> 4.36 us  [pair_swap(): lax.ppermute(jnp.where(even, even_sends, odd_sends), axis, outer)]
    pallas_call x1, Pallas kernels: 1.85 us -> 3.28 us  [convolve(): pl.pallas_call(convolve_kernel, out_shape=(jax.ShapeDtypeStruct((rows * c...]
    pallas_call x1, Pallas kernels: 1.96 us -> 1.25 us  [finish(): pl.pallas_call(finish_kernel, out_shape=(jax.ShapeDtypeStruct(act.shape,...]
    unnamed x8 -> x12, local copies, waits for them, and re-layouts: 0.02 us -> 0.66 us
    all_to_all x1, waiting for transfers between devices: 2.02 us -> 1.48 us  [per_device(): lax.all_to_all(outgoing, ('face', 'lon'), split_axis=0, concat_axis=0, ti...]
  transfers between devices with their start and end apart: 13 -> 13, of which waited for: 8 -> 7; matrix products, arithmetic and copies ran while one was open for 4% -> 4% of each run, Pallas kernels for 10% -> 12%
where the time goes in v6:
time: 52.9 us; the launch traced here: 52.7 us
  starting transfers between devices  24.4 us (46%)
  Pallas kernels  13.7 us (26%)
  waiting for transfers between devices  11 us (21%)
  other arithmetic  1.53 us (3%)
  local copies, waits for them, and re-layouts  1.24 us (2%)
  between operations  0.87 us (2%)
    ppermute x8, waiting for transfers between devices, swap(): lax.ppermute(x, axis, [(i, i ^ bit) for i in range(lax.axis_size(axis))])  8.22 us
    ppermute x8, starting transfers between devices, swap(): lax.ppermute(x, axis, [(i, i ^ bit) for i in range(lax.axis_size(axis))])  8.15 us
    all_to_all x1, starting transfers between devices, per_device(): lax.all_to_all(outgoing, ('face', 'lon'), split_axis=0, concat_axis=0, ti...  7.3 us
    ppermute x2, starting transfers between devices, pair_swap(): lax.ppermute(jnp.where(even, odd_sends, even_sends), axis, inner)  4.61 us
    ppermute x2, starting transfers between devices, pair_swap(): lax.ppermute(jnp.where(even, even_sends, odd_sends), axis, outer)  4.36 us
    pallas_call x1, Pallas kernels, regrid(): pl.pallas_call(functools.partial(regrid_kernel, capacity), out_shape=jax....  3.4 us
    pallas_call x1, Pallas kernels, convolve(): pl.pallas_call(convolve_kernel, out_shape=(jax.ShapeDtypeStruct((rows * c...  3.28 us
    pallas_call x1, Pallas kernels, backward(): pl.pallas_call(functools.partial(backward_kernel, capacity, channels, nor...  3.28 us
  transfers between devices with their start and end apart: 13, of which 7 were waited for; matrix products, arithmetic and copies ran while one was open for 4% of the time, Pallas kernels for 12%

profile of v6, /device:TPU:0, one launch (start us, length us, event | category | flops | bytes accessed | tf_op | source)
XLA Modules:
  0.0 52.7 jit_solution(4361784034081013027)
XLA Ops:
  0.6 3.4 %regrid.1 = bf16[32,9,8,128]{3,2,1,0:T(8,128)(2,1)} custom-call(s32[4,32]{1,0:T(4,128)} %bitcast.30, s32[4,32]{1,0:T(4,128)} %bitcast.31, bf16[32,8,128]{2,1,0:T(8,128)(2,1)} %src_hbm.1, bf16[32,4,128,128]{3,2,1,0:T(8,128)(2,1)} %wts_hbm.1), custom_call_target="tpu_custom_call" | custom-call | flops 33554432 | bytes 4194304 | tf_op jit(solution)/shard_map/regrid/pallas_call | solution.py:92
  4.1 7.3 %all-to-all-start = ((bf16[32,9,8,128]{3,2,1,0:T(8,128)(2,1)}), bf16[32,9,8,128]{3,2,1,0:T(8,128)(2,1)S(1)}, u32[]{:S(2)}, u32[]{:S(2)}) async-start(bf16[32,9,8,128]{3,2,1,0:T(8,128)(2,1)} %regrid.1), calls=%async_computation | async-start | bytes 1179648 | tf_op jit(solution)/shard_map/all_to_all | solution.py:581
  11.4 0.1 copy.21
  11.5 0.7 %collective-permute-start = (bf16[8,256]{1,0:T(8,128)(2,1)S(1)}, bf16[8,256]{1,0:T(8,128)(2,1)S(1)}, u32[]{:S(2)}, u32[]{:S(2)}) collective-permute-start(bf16[8,256]{1,0:T(8,128)(2,1)S(1)} %get-tuple-element.62), channel_id=1, source_target_pairs={{8,16},{16,8},{9,17},{17,9},{10,18},{18,10},{11,19},{19,11},{12,20... | collective-permute-start | bytes 12296 | tf_op jit(solution)/shard_map/ppermute | solution.py:554
  12.2 4.5 %collective-permute-start.1 = (bf16[8,256]{1,0:T(8,128)(2,1)S(1)}, bf16[8,256]{1,0:T(8,128)(2,1)S(1)}, u32[]{:S(2)}, u32[]{:S(2)}) collective-permute-start(bf16[8,256]{1,0:T(8,128)(2,1)S(1)} %get-tuple-element.63), channel_id=1, source_target_pairs={{0,8},{8,0},{16,24},{24,16},{1,9},{9,1},{17,25},{25,17},{2,10},{10... | collective-permute-start | bytes 12296 | tf_op jit(solution)/shard_map/ppermute | solution.py:553
  16.7 0.3 copy.17
  17.1 0.1 copy.16.readout_ref
  17.2 1.3 %collective-permute-done.1 = bf16[8,256]{1,0:T(8,128)(2,1)S(1)} collective-permute-done((bf16[8,256]{1,0:T(8,128)(2,1)S(1)}, bf16[8,256]{1,0:T(8,128)(2,1)S(1)}, u32[]{:S(2)}, u32[]{:S(2)}) %collective-permute-start.1) | collective-permute-done | bytes 4128 | tf_op jit(solution)/shard_map/ppermute | solution.py:553
  18.5 0.1 fusion.13
  18.6 0.1 broadcast_select_fusion.5
  18.7 0.1 collective-permute-start.3
  18.8 3.7 %collective-permute-start.2 = (bf16[8,128]{1,0:T(8,128)(2,1)S(1)}, bf16[8,128]{1,0:T(8,128)(2,1)S(1)}, u32[]{:S(2)}, u32[]{:S(2)}) collective-permute-start(bf16[8,128]{1,0:T(8,128)(2,1)S(1)} %get-tuple-element.57), channel_id=1, source_target_pairs={{1,2},{2,1},{3,4},{4,3},{5,6},{6,5},{7,0},{0,7},{9,10},{10,9},{11,... | collective-permute-start | bytes 6152 | tf_op jit(solution)/shard_map/ppermute | solution.py:554
  22.5 3.3 %convolve.1 = (f32[2048,256]{1,0:T(8,128)S(1)}, f32[8,32,256]{2,1,0:T(8,128)S(1)}, f32[64,256]{1,0:T(8,128)S(1)}, bf16[80,8]{1,0:T(8,128)(2,1)S(1)}, bf16[192,24...) custom-call(bf16[32,8,256]{2,1,0:T(8,128)(2,1)S(1)} %bitcast.25, ...), custom_call_target="tpu_custom_call" | custom-call | flops 754974720 | bytes 4194304 | tf_op jit(solution)/shard_map/convolve/pallas_call | solution.py:187
  25.8 0.6 %copy-done.2 = bf16[3,64,192]{2,1,0:T(8,128)(2,1)} copy-done((bf16[3,64,192]{2,1,0:T(8,128)(2,1)}, bf16[3,64,192]{2,1,0:T(8,128)(2,1)S(1)}, u32[]{:S(2)}) %copy-start.2) | copy-done | bytes 73752
  26.4 1.2 %finish.1 = (f32[2048,256]{1,0:T(8,128)S(1)}, f32[8,32,256]{2,1,0:T(8,128)S(1)}, bf16[240,256]{1,0:T(8,128)(2,1)S(1)}) custom-call(f32[2048,256]{1,0:T(8,128)S(1)} %get-tuple-element.36.old_act_ref, f32[8,32,256]{2,1,0:T(8,128)S(1)} %get-tuple-element.37.old_forecast_ref, ...), custom_call_target="tpu_custom_call", output_to_operand_aliasing={{0}: (0, {}), {1}: (1, {})} | custom-call | flops 1048576 | bytes 4194304 | tf_op jit(solution)/shard_map/finish/pallas_call | solution.py:265
  27.7 1.5 %all-to-all-done = bf16[32,9,8,128]{3,2,1,0:T(8,128)(2,1)S(1)} async-done(((bf16[32,9,8,128]{3,2,1,0:T(8,128)(2,1)}), bf16[32,9,8,128]{3,2,1,0:T(8,128)(2,1)S(1)}, u32[]{:S(2)}, u32[]{:S(2)}) %all-to-all-start) | async-done | bytes 589856 | tf_op jit(solution)/shard_map/all_to_all | solution.py:581
  29.2 3.3 %backward.1 = (f32[8,32,256]{2,1,0:T(8,128)S(1)}, f32[2,152,128]{2,1,0:T(8,128)S(1)}, bf16[2176,256]{1,0:T(8,128)(2,1)S(1)}, f32[3,8,192]{2,1,0:T(8,128)S(1)}) custom-call(bf16[32,72,128]{2,1,0:T(8,128)(2,1)S(1)} %bitcast.23, bf16[32,8,256]{2,1,0:T(8,128)(2,1)S(1)} %bitcast.26, bf16[2,8,256]{2,1,0:T(8,128)(2,1)S(1)} %pad_maximum_fusion.edge_ref, ...), custom_call_target="tpu_custom_call" | custom-call | flops 754974720 | bytes 4194304 | tf_op jit(solution)/shard_map/backward/pallas_call | solution.py:413
  32.6 1.6 %lift_gradient.1 = f32[152,128]{1,0:T(8,128)S(1)} custom-call(bf16[2176,256]{1,0:T(8,128)(2,1)S(1)} %get-tuple-element.46.slope_ref, bf16[32,8,256]{2,1,0:T(8,128)(2,1)S(1)} %bitcast.27, bf16[192,192]{1,0:T(8,128)(2,1)S(1)} %get-tuple-element.47.back_ref, bf16[3,64,192]{2,1,0:T(8,128)(2,1)S(1)} %copy-done.3, f32[3,8,192]{2,1,0:T(8,128)S(1)} %get-tuple-element.49.moment_ref), custom_call_target="tpu_custom_call" | custom-call | flops 603979776 | bytes 1114112 | tf_op jit(solution)/shard_map/lift_gradient/pallas_call | solution.py:482
  34.2 0.9 %collective-permute-start.7 = (f32[152,128]{1,0:T(8,128)S(1)}, f32[152,128]{1,0:T(8,128)S(1)}, u32[]{:S(2)}, u32[]{:S(2)}) collective-permute-start(f32[152,128]{1,0:T(8,128)S(1)} %fusion), channel_id=1, source_target_pairs={{0,24},{8,16},{16,8},{24,0},{1,25},{9,17},{17,9},{25,1},{2,26},{10... | collective-permute-start | bytes 233480 | tf_op jit(solution)/shard_map/ppermute | solution.py:531
  35.1 1.5 %collective-permute-start.6 = (f32[152,128]{1,0:T(8,128)S(1)}, f32[152,128]{1,0:T(8,128)S(1)}, u32[]{:S(2)}, u32[]{:S(2)}) collective-permute-start(f32[152,128]{1,0:T(8,128)S(1)} %fusion), channel_id=1, source_target_pairs={{0,16},{8,24},{16,0},{24,8},{1,17},{9,25},{17,1},{25,9},{2,18},{10... | collective-permute-start | bytes 233480 | tf_op jit(solution)/shard_map/ppermute | solution.py:531
  36.6 1.2 %collective-permute-start.5 = (f32[152,128]{1,0:T(8,128)S(1)}, f32[152,128]{1,0:T(8,128)S(1)}, u32[]{:S(2)}, u32[]{:S(2)}) collective-permute-start(f32[152,128]{1,0:T(8,128)S(1)} %fusion), channel_id=1, source_target_pairs={{0,8},{8,0},{16,24},{24,16},{1,9},{9,1},{17,25},{25,17},{2,10},{10... | collective-permute-start | bytes 233480 | tf_op jit(solution)/shard_map/ppermute | solution.py:531
  37.8 0.7 %convert_element_type.10 = bf16[8,32,256]{2,1,0:T(8,128)(2,1)} convert(f32[8,32,256]{2,1,0:T(8,128)S(1)} %get-tuple-element.44.forecast_ref) | non-fusion elementwise | flops 65536 | bytes 393216 | tf_op jit(solution)/shard_map/convert_element_type | solution.py:609
  38.4 0.7 %convert_element_type.9 = bf16[8,32,256]{2,1,0:T(8,128)(2,1)} convert(f32[8,32,256]{2,1,0:T(8,128)S(1)} %get-tuple-element.50) | non-fusion elementwise | flops 65536 | bytes 393216 | tf_op jit(solution)/shard_map/convert_element_type | solution.py:609
  39.1 1.3 %collective-permute-done.7 = f32[152,128]{1,0:T(8,128)S(1)} collective-permute-done((f32[152,128]{1,0:T(8,128)S(1)}, f32[152,128]{1,0:T(8,128)S(1)}, u32[]{:S(2)}, u32[]{:S(2)}) %collective-permute-start.7) | collective-permute-done | bytes 77856 | tf_op jit(solution)/shard_map/ppermute | solution.py:531
  40.4 0.6 %collective-permute-done.6 = f32[152,128]{1,0:T(8,128)S(1)} collective-permute-done((f32[152,128]{1,0:T(8,128)S(1)}, f32[152,128]{1,0:T(8,128)S(1)}, u32[]{:S(2)}, u32[]{:S(2)}) %collective-permute-start.6) | collective-permute-done | bytes 77856 | tf_op jit(solution)/shard_map/ppermute | solution.py:531
  41.0 1.1 %collective-permute-start.10 = (f32[152,128]{1,0:T(8,128)S(1)}, f32[152,128]{1,0:T(8,128)S(1)}, u32[]{:S(2)}, u32[]{:S(2)}) collective-permute-start(f32[152,128]{1,0:T(8,128)S(1)} %add_add_fusion.1), channel_id=1, source_target_pairs={{0,6},{1,7},{2,4},{3,5},{4,2},{5,3},{6,0},{7,1},{8,14},{9,15},{10,... | collective-permute-start | bytes 233480 | tf_op jit(solution)/shard_map/ppermute | solution.py:531
  42.2 1.6 %collective-permute-start.9 = (f32[152,128]{1,0:T(8,128)S(1)}, f32[152,128]{1,0:T(8,128)S(1)}, u32[]{:S(2)}, u32[]{:S(2)}) collective-permute-start(f32[152,128]{1,0:T(8,128)S(1)} %add_add_fusion.1), channel_id=1, source_target_pairs={{0,4},{1,5},{2,6},{3,7},{4,0},{5,1},{6,2},{7,3},{8,12},{9,13},{10,... | collective-permute-start | bytes 233480 | tf_op jit(solution)/shard_map/ppermute | solution.py:531
  43.8 1.7 %collective-permute-start.8 = (f32[152,128]{1,0:T(8,128)S(1)}, f32[152,128]{1,0:T(8,128)S(1)}, u32[]{:S(2)}, u32[]{:S(2)}) collective-permute-start(f32[152,128]{1,0:T(8,128)S(1)} %add_add_fusion.1), channel_id=1, source_target_pairs={{0,2},{1,3},{2,0},{3,1},{4,6},{5,7},{6,4},{7,5},{8,10},{9,11},{10,... | collective-permute-start | bytes 233480 | tf_op jit(solution)/shard_map/ppermute | solution.py:531
  45.5 2.6 %collective-permute-done.10 = f32[152,128]{1,0:T(8,128)S(1)} collective-permute-done((f32[152,128]{1,0:T(8,128)S(1)}, f32[152,128]{1,0:T(8,128)S(1)}, u32[]{:S(2)}, u32[]{:S(2)}) %collective-permute-start.10) | collective-permute-done | bytes 77856 | tf_op jit(solution)/shard_map/ppermute | solution.py:531
  48.1 2.5 %collective-permute-done.9 = f32[152,128]{1,0:T(8,128)S(1)} collective-permute-done((f32[152,128]{1,0:T(8,128)S(1)}, f32[152,128]{1,0:T(8,128)S(1)}, u32[]{:S(2)}, u32[]{:S(2)}) %collective-permute-start.9) | collective-permute-done | bytes 77856 | tf_op jit(solution)/shard_map/ppermute | solution.py:531
  50.7 1.3 %collective-permute-done.11.other_ref = f32[152,128]{1,0:T(8,128)S(1)} collective-permute-done((f32[152,128]{1,0:T(8,128)S(1)}, f32[152,128]{1,0:T(8,128)S(1)}, u32[]{:S(2)}, u32[]{:S(2)}) %collective-permute-start.11) | collective-permute-done | bytes 77856 | tf_op jit(solution)/shard_map/ppermute | solution.py:531
  51.9 0.8 %unpack.1 = (f32[9,64,64]{2,1,0:T(8,128)}, f32[8,64]{1,0:T(8,128)}, f32[8,64]{1,0:T(8,128)}) custom-call(f32[152,128]{1,0:T(8,128)S(1)} %add_add_fusion.mine_ref, f32[152,128]{1,0:T(8,128)S(1)} %collective-permute-done.11.other_ref), custom_call_target="tpu_custom_call" | custom-call | tf_op jit(solution)/shard_map/unpack/pallas_call | solution.py:518
  (31 shorter events, 0.3 us)
Async XLA Ops:
  0.6 10.8 %copy-start.4 = (bf16[8,32,256]{2,1,0:T(8,128)(2,1)S(1)}, bf16[8,32,256]{2,1,0:T(8,128)(2,1)}, u32[]{:S(2)}) copy-start(bf16[8,32,256]{2,1,0:T(8,128)(2,1)} %param.12) | copy-start | bytes 393220
  4.1 13.0 %copy-start.5 = (bf16[64,8]{0,1:T(8,128)(2,1)S(1)}, bf16[64,8]{0,1:T(8,128)(2,1)}, u32[]{:S(2)}) copy-start(bf16[64,8]{0,1:T(8,128)(2,1)} %param.15) | copy-start | bytes 3076
  4.1 18.4 %copy-start = (bf16[9,64,64]{2,1,0:T(8,128)(2,1)S(1)}, bf16[9,64,64]{2,1,0:T(8,128)(2,1)}, u32[]{:S(2)}) copy-start(bf16[9,64,64]{2,1,0:T(8,128)(2,1)} %kernel_ref) | copy-start | bytes 221188
  4.1 18.4 %copy-start.1 = (bf16[8,64]{1,0:T(8,128)(2,1)S(1)}, bf16[8,64]{1,0:T(8,128)(2,1)}, u32[]{:S(2)}) copy-start(bf16[8,64]{1,0:T(8,128)(2,1)} %lift_weight_ref) | copy-start | bytes 3076
  4.1 25.1 %all-to-all-start = ((bf16[32,9,8,128]{3,2,1,0:T(8,128)(2,1)}), bf16[32,9,8,128]{3,2,1,0:T(8,128)(2,1)S(1)}, u32[]{:S(2)}, u32[]{:S(2)}) async-start(bf16[32,9,8,128]{3,2,1,0:T(8,128)(2,1)} %regrid.1), calls=%async_computation | async-start | bytes 1179648 | tf_op jit(solution)/shard_map/all_to_all | solution.py:581
  11.5 5.7 %collective-permute-start = (bf16[8,256]{1,0:T(8,128)(2,1)S(1)}, bf16[8,256]{1,0:T(8,128)(2,1)S(1)}, u32[]{:S(2)}, u32[]{:S(2)}) collective-permute-start(bf16[8,256]{1,0:T(8,128)(2,1)S(1)} %get-tuple-element.62), channel_id=1, source_target_pairs={{8,16},{16,8},{9,17},{17,9},{10,18},{18,10},{11,19},{19,11},{12,20... | collective-permute-start | bytes 12296 | tf_op jit(solution)/shard_map/ppermute | solution.py:554
  12.2 6.3 %collective-permute-start.1 = (bf16[8,256]{1,0:T(8,128)(2,1)S(1)}, bf16[8,256]{1,0:T(8,128)(2,1)S(1)}, u32[]{:S(2)}, u32[]{:S(2)}) collective-permute-start(bf16[8,256]{1,0:T(8,128)(2,1)S(1)} %get-tuple-element.63), channel_id=1, source_target_pairs={{0,8},{8,0},{16,24},{24,16},{1,9},{9,1},{17,25},{25,17},{2,10},{10... | collective-permute-start | bytes 12296 | tf_op jit(solution)/shard_map/ppermute | solution.py:553
  18.7 7.7 %collective-permute-start.3 = (bf16[8,128]{1,0:T(8,128)(2,1)S(1)}, bf16[8,128]{1,0:T(8,128)(2,1)S(1)}, u32[]{:S(2)}, u32[]{:S(2)}) collective-permute-start(bf16[8,128]{1,0:T(8,128)(2,1)S(1)} %broadcast_select_fusion.4), channel_id=1, source_target_pairs={{0,1},{1,0},{2,3},{3,2},{4,5},{5,4},{6,7},{7,6},{8,9},{9,8},{10,11... | collective-permute-start | bytes 6152 | tf_op jit(solution)/shard_map/ppermute | solution.py:553
  18.8 7.7 %collective-permute-start.2 = (bf16[8,128]{1,0:T(8,128)(2,1)S(1)}, bf16[8,128]{1,0:T(8,128)(2,1)S(1)}, u32[]{:S(2)}, u32[]{:S(2)}) collective-permute-start(bf16[8,128]{1,0:T(8,128)(2,1)S(1)} %get-tuple-element.57), channel_id=1, source_target_pairs={{1,2},{2,1},{3,4},{4,3},{5,6},{6,5},{7,0},{0,7},{9,10},{10,9},{11,... | collective-permute-start | bytes 6152 | tf_op jit(solution)/shard_map/ppermute | solution.py:554
  25.8 0.6 %copy-start.2 = (bf16[3,64,192]{2,1,0:T(8,128)(2,1)}, bf16[3,64,192]{2,1,0:T(8,128)(2,1)S(1)}, u32[]{:S(2)}) copy-start(bf16[3,64,192]{2,1,0:T(8,128)(2,1)S(1)} %get-tuple-element.48.contract_ref) | copy-start | bytes 221188
  27.7 4.9 %copy-start.3 = (bf16[3,64,192]{2,1,0:T(8,128)(2,1)S(1)}, bf16[3,64,192]{2,1,0:T(8,128)(2,1)}, u32[]{:S(2)}) copy-start(bf16[3,64,192]{2,1,0:T(8,128)(2,1)} %copy-done.2) | copy-start | bytes 221188
  32.5 1.7 %collective-permute-start.4 = (f32[152,128]{1,0:T(8,128)S(1)}, f32[152,128]{1,0:T(8,128)S(1)}, u32[]{:S(2)}, u32[]{:S(2)}) collective-permute-start(f32[152,128]{1,0:T(8,128)S(1)} %slice_bitcast_fusion), channel_id=1, source_target_pairs={{0,1},{1,0},{2,3},{3,2},{4,5},{5,4},{6,7},{7,6},{8,9},{9,8},{10,11... | collective-permute-start | bytes 233480 | tf_op jit(solution)/shard_map/ppermute | solution.py:531
  34.2 6.2 %collective-permute-start.7 = (f32[152,128]{1,0:T(8,128)S(1)}, f32[152,128]{1,0:T(8,128)S(1)}, u32[]{:S(2)}, u32[]{:S(2)}) collective-permute-start(f32[152,128]{1,0:T(8,128)S(1)} %fusion), channel_id=1, source_target_pairs={{0,24},{8,16},{16,8},{24,0},{1,25},{9,17},{17,9},{25,1},{2,26},{10... | collective-permute-start | bytes 233480 | tf_op jit(solution)/shard_map/ppermute | solution.py:531
  35.1 5.9 %collective-permute-start.6 = (f32[152,128]{1,0:T(8,128)S(1)}, f32[152,128]{1,0:T(8,128)S(1)}, u32[]{:S(2)}, u32[]{:S(2)}) collective-permute-start(f32[152,128]{1,0:T(8,128)S(1)} %fusion), channel_id=1, source_target_pairs={{0,16},{8,24},{16,0},{24,8},{1,17},{9,25},{17,1},{25,9},{2,18},{10... | collective-permute-start | bytes 233480 | tf_op jit(solution)/shard_map/ppermute | solution.py:531
  36.6 4.4 %collective-permute-start.5 = (f32[152,128]{1,0:T(8,128)S(1)}, f32[152,128]{1,0:T(8,128)S(1)}, u32[]{:S(2)}, u32[]{:S(2)}) collective-permute-start(f32[152,128]{1,0:T(8,128)S(1)} %fusion), channel_id=1, source_target_pairs={{0,8},{8,0},{16,24},{24,16},{1,9},{9,1},{17,25},{25,17},{2,10},{10... | collective-permute-start | bytes 233480 | tf_op jit(solution)/shard_map/ppermute | solution.py:531
  41.0 7.1 %collective-permute-start.10 = (f32[152,128]{1,0:T(8,128)S(1)}, f32[152,128]{1,0:T(8,128)S(1)}, u32[]{:S(2)}, u32[]{:S(2)}) collective-permute-start(f32[152,128]{1,0:T(8,128)S(1)} %add_add_fusion.1), channel_id=1, source_target_pairs={{0,6},{1,7},{2,4},{3,5},{4,2},{5,3},{6,0},{7,1},{8,14},{9,15},{10,... | collective-permute-start | bytes 233480 | tf_op jit(solution)/shard_map/ppermute | solution.py:531
  42.2 8.4 %collective-permute-start.9 = (f32[152,128]{1,0:T(8,128)S(1)}, f32[152,128]{1,0:T(8,128)S(1)}, u32[]{:S(2)}, u32[]{:S(2)}) collective-permute-start(f32[152,128]{1,0:T(8,128)S(1)} %add_add_fusion.1), channel_id=1, source_target_pairs={{0,4},{1,5},{2,6},{3,7},{4,0},{5,1},{6,2},{7,3},{8,12},{9,13},{10,... | collective-permute-start | bytes 233480 | tf_op jit(solution)/shard_map/ppermute | solution.py:531
  43.8 6.8 %collective-permute-start.8 = (f32[152,128]{1,0:T(8,128)S(1)}, f32[152,128]{1,0:T(8,128)S(1)}, u32[]{:S(2)}, u32[]{:S(2)}) collective-permute-start(f32[152,128]{1,0:T(8,128)S(1)} %add_add_fusion.1), channel_id=1, source_target_pairs={{0,2},{1,3},{2,0},{3,1},{4,6},{5,7},{6,4},{7,5},{8,10},{9,11},{10,... | collective-permute-start | bytes 233480 | tf_op jit(solution)/shard_map/ppermute | solution.py:531
  50.6 1.3 %collective-permute-start.11 = (f32[152,128]{1,0:T(8,128)S(1)}, f32[152,128]{1,0:T(8,128)S(1)}, u32[]{:S(2)}, u32[]{:S(2)}) collective-permute-start(f32[152,128]{1,0:T(8,128)S(1)} %add_add_fusion.mine_ref), channel_id=1, source_target_pairs={{0,1},{1,0},{2,3},{3,2},{4,5},{5,4},{6,7},{7,6},{8,9},{9,8},{10,11... | collective-permute-start | bytes 233480 | tf_op jit(solution)/shard_map/ppermute | solution.py:531

commit v7 on v6

--- a/solution.py
+++ b/solution.py
@@ -19,10 +19,6 @@
 
 def dot_nt(a, b):
     return lax.dot_general(a, b, NT, preferred_element_type=jnp.float32)
-
-
-def sigmoid(x):
-    return 1.0 / (1.0 + jnp.exp(-x))
 
 
 def regrid_kernel(
@@ -168,7 +164,7 @@
         right = jnp.where(col == width - 1, 0.0, pltpu.roll(parts[2 * channels :], width - 1, 1))
         act = parts[channels : 2 * channels] + left + right
         act_ref[y * channels : (y + 1) * channels, :] = act
-        hidden_ref[y * channels : (y + 1) * channels, :] = (act * sigmoid(act)).astype(jnp.bfloat16)
+        hidden_ref[y * channels : (y + 1) * channels, :] = (act * lax.logistic(act)).astype(jnp.bfloat16)
         ends_left += pltpu.roll(jnp.where(lane == 0, act[:, :128], 0.0), y, 1)
         ends_right += pltpu.roll(jnp.where(lane == 127, act[:, -128:], 0.0), y + 1, 1)
     ends_ref[:, :128] = ends_left
@@ -234,7 +230,7 @@
     stack_ref[...] = stack
     left = ends_ref[:, :128] + dot(conv_ref[:channels, :], stack[:, :128])
     right = ends_ref[:, 128:] + dot(conv_ref[2 * channels :, :], stack[:, 128:])
-    hidden = jnp.concatenate([(act * sigmoid(act)).astype(jnp.bfloat16) for act in (left, right)], axis=1)
+    hidden = jnp.concatenate([(act * lax.logistic(act)).astype(jnp.bfloat16) for act in (left, right)], axis=1)
     forecast = pltpu.roll(own_ref[...].astype(jnp.float32), 255, 1) + dot(turned_ref[...], hidden)
 
     lane = lax.broadcasted_iota(jnp.int32, (channels, 128), 1)
@@ -357,10 +353,11 @@
         for y in range(first, first + batch):
             here = slice(y * channels, (y + 1) * channels)
             act = act_ref[here, :]
-            sig = sigmoid(act)
-            hidden_ref[here, :] = (act * sig).astype(jnp.bfloat16)
+            sig = lax.logistic(act)
+            silu = act * sig
+            hidden_ref[here, :] = silu.astype(jnp.bfloat16)
             latent = latents[(y - first) * channels : (y - first + 1) * channels]
-            slope = latent * sig * (1.0 + act * (1.0 - sig))
+            slope = latent * (sig + silu * (1.0 - sig))
             slope_ref[(y + 1) * channels : (y + 2) * channels, :] = slope.astype(jnp.bfloat16)
             before = jnp.where(col == width - 1, 0.0, pltpu.roll(slope, width - 1, 1))
             before_ref[here, :] = before.astype(jnp.bfloat16)

time: 52.9 us -> 52.7 us (level)
  transfers between devices with their start and end apart: 13 -> 13, of which waited for: 7 -> 7; matrix products, arithmetic and copies ran while one was open for 4% -> 4% of each run, Pallas kernels for 12% -> 11%
where the time goes in v7:
time: 52.7 us; the launch traced here: 52.5 us
  starting transfers between devices  24.4 us (46%)
  Pallas kernels  13.3 us (25%)
  waiting for transfers between devices  11.1 us (21%)
  other arithmetic  1.53 us (3%)
  local copies, waits for them, and re-layouts  1.24 us (2%)
  between operations  0.87 us (2%)
    ppermute x8, waiting for transfers between devices, swap(): lax.ppermute(x, axis, [(i, i ^ bit) for i in range(lax.axis_size(axis))])  8.19 us
    ppermute x8, starting transfers between devices, swap(): lax.ppermute(x, axis, [(i, i ^ bit) for i in range(lax.axis_size(axis))])  8.15 us
    all_to_all x1, starting transfers between devices, per_device(): lax.all_to_all(outgoing, ('face', 'lon'), split_axis=0, concat_axis=0, ti...  7.31 us
    ppermute x2, starting transfers between devices, pair_swap(): lax.ppermute(jnp.where(even, odd_sends, even_sends), axis, inner)  4.61 us
    ppermute x2, starting transfers between devices, pair_swap(): lax.ppermute(jnp.where(even, even_sends, odd_sends), axis, outer)  4.36 us
    pallas_call x1, Pallas kernels, regrid(): pl.pallas_call(functools.partial(regrid_kernel, capacity), out_shape=jax....  3.4 us
    pallas_call x1, Pallas kernels, convolve(): pl.pallas_call(convolve_kernel, out_shape=(jax.ShapeDtypeStruct((rows * c...  3.14 us
    pallas_call x1, Pallas kernels, backward(): pl.pallas_call(functools.partial(backward_kernel, capacity, channels, nor...  3.06 us
  transfers between devices with their start and end apart: 13, of which 7 were waited for; matrix products, arithmetic and copies ran while one was open for 4% of the time, Pallas kernels for 11%

profile of v7, /device:TPU:0, one launch (start us, length us, event | category | flops | bytes accessed | tf_op | source)
XLA Modules:
  0.0 52.5 jit_solution(6800720620845380742)
XLA Ops:
  0.6 3.4 %regrid.1 = bf16[32,9,8,128]{3,2,1,0:T(8,128)(2,1)} custom-call(s32[4,32]{1,0:T(4,128)} %bitcast.30, s32[4,32]{1,0:T(4,128)} %bitcast.31, bf16[32,8,128]{2,1,0:T(8,128)(2,1)} %src_hbm.1, bf16[32,4,128,128]{3,2,1,0:T(8,128)(2,1)} %wts_hbm.1), custom_call_target="tpu_custom_call" | custom-call | flops 33554432 | bytes 4194304 | tf_op jit(solution)/shard_map/regrid/pallas_call | solution.py:88
  4.1 7.3 %all-to-all-start = ((bf16[32,9,8,128]{3,2,1,0:T(8,128)(2,1)}), bf16[32,9,8,128]{3,2,1,0:T(8,128)(2,1)S(1)}, u32[]{:S(2)}, u32[]{:S(2)}) async-start(bf16[32,9,8,128]{3,2,1,0:T(8,128)(2,1)} %regrid.1), calls=%async_computation | async-start | bytes 1179648 | tf_op jit(solution)/shard_map/all_to_all | solution.py:578
  11.4 0.1 copy.21
  11.5 0.7 %collective-permute-start = (bf16[8,256]{1,0:T(8,128)(2,1)S(1)}, bf16[8,256]{1,0:T(8,128)(2,1)S(1)}, u32[]{:S(2)}, u32[]{:S(2)}) collective-permute-start(bf16[8,256]{1,0:T(8,128)(2,1)S(1)} %get-tuple-element.62), channel_id=1, source_target_pairs={{8,16},{16,8},{9,17},{17,9},{10,18},{18,10},{11,19},{19,11},{12,20... | collective-permute-start | bytes 12296 | tf_op jit(solution)/shard_map/ppermute | solution.py:551
  12.2 4.5 %collective-permute-start.1 = (bf16[8,256]{1,0:T(8,128)(2,1)S(1)}, bf16[8,256]{1,0:T(8,128)(2,1)S(1)}, u32[]{:S(2)}, u32[]{:S(2)}) collective-permute-start(bf16[8,256]{1,0:T(8,128)(2,1)S(1)} %get-tuple-element.63), channel_id=1, source_target_pairs={{0,8},{8,0},{16,24},{24,16},{1,9},{9,1},{17,25},{25,17},{2,10},{10... | collective-permute-start | bytes 12296 | tf_op jit(solution)/shard_map/ppermute | solution.py:550
  16.7 0.3 copy.17
  17.1 0.1 copy.16.readout_ref
  17.2 1.3 %collective-permute-done.1 = bf16[8,256]{1,0:T(8,128)(2,1)S(1)} collective-permute-done((bf16[8,256]{1,0:T(8,128)(2,1)S(1)}, bf16[8,256]{1,0:T(8,128)(2,1)S(1)}, u32[]{:S(2)}, u32[]{:S(2)}) %collective-permute-start.1) | collective-permute-done | bytes 4128 | tf_op jit(solution)/shard_map/ppermute | solution.py:550
  18.5 0.1 fusion.13
  18.6 0.1 broadcast_select_fusion.5
  18.7 0.1 collective-permute-start.3
  18.8 3.7 %collective-permute-start.2 = (bf16[8,128]{1,0:T(8,128)(2,1)S(1)}, bf16[8,128]{1,0:T(8,128)(2,1)S(1)}, u32[]{:S(2)}, u32[]{:S(2)}) collective-permute-start(bf16[8,128]{1,0:T(8,128)(2,1)S(1)} %get-tuple-element.57), channel_id=1, source_target_pairs={{1,2},{2,1},{3,4},{4,3},{5,6},{6,5},{7,0},{0,7},{9,10},{10,9},{11,... | collective-permute-start | bytes 6152 | tf_op jit(solution)/shard_map/ppermute | solution.py:551
  22.5 3.1 %convolve.1 = (f32[2048,256]{1,0:T(8,128)S(1)}, f32[8,32,256]{2,1,0:T(8,128)S(1)}, f32[64,256]{1,0:T(8,128)S(1)}, bf16[80,8]{1,0:T(8,128)(2,1)S(1)}, bf16[192,24...) custom-call(bf16[32,8,256]{2,1,0:T(8,128)(2,1)S(1)} %bitcast.25, ...), custom_call_target="tpu_custom_call" | custom-call | flops 754974720 | bytes 4194304 | tf_op jit(solution)/shard_map/convolve/pallas_call | solution.py:183
  25.6 0.6 %copy-done.2 = bf16[3,64,192]{2,1,0:T(8,128)(2,1)} copy-done((bf16[3,64,192]{2,1,0:T(8,128)(2,1)}, bf16[3,64,192]{2,1,0:T(8,128)(2,1)S(1)}, u32[]{:S(2)}) %copy-start.2) | copy-done | bytes 73752
  26.3 1.3 %finish.1 = (f32[2048,256]{1,0:T(8,128)S(1)}, f32[8,32,256]{2,1,0:T(8,128)S(1)}, bf16[240,256]{1,0:T(8,128)(2,1)S(1)}) custom-call(f32[2048,256]{1,0:T(8,128)S(1)} %get-tuple-element.36.old_act_ref, f32[8,32,256]{2,1,0:T(8,128)S(1)} %get-tuple-element.37.old_forecast_ref, ...), custom_call_target="tpu_custom_call", output_to_operand_aliasing={{0}: (0, {}), {1}: (1, {})} | custom-call | flops 1048576 | bytes 4194304 | tf_op jit(solution)/shard_map/finish/pallas_call | solution.py:261
  27.6 1.6 %all-to-all-done = bf16[32,9,8,128]{3,2,1,0:T(8,128)(2,1)S(1)} async-done(((bf16[32,9,8,128]{3,2,1,0:T(8,128)(2,1)}), bf16[32,9,8,128]{3,2,1,0:T(8,128)(2,1)S(1)}, u32[]{:S(2)}, u32[]{:S(2)}) %all-to-all-start) | async-done | bytes 589856 | tf_op jit(solution)/shard_map/all_to_all | solution.py:578
  29.2 3.1 %backward.1 = (f32[8,32,256]{2,1,0:T(8,128)S(1)}, f32[2,152,128]{2,1,0:T(8,128)S(1)}, bf16[2176,256]{1,0:T(8,128)(2,1)S(1)}, f32[3,8,192]{2,1,0:T(8,128)S(1)}) custom-call(bf16[32,72,128]{2,1,0:T(8,128)(2,1)S(1)} %bitcast.23, bf16[32,8,256]{2,1,0:T(8,128)(2,1)S(1)} %bitcast.26, bf16[2,8,256]{2,1,0:T(8,128)(2,1)S(1)} %pad_maximum_fusion.edge_ref, ...), custom_call_target="tpu_custom_call" | custom-call | flops 754974720 | bytes 4194304 | tf_op jit(solution)/shard_map/backward/pallas_call | solution.py:410
  32.3 1.6 %lift_gradient.1 = f32[152,128]{1,0:T(8,128)S(1)} custom-call(bf16[2176,256]{1,0:T(8,128)(2,1)S(1)} %get-tuple-element.46.slope_ref, bf16[32,8,256]{2,1,0:T(8,128)(2,1)S(1)} %bitcast.27, bf16[192,192]{1,0:T(8,128)(2,1)S(1)} %get-tuple-element.47.back_ref, bf16[3,64,192]{2,1,0:T(8,128)(2,1)S(1)} %copy-done.3, f32[3,8,192]{2,1,0:T(8,128)S(1)} %get-tuple-element.49.moment_ref), custom_call_target="tpu_custom_call" | custom-call | flops 603979776 | bytes 1114112 | tf_op jit(solution)/shard_map/lift_gradient/pallas_call | solution.py:479
  34.0 0.9 %collective-permute-start.7 = (f32[152,128]{1,0:T(8,128)S(1)}, f32[152,128]{1,0:T(8,128)S(1)}, u32[]{:S(2)}, u32[]{:S(2)}) collective-permute-start(f32[152,128]{1,0:T(8,128)S(1)} %fusion), channel_id=1, source_target_pairs={{0,24},{8,16},{16,8},{24,0},{1,25},{9,17},{17,9},{25,1},{2,26},{10... | collective-permute-start | bytes 233480 | tf_op jit(solution)/shard_map/ppermute | solution.py:528
  34.9 1.5 %collective-permute-start.6 = (f32[152,128]{1,0:T(8,128)S(1)}, f32[152,128]{1,0:T(8,128)S(1)}, u32[]{:S(2)}, u32[]{:S(2)}) collective-permute-start(f32[152,128]{1,0:T(8,128)S(1)} %fusion), channel_id=1, source_target_pairs={{0,16},{8,24},{16,0},{24,8},{1,17},{9,25},{17,1},{25,9},{2,18},{10... | collective-permute-start | bytes 233480 | tf_op jit(solution)/shard_map/ppermute | solution.py:528
  36.4 1.2 %collective-permute-start.5 = (f32[152,128]{1,0:T(8,128)S(1)}, f32[152,128]{1,0:T(8,128)S(1)}, u32[]{:S(2)}, u32[]{:S(2)}) collective-permute-start(f32[152,128]{1,0:T(8,128)S(1)} %fusion), channel_id=1, source_target_pairs={{0,8},{8,0},{16,24},{24,16},{1,9},{9,1},{17,25},{25,17},{2,10},{10... | collective-permute-start | bytes 233480 | tf_op jit(solution)/shard_map/ppermute | solution.py:528
  37.6 0.7 %convert_element_type.10 = bf16[8,32,256]{2,1,0:T(8,128)(2,1)} convert(f32[8,32,256]{2,1,0:T(8,128)S(1)} %get-tuple-element.44.forecast_ref) | non-fusion elementwise | flops 65536 | bytes 393216 | tf_op jit(solution)/shard_map/convert_element_type | solution.py:606
  38.2 0.7 %convert_element_type.9 = bf16[8,32,256]{2,1,0:T(8,128)(2,1)} convert(f32[8,32,256]{2,1,0:T(8,128)S(1)} %get-tuple-element.50) | non-fusion elementwise | flops 65536 | bytes 393216 | tf_op jit(solution)/shard_map/convert_element_type | solution.py:606
  38.9 1.3 %collective-permute-done.7 = f32[152,128]{1,0:T(8,128)S(1)} collective-permute-done((f32[152,128]{1,0:T(8,128)S(1)}, f32[152,128]{1,0:T(8,128)S(1)}, u32[]{:S(2)}, u32[]{:S(2)}) %collective-permute-start.7) | collective-permute-done | bytes 77856 | tf_op jit(solution)/shard_map/ppermute | solution.py:528
  40.2 0.6 %collective-permute-done.6 = f32[152,128]{1,0:T(8,128)S(1)} collective-permute-done((f32[152,128]{1,0:T(8,128)S(1)}, f32[152,128]{1,0:T(8,128)S(1)}, u32[]{:S(2)}, u32[]{:S(2)}) %collective-permute-start.6) | collective-permute-done | bytes 77856 | tf_op jit(solution)/shard_map/ppermute | solution.py:528
  40.8 1.1 %collective-permute-start.10 = (f32[152,128]{1,0:T(8,128)S(1)}, f32[152,128]{1,0:T(8,128)S(1)}, u32[]{:S(2)}, u32[]{:S(2)}) collective-permute-start(f32[152,128]{1,0:T(8,128)S(1)} %add_add_fusion.1), channel_id=1, source_target_pairs={{0,6},{1,7},{2,4},{3,5},{4,2},{5,3},{6,0},{7,1},{8,14},{9,15},{10,... | collective-permute-start | bytes 233480 | tf_op jit(solution)/shard_map/ppermute | solution.py:528
  41.9 1.6 %collective-permute-start.9 = (f32[152,128]{1,0:T(8,128)S(1)}, f32[152,128]{1,0:T(8,128)S(1)}, u32[]{:S(2)}, u32[]{:S(2)}) collective-permute-start(f32[152,128]{1,0:T(8,128)S(1)} %add_add_fusion.1), channel_id=1, source_target_pairs={{0,4},{1,5},{2,6},{3,7},{4,0},{5,1},{6,2},{7,3},{8,12},{9,13},{10,... | collective-permute-start | bytes 233480 | tf_op jit(solution)/shard_map/ppermute | solution.py:528
  43.6 1.7 %collective-permute-start.8 = (f32[152,128]{1,0:T(8,128)S(1)}, f32[152,128]{1,0:T(8,128)S(1)}, u32[]{:S(2)}, u32[]{:S(2)}) collective-permute-start(f32[152,128]{1,0:T(8,128)S(1)} %add_add_fusion.1), channel_id=1, source_target_pairs={{0,2},{1,3},{2,0},{3,1},{4,6},{5,7},{6,4},{7,5},{8,10},{9,11},{10,... | collective-permute-start | bytes 233480 | tf_op jit(solution)/shard_map/ppermute | solution.py:528
  45.2 2.6 %collective-permute-done.10 = f32[152,128]{1,0:T(8,128)S(1)} collective-permute-done((f32[152,128]{1,0:T(8,128)S(1)}, f32[152,128]{1,0:T(8,128)S(1)}, u32[]{:S(2)}, u32[]{:S(2)}) %collective-permute-start.10) | collective-permute-done | bytes 77856 | tf_op jit(solution)/shard_map/ppermute | solution.py:528
  47.8 2.5 %collective-permute-done.9 = f32[152,128]{1,0:T(8,128)S(1)} collective-permute-done((f32[152,128]{1,0:T(8,128)S(1)}, f32[152,128]{1,0:T(8,128)S(1)}, u32[]{:S(2)}, u32[]{:S(2)}) %collective-permute-start.9) | collective-permute-done | bytes 77856 | tf_op jit(solution)/shard_map/ppermute | solution.py:528
  50.4 1.3 %collective-permute-done.11.other_ref = f32[152,128]{1,0:T(8,128)S(1)} collective-permute-done((f32[152,128]{1,0:T(8,128)S(1)}, f32[152,128]{1,0:T(8,128)S(1)}, u32[]{:S(2)}, u32[]{:S(2)}) %collective-permute-start.11) | collective-permute-done | bytes 77856 | tf_op jit(solution)/shard_map/ppermute | solution.py:528
  51.7 0.8 %unpack.1 = (f32[9,64,64]{2,1,0:T(8,128)}, f32[8,64]{1,0:T(8,128)}, f32[8,64]{1,0:T(8,128)}) custom-call(f32[152,128]{1,0:T(8,128)S(1)} %add_add_fusion.mine_ref, f32[152,128]{1,0:T(8,128)S(1)} %collective-permute-done.11.other_ref), custom_call_target="tpu_custom_call" | custom-call | tf_op jit(solution)/shard_map/unpack/pallas_call | solution.py:515
  (31 shorter events, 0.3 us)
Async XLA Ops:
  0.6 10.8 %copy-start.4 = (bf16[8,32,256]{2,1,0:T(8,128)(2,1)S(1)}, bf16[8,32,256]{2,1,0:T(8,128)(2,1)}, u32[]{:S(2)}) copy-start(bf16[8,32,256]{2,1,0:T(8,128)(2,1)} %param.12) | copy-start | bytes 393220
  4.0 13.0 %copy-start.5 = (bf16[64,8]{0,1:T(8,128)(2,1)S(1)}, bf16[64,8]{0,1:T(8,128)(2,1)}, u32[]{:S(2)}) copy-start(bf16[64,8]{0,1:T(8,128)(2,1)} %param.15) | copy-start | bytes 3076
  4.1 18.4 %copy-start = (bf16[9,64,64]{2,1,0:T(8,128)(2,1)S(1)}, bf16[9,64,64]{2,1,0:T(8,128)(2,1)}, u32[]{:S(2)}) copy-start(bf16[9,64,64]{2,1,0:T(8,128)(2,1)} %kernel_ref) | copy-start | bytes 221188
  4.1 18.4 %copy-start.1 = (bf16[8,64]{1,0:T(8,128)(2,1)S(1)}, bf16[8,64]{1,0:T(8,128)(2,1)}, u32[]{:S(2)}) copy-start(bf16[8,64]{1,0:T(8,128)(2,1)} %lift_weight_ref) | copy-start | bytes 3076
  4.1 25.1 %all-to-all-start = ((bf16[32,9,8,128]{3,2,1,0:T(8,128)(2,1)}), bf16[32,9,8,128]{3,2,1,0:T(8,128)(2,1)S(1)}, u32[]{:S(2)}, u32[]{:S(2)}) async-start(bf16[32,9,8,128]{3,2,1,0:T(8,128)(2,1)} %regrid.1), calls=%async_computation | async-start | bytes 1179648 | tf_op jit(solution)/shard_map/all_to_all | solution.py:578
  11.5 5.7 %collective-permute-start = (bf16[8,256]{1,0:T(8,128)(2,1)S(1)}, bf16[8,256]{1,0:T(8,128)(2,1)S(1)}, u32[]{:S(2)}, u32[]{:S(2)}) collective-permute-start(bf16[8,256]{1,0:T(8,128)(2,1)S(1)} %get-tuple-element.62), channel_id=1, source_target_pairs={{8,16},{16,8},{9,17},{17,9},{10,18},{18,10},{11,19},{19,11},{12,20... | collective-permute-start | bytes 12296 | tf_op jit(solution)/shard_map/ppermute | solution.py:551
  12.2 6.3 %collective-permute-start.1 = (bf16[8,256]{1,0:T(8,128)(2,1)S(1)}, bf16[8,256]{1,0:T(8,128)(2,1)S(1)}, u32[]{:S(2)}, u32[]{:S(2)}) collective-permute-start(bf16[8,256]{1,0:T(8,128)(2,1)S(1)} %get-tuple-element.63), channel_id=1, source_target_pairs={{0,8},{8,0},{16,24},{24,16},{1,9},{9,1},{17,25},{25,17},{2,10},{10... | collective-permute-start | bytes 12296 | tf_op jit(solution)/shard_map/ppermute | solution.py:550
  18.7 7.6 %collective-permute-start.3 = (bf16[8,128]{1,0:T(8,128)(2,1)S(1)}, bf16[8,128]{1,0:T(8,128)(2,1)S(1)}, u32[]{:S(2)}, u32[]{:S(2)}) collective-permute-start(bf16[8,128]{1,0:T(8,128)(2,1)S(1)} %broadcast_select_fusion.4), channel_id=1, source_target_pairs={{0,1},{1,0},{2,3},{3,2},{4,5},{5,4},{6,7},{7,6},{8,9},{9,8},{10,11... | collective-permute-start | bytes 6152 | tf_op jit(solution)/shard_map/ppermute | solution.py:550
  18.8 7.5 %collective-permute-start.2 = (bf16[8,128]{1,0:T(8,128)(2,1)S(1)}, bf16[8,128]{1,0:T(8,128)(2,1)S(1)}, u32[]{:S(2)}, u32[]{:S(2)}) collective-permute-start(bf16[8,128]{1,0:T(8,128)(2,1)S(1)} %get-tuple-element.57), channel_id=1, source_target_pairs={{1,2},{2,1},{3,4},{4,3},{5,6},{6,5},{7,0},{0,7},{9,10},{10,9},{11,... | collective-permute-start | bytes 6152 | tf_op jit(solution)/shard_map/ppermute | solution.py:551
  25.6 0.6 %copy-start.2 = (bf16[3,64,192]{2,1,0:T(8,128)(2,1)}, bf16[3,64,192]{2,1,0:T(8,128)(2,1)S(1)}, u32[]{:S(2)}) copy-start(bf16[3,64,192]{2,1,0:T(8,128)(2,1)S(1)} %get-tuple-element.48.contract_ref) | copy-start | bytes 221188
  27.6 4.8 %copy-start.3 = (bf16[3,64,192]{2,1,0:T(8,128)(2,1)S(1)}, bf16[3,64,192]{2,1,0:T(8,128)(2,1)}, u32[]{:S(2)}) copy-start(bf16[3,64,192]{2,1,0:T(8,128)(2,1)} %copy-done.2) | copy-start | bytes 221188
  32.3 1.7 %collective-permute-start.4 = (f32[152,128]{1,0:T(8,128)S(1)}, f32[152,128]{1,0:T(8,128)S(1)}, u32[]{:S(2)}, u32[]{:S(2)}) collective-permute-start(f32[152,128]{1,0:T(8,128)S(1)} %slice_bitcast_fusion), channel_id=1, source_target_pairs={{0,1},{1,0},{2,3},{3,2},{4,5},{5,4},{6,7},{7,6},{8,9},{9,8},{10,11... | collective-permute-start | bytes 233480 | tf_op jit(solution)/shard_map/ppermute | solution.py:528
  34.0 6.2 %collective-permute-start.7 = (f32[152,128]{1,0:T(8,128)S(1)}, f32[152,128]{1,0:T(8,128)S(1)}, u32[]{:S(2)}, u32[]{:S(2)}) collective-permute-start(f32[152,128]{1,0:T(8,128)S(1)} %fusion), channel_id=1, source_target_pairs={{0,24},{8,16},{16,8},{24,0},{1,25},{9,17},{17,9},{25,1},{2,26},{10... | collective-permute-start | bytes 233480 | tf_op jit(solution)/shard_map/ppermute | solution.py:528
  34.9 5.9 %collective-permute-start.6 = (f32[152,128]{1,0:T(8,128)S(1)}, f32[152,128]{1,0:T(8,128)S(1)}, u32[]{:S(2)}, u32[]{:S(2)}) collective-permute-start(f32[152,128]{1,0:T(8,128)S(1)} %fusion), channel_id=1, source_target_pairs={{0,16},{8,24},{16,0},{24,8},{1,17},{9,25},{17,1},{25,9},{2,18},{10... | collective-permute-start | bytes 233480 | tf_op jit(solution)/shard_map/ppermute | solution.py:528
  36.4 4.4 %collective-permute-start.5 = (f32[152,128]{1,0:T(8,128)S(1)}, f32[152,128]{1,0:T(8,128)S(1)}, u32[]{:S(2)}, u32[]{:S(2)}) collective-permute-start(f32[152,128]{1,0:T(8,128)S(1)} %fusion), channel_id=1, source_target_pairs={{0,8},{8,0},{16,24},{24,16},{1,9},{9,1},{17,25},{25,17},{2,10},{10... | collective-permute-start | bytes 233480 | tf_op jit(solution)/shard_map/ppermute | solution.py:528
  40.8 7.0 %collective-permute-start.10 = (f32[152,128]{1,0:T(8,128)S(1)}, f32[152,128]{1,0:T(8,128)S(1)}, u32[]{:S(2)}, u32[]{:S(2)}) collective-permute-start(f32[152,128]{1,0:T(8,128)S(1)} %add_add_fusion.1), channel_id=1, source_target_pairs={{0,6},{1,7},{2,4},{3,5},{4,2},{5,3},{6,0},{7,1},{8,14},{9,15},{10,... | collective-permute-start | bytes 233480 | tf_op jit(solution)/shard_map/ppermute | solution.py:528
  41.9 8.4 %collective-permute-start.9 = (f32[152,128]{1,0:T(8,128)S(1)}, f32[152,128]{1,0:T(8,128)S(1)}, u32[]{:S(2)}, u32[]{:S(2)}) collective-permute-start(f32[152,128]{1,0:T(8,128)S(1)} %add_add_fusion.1), channel_id=1, source_target_pairs={{0,4},{1,5},{2,6},{3,7},{4,0},{5,1},{6,2},{7,3},{8,12},{9,13},{10,... | collective-permute-start | bytes 233480 | tf_op jit(solution)/shard_map/ppermute | solution.py:528
  43.6 6.7 %collective-permute-start.8 = (f32[152,128]{1,0:T(8,128)S(1)}, f32[152,128]{1,0:T(8,128)S(1)}, u32[]{:S(2)}, u32[]{:S(2)}) collective-permute-start(f32[152,128]{1,0:T(8,128)S(1)} %add_add_fusion.1), channel_id=1, source_target_pairs={{0,2},{1,3},{2,0},{3,1},{4,6},{5,7},{6,4},{7,5},{8,10},{9,11},{10,... | collective-permute-start | bytes 233480 | tf_op jit(solution)/shard_map/ppermute | solution.py:528
  50.3 1.3 %collective-permute-start.11 = (f32[152,128]{1,0:T(8,128)S(1)}, f32[152,128]{1,0:T(8,128)S(1)}, u32[]{:S(2)}, u32[]{:S(2)}) collective-permute-start(f32[152,128]{1,0:T(8,128)S(1)} %add_add_fusion.mine_ref), channel_id=1, source_target_pairs={{0,1},{1,0},{2,3},{3,2},{4,5},{5,4},{6,7},{7,6},{8,9},{9,8},{10,11... | collective-permute-start | bytes 233480 | tf_op jit(solution)/shard_map/ppermute | solution.py:528

commit v8 on v7

--- a/solution.py
+++ b/solution.py
@@ -441,6 +441,14 @@
     channels = contract_ref.shape[1]
     col = lax.broadcasted_iota(jnp.int32, (fields, width), 1)
     inside = (col > 0) & (col < width - 1)
+    grad_lift = jnp.zeros((fields, channels), jnp.float32)
+    for i in range(3):
+        rest, pieces = moment_ref[i], []
+        for _ in range(3):
+            pieces.append(rest.astype(jnp.bfloat16).astype(jnp.float32))
+            rest = rest - pieces[-1]
+        part = dot_nt(jnp.concatenate(pieces, axis=0).astype(jnp.bfloat16), contract_ref[i])
+        grad_lift += part[:fields] + part[fields : 2 * fields] + part[2 * fields :]
     delta_ref[:channels, :] = jnp.zeros((channels, width), jnp.bfloat16)
     delta_ref[(rows - 1) * channels :, :] = jnp.zeros((channels, width), jnp.bfloat16)
     for y in range(1, rows - 1):
@@ -460,14 +468,7 @@
         states = jnp.concatenate(states, axis=1)
         deltas = jnp.concatenate([delta_ref[y * channels : (y + 1) * channels, :] for y in span], axis=1)
         crossed += dot_nt(deltas, states)
-    grad_lift = crossed.T
-    for i in range(3):
-        rest, pieces = moment_ref[i], []
-        for _ in range(3):
-            pieces.append(rest.astype(jnp.bfloat16).astype(jnp.float32))
-            rest = rest - pieces[-1]
-        part = dot_nt(jnp.concatenate(pieces, axis=0).astype(jnp.bfloat16), contract_ref[i])
-        grad_lift += part[:fields] + part[fields : 2 * fields] + part[2 * fields :]
+    grad_lift += crossed.T
     out_ref[...] = jnp.zeros_like(out_ref)
     out_ref[-fields:, channels:] = grad_lift
 
@@ -530,7 +531,7 @@
 
 def sum_over(x, axis, low, high):
     if high // low == 4:
-        a, b, c = (swap(x, axis, k * low) for k in (1, 2, 3))
+        b, a, c = (swap(x, axis, k * low) for k in (2, 1, 3))
         return (x + a) + (b + c)
     bit = low
     while bit < high:

time: 52.7 us -> 52.7 us (level)
  transfers between devices with their start and end apart: 13 -> 13, of which waited for: 7 -> 7; matrix products, arithmetic and copies ran while one was open for 4% -> 4% of each run, Pallas kernels for 11% -> 12%
where the time goes in v8:
time: 52.7 us; the launch traced here: 52.5 us
  starting transfers between devices  24.4 us (46%)
  Pallas kernels  13.3 us (25%)
  waiting for transfers between devices  11.1 us (21%)
  other arithmetic  1.53 us (3%)
  local copies, waits for them, and re-layouts  1.24 us (2%)
  between operations  0.87 us (2%)
    ppermute x8, waiting for transfers between devices, swap(): lax.ppermute(x, axis, [(i, i ^ bit) for i in range(lax.axis_size(axis))])  8.2 us
    ppermute x8, starting transfers between devices, swap(): lax.ppermute(x, axis, [(i, i ^ bit) for i in range(lax.axis_size(axis))])  8.15 us
    all_to_all x1, starting transfers between devices, per_device(): lax.all_to_all(outgoing, ('face', 'lon'), split_axis=0, concat_axis=0, ti...  7.31 us
    ppermute x2, starting transfers between devices, pair_swap(): lax.ppermute(jnp.where(even, odd_sends, even_sends), axis, inner)  4.61 us
    ppermute x2, starting transfers between devices, pair_swap(): lax.ppermute(jnp.where(even, even_sends, odd_sends), axis, outer)  4.36 us
    pallas_call x1, Pallas kernels, regrid(): pl.pallas_call(functools.partial(regrid_kernel, capacity), out_shape=jax....  3.4 us
    pallas_call x1, Pallas kernels, convolve(): pl.pallas_call(convolve_kernel, out_shape=(jax.ShapeDtypeStruct((rows * c...  3.14 us
    pallas_call x1, Pallas kernels, backward(): pl.pallas_call(functools.partial(backward_kernel, capacity, channels, nor...  3.05 us
  transfers between devices with their start and end apart: 13, of which 7 were waited for; matrix products, arithmetic and copies ran while one was open for 4% of the time, Pallas kernels for 12%

profile of v8, /device:TPU:0, one launch (start us, length us, event | category | flops | bytes accessed | tf_op | source)
XLA Modules:
  0.0 52.5 jit_solution(12619493411195509624)
XLA Ops:
  0.6 3.4 %regrid.1 = bf16[32,9,8,128]{3,2,1,0:T(8,128)(2,1)} custom-call(s32[4,32]{1,0:T(4,128)} %bitcast.30, s32[4,32]{1,0:T(4,128)} %bitcast.31, bf16[32,8,128]{2,1,0:T(8,128)(2,1)} %src_hbm.1, bf16[32,4,128,128]{3,2,1,0:T(8,128)(2,1)} %wts_hbm.1), custom_call_target="tpu_custom_call" | custom-call | flops 33554432 | bytes 4194304 | tf_op jit(solution)/shard_map/regrid/pallas_call | solution.py:88
  4.1 7.3 %all-to-all-start = ((bf16[32,9,8,128]{3,2,1,0:T(8,128)(2,1)}), bf16[32,9,8,128]{3,2,1,0:T(8,128)(2,1)S(1)}, u32[]{:S(2)}, u32[]{:S(2)}) async-start(bf16[32,9,8,128]{3,2,1,0:T(8,128)(2,1)} %regrid.1), calls=%async_computation | async-start | bytes 1179648 | tf_op jit(solution)/shard_map/all_to_all | solution.py:579
  11.4 0.1 copy.21
  11.5 0.7 %collective-permute-start = (bf16[8,256]{1,0:T(8,128)(2,1)S(1)}, bf16[8,256]{1,0:T(8,128)(2,1)S(1)}, u32[]{:S(2)}, u32[]{:S(2)}) collective-permute-start(bf16[8,256]{1,0:T(8,128)(2,1)S(1)} %get-tuple-element.62), channel_id=1, source_target_pairs={{8,16},{16,8},{9,17},{17,9},{10,18},{18,10},{11,19},{19,11},{12,20... | collective-permute-start | bytes 12296 | tf_op jit(solution)/shard_map/ppermute | solution.py:552
  12.2 4.5 %collective-permute-start.1 = (bf16[8,256]{1,0:T(8,128)(2,1)S(1)}, bf16[8,256]{1,0:T(8,128)(2,1)S(1)}, u32[]{:S(2)}, u32[]{:S(2)}) collective-permute-start(bf16[8,256]{1,0:T(8,128)(2,1)S(1)} %get-tuple-element.63), channel_id=1, source_target_pairs={{0,8},{8,0},{16,24},{24,16},{1,9},{9,1},{17,25},{25,17},{2,10},{10... | collective-permute-start | bytes 12296 | tf_op jit(solution)/shard_map/ppermute | solution.py:551
  16.7 0.3 copy.17
  17.1 0.1 copy.16.readout_ref
  17.2 1.3 %collective-permute-done.1 = bf16[8,256]{1,0:T(8,128)(2,1)S(1)} collective-permute-done((bf16[8,256]{1,0:T(8,128)(2,1)S(1)}, bf16[8,256]{1,0:T(8,128)(2,1)S(1)}, u32[]{:S(2)}, u32[]{:S(2)}) %collective-permute-start.1) | collective-permute-done | bytes 4128 | tf_op jit(solution)/shard_map/ppermute | solution.py:551
  18.5 0.1 fusion.13
  18.6 0.1 broadcast_select_fusion.5
  18.7 0.1 collective-permute-start.3
  18.8 3.7 %collective-permute-start.2 = (bf16[8,128]{1,0:T(8,128)(2,1)S(1)}, bf16[8,128]{1,0:T(8,128)(2,1)S(1)}, u32[]{:S(2)}, u32[]{:S(2)}) collective-permute-start(bf16[8,128]{1,0:T(8,128)(2,1)S(1)} %get-tuple-element.57), channel_id=1, source_target_pairs={{1,2},{2,1},{3,4},{4,3},{5,6},{6,5},{7,0},{0,7},{9,10},{10,9},{11,... | collective-permute-start | bytes 6152 | tf_op jit(solution)/shard_map/ppermute | solution.py:552
  22.5 3.1 %convolve.1 = (f32[2048,256]{1,0:T(8,128)S(1)}, f32[8,32,256]{2,1,0:T(8,128)S(1)}, f32[64,256]{1,0:T(8,128)S(1)}, bf16[80,8]{1,0:T(8,128)(2,1)S(1)}, bf16[192,24...) custom-call(bf16[32,8,256]{2,1,0:T(8,128)(2,1)S(1)} %bitcast.25, ...), custom_call_target="tpu_custom_call" | custom-call | flops 754974720 | bytes 4194304 | tf_op jit(solution)/shard_map/convolve/pallas_call | solution.py:183
  25.6 0.6 %copy-done.2 = bf16[3,64,192]{2,1,0:T(8,128)(2,1)} copy-done((bf16[3,64,192]{2,1,0:T(8,128)(2,1)}, bf16[3,64,192]{2,1,0:T(8,128)(2,1)S(1)}, u32[]{:S(2)}) %copy-start.2) | copy-done | bytes 73752
  26.3 1.3 %finish.1 = (f32[2048,256]{1,0:T(8,128)S(1)}, f32[8,32,256]{2,1,0:T(8,128)S(1)}, bf16[240,256]{1,0:T(8,128)(2,1)S(1)}) custom-call(f32[2048,256]{1,0:T(8,128)S(1)} %get-tuple-element.36.old_act_ref, f32[8,32,256]{2,1,0:T(8,128)S(1)} %get-tuple-element.37.old_forecast_ref, ...), custom_call_target="tpu_custom_call", output_to_operand_aliasing={{0}: (0, {}), {1}: (1, {})} | custom-call | flops 1048576 | bytes 4194304 | tf_op jit(solution)/shard_map/finish/pallas_call | solution.py:261
  27.6 1.6 %all-to-all-done = bf16[32,9,8,128]{3,2,1,0:T(8,128)(2,1)S(1)} async-done(((bf16[32,9,8,128]{3,2,1,0:T(8,128)(2,1)}), bf16[32,9,8,128]{3,2,1,0:T(8,128)(2,1)S(1)}, u32[]{:S(2)}, u32[]{:S(2)}) %all-to-all-start) | async-done | bytes 589856 | tf_op jit(solution)/shard_map/all_to_all | solution.py:579
  29.2 3.1 %backward.1 = (f32[8,32,256]{2,1,0:T(8,128)S(1)}, f32[2,152,128]{2,1,0:T(8,128)S(1)}, bf16[2176,256]{1,0:T(8,128)(2,1)S(1)}, f32[3,8,192]{2,1,0:T(8,128)S(1)}) custom-call(bf16[32,72,128]{2,1,0:T(8,128)(2,1)S(1)} %bitcast.23, bf16[32,8,256]{2,1,0:T(8,128)(2,1)S(1)} %bitcast.26, bf16[2,8,256]{2,1,0:T(8,128)(2,1)S(1)} %pad_maximum_fusion.edge_ref, ...), custom_call_target="tpu_custom_call" | custom-call | flops 754974720 | bytes 4194304 | tf_op jit(solution)/shard_map/backward/pallas_call | solution.py:410
  32.3 1.7 %lift_gradient.1 = f32[152,128]{1,0:T(8,128)S(1)} custom-call(bf16[2176,256]{1,0:T(8,128)(2,1)S(1)} %get-tuple-element.46.slope_ref, bf16[32,8,256]{2,1,0:T(8,128)(2,1)S(1)} %bitcast.27, bf16[192,192]{1,0:T(8,128)(2,1)S(1)} %get-tuple-element.47.back_ref, bf16[3,64,192]{2,1,0:T(8,128)(2,1)S(1)} %copy-done.3, f32[3,8,192]{2,1,0:T(8,128)S(1)} %get-tuple-element.49.moment_ref), custom_call_target="tpu_custom_call" | custom-call | flops 603979776 | bytes 1114112 | tf_op jit(solution)/shard_map/lift_gradient/pallas_call | solution.py:480
  34.0 0.9 %collective-permute-start.7 = (f32[152,128]{1,0:T(8,128)S(1)}, f32[152,128]{1,0:T(8,128)S(1)}, u32[]{:S(2)}, u32[]{:S(2)}) collective-permute-start(f32[152,128]{1,0:T(8,128)S(1)} %fusion), channel_id=1, source_target_pairs={{0,24},{8,16},{16,8},{24,0},{1,25},{9,17},{17,9},{25,1},{2,26},{10... | collective-permute-start | bytes 233480 | tf_op jit(solution)/shard_map/ppermute | solution.py:529
  34.9 1.5 %collective-permute-start.6 = (f32[152,128]{1,0:T(8,128)S(1)}, f32[152,128]{1,0:T(8,128)S(1)}, u32[]{:S(2)}, u32[]{:S(2)}) collective-permute-start(f32[152,128]{1,0:T(8,128)S(1)} %fusion), channel_id=1, source_target_pairs={{0,16},{8,24},{16,0},{24,8},{1,17},{9,25},{17,1},{25,9},{2,18},{10... | collective-permute-start | bytes 233480 | tf_op jit(solution)/shard_map/ppermute | solution.py:529
  36.4 1.2 %collective-permute-start.5 = (f32[152,128]{1,0:T(8,128)S(1)}, f32[152,128]{1,0:T(8,128)S(1)}, u32[]{:S(2)}, u32[]{:S(2)}) collective-permute-start(f32[152,128]{1,0:T(8,128)S(1)} %fusion), channel_id=1, source_target_pairs={{0,8},{8,0},{16,24},{24,16},{1,9},{9,1},{17,25},{25,17},{2,10},{10... | collective-permute-start | bytes 233480 | tf_op jit(solution)/shard_map/ppermute | solution.py:529
  37.6 0.7 %convert_element_type.10 = bf16[8,32,256]{2,1,0:T(8,128)(2,1)} convert(f32[8,32,256]{2,1,0:T(8,128)S(1)} %get-tuple-element.44.forecast_ref) | non-fusion elementwise | flops 65536 | bytes 393216 | tf_op jit(solution)/shard_map/convert_element_type | solution.py:607
  38.3 0.7 %convert_element_type.9 = bf16[8,32,256]{2,1,0:T(8,128)(2,1)} convert(f32[8,32,256]{2,1,0:T(8,128)S(1)} %get-tuple-element.50) | non-fusion elementwise | flops 65536 | bytes 393216 | tf_op jit(solution)/shard_map/convert_element_type | solution.py:607
  38.9 1.3 %collective-permute-done.7 = f32[152,128]{1,0:T(8,128)S(1)} collective-permute-done((f32[152,128]{1,0:T(8,128)S(1)}, f32[152,128]{1,0:T(8,128)S(1)}, u32[]{:S(2)}, u32[]{:S(2)}) %collective-permute-start.7) | collective-permute-done | bytes 77856 | tf_op jit(solution)/shard_map/ppermute | solution.py:529
  40.2 0.6 %collective-permute-done.6 = f32[152,128]{1,0:T(8,128)S(1)} collective-permute-done((f32[152,128]{1,0:T(8,128)S(1)}, f32[152,128]{1,0:T(8,128)S(1)}, u32[]{:S(2)}, u32[]{:S(2)}) %collective-permute-start.6) | collective-permute-done | bytes 77856 | tf_op jit(solution)/shard_map/ppermute | solution.py:529
  40.8 1.1 %collective-permute-start.10 = (f32[152,128]{1,0:T(8,128)S(1)}, f32[152,128]{1,0:T(8,128)S(1)}, u32[]{:S(2)}, u32[]{:S(2)}) collective-permute-start(f32[152,128]{1,0:T(8,128)S(1)} %add_add_fusion.1), channel_id=1, source_target_pairs={{0,6},{1,7},{2,4},{3,5},{4,2},{5,3},{6,0},{7,1},{8,14},{9,15},{10,... | collective-permute-start | bytes 233480 | tf_op jit(solution)/shard_map/ppermute | solution.py:529
  42.0 1.6 %collective-permute-start.9 = (f32[152,128]{1,0:T(8,128)S(1)}, f32[152,128]{1,0:T(8,128)S(1)}, u32[]{:S(2)}, u32[]{:S(2)}) collective-permute-start(f32[152,128]{1,0:T(8,128)S(1)} %add_add_fusion.1), channel_id=1, source_target_pairs={{0,4},{1,5},{2,6},{3,7},{4,0},{5,1},{6,2},{7,3},{8,12},{9,13},{10,... | collective-permute-start | bytes 233480 | tf_op jit(solution)/shard_map/ppermute | solution.py:529
  43.6 1.7 %collective-permute-start.8 = (f32[152,128]{1,0:T(8,128)S(1)}, f32[152,128]{1,0:T(8,128)S(1)}, u32[]{:S(2)}, u32[]{:S(2)}) collective-permute-start(f32[152,128]{1,0:T(8,128)S(1)} %add_add_fusion.1), channel_id=1, source_target_pairs={{0,2},{1,3},{2,0},{3,1},{4,6},{5,7},{6,4},{7,5},{8,10},{9,11},{10,... | collective-permute-start | bytes 233480 | tf_op jit(solution)/shard_map/ppermute | solution.py:529
  45.3 2.6 %collective-permute-done.10 = f32[152,128]{1,0:T(8,128)S(1)} collective-permute-done((f32[152,128]{1,0:T(8,128)S(1)}, f32[152,128]{1,0:T(8,128)S(1)}, u32[]{:S(2)}, u32[]{:S(2)}) %collective-permute-start.10) | collective-permute-done | bytes 77856 | tf_op jit(solution)/shard_map/ppermute | solution.py:529
  47.8 2.5 %collective-permute-done.9 = f32[152,128]{1,0:T(8,128)S(1)} collective-permute-done((f32[152,128]{1,0:T(8,128)S(1)}, f32[152,128]{1,0:T(8,128)S(1)}, u32[]{:S(2)}, u32[]{:S(2)}) %collective-permute-start.9) | collective-permute-done | bytes 77856 | tf_op jit(solution)/shard_map/ppermute | solution.py:529
  50.4 1.3 %collective-permute-done.11.other_ref = f32[152,128]{1,0:T(8,128)S(1)} collective-permute-done((f32[152,128]{1,0:T(8,128)S(1)}, f32[152,128]{1,0:T(8,128)S(1)}, u32[]{:S(2)}, u32[]{:S(2)}) %collective-permute-start.11) | collective-permute-done | bytes 77856 | tf_op jit(solution)/shard_map/ppermute | solution.py:529
  51.7 0.8 %unpack.1 = (f32[9,64,64]{2,1,0:T(8,128)}, f32[8,64]{1,0:T(8,128)}, f32[8,64]{1,0:T(8,128)}) custom-call(f32[152,128]{1,0:T(8,128)S(1)} %add_add_fusion.mine_ref, f32[152,128]{1,0:T(8,128)S(1)} %collective-permute-done.11.other_ref), custom_call_target="tpu_custom_call" | custom-call | tf_op jit(solution)/shard_map/unpack/pallas_call | solution.py:516
  (31 shorter events, 0.3 us)
Async XLA Ops:
  0.6 10.8 %copy-start.4 = (bf16[8,32,256]{2,1,0:T(8,128)(2,1)S(1)}, bf16[8,32,256]{2,1,0:T(8,128)(2,1)}, u32[]{:S(2)}) copy-start(bf16[8,32,256]{2,1,0:T(8,128)(2,1)} %param.12) | copy-start | bytes 393220
  4.0 13.0 %copy-start.5 = (bf16[64,8]{0,1:T(8,128)(2,1)S(1)}, bf16[64,8]{0,1:T(8,128)(2,1)}, u32[]{:S(2)}) copy-start(bf16[64,8]{0,1:T(8,128)(2,1)} %param.15) | copy-start | bytes 3076
  4.1 18.4 %copy-start = (bf16[9,64,64]{2,1,0:T(8,128)(2,1)S(1)}, bf16[9,64,64]{2,1,0:T(8,128)(2,1)}, u32[]{:S(2)}) copy-start(bf16[9,64,64]{2,1,0:T(8,128)(2,1)} %kernel_ref) | copy-start | bytes 221188
  4.1 18.4 %copy-start.1 = (bf16[8,64]{1,0:T(8,128)(2,1)S(1)}, bf16[8,64]{1,0:T(8,128)(2,1)}, u32[]{:S(2)}) copy-start(bf16[8,64]{1,0:T(8,128)(2,1)} %lift_weight_ref) | copy-start | bytes 3076
  4.1 25.1 %all-to-all-start = ((bf16[32,9,8,128]{3,2,1,0:T(8,128)(2,1)}), bf16[32,9,8,128]{3,2,1,0:T(8,128)(2,1)S(1)}, u32[]{:S(2)}, u32[]{:S(2)}) async-start(bf16[32,9,8,128]{3,2,1,0:T(8,128)(2,1)} %regrid.1), calls=%async_computation | async-start | bytes 1179648 | tf_op jit(solution)/shard_map/all_to_all | solution.py:579
  11.5 5.7 %collective-permute-start = (bf16[8,256]{1,0:T(8,128)(2,1)S(1)}, bf16[8,256]{1,0:T(8,128)(2,1)S(1)}, u32[]{:S(2)}, u32[]{:S(2)}) collective-permute-start(bf16[8,256]{1,0:T(8,128)(2,1)S(1)} %get-tuple-element.62), channel_id=1, source_target_pairs={{8,16},{16,8},{9,17},{17,9},{10,18},{18,10},{11,19},{19,11},{12,20... | collective-permute-start | bytes 12296 | tf_op jit(solution)/shard_map/ppermute | solution.py:552
  12.2 6.3 %collective-permute-start.1 = (bf16[8,256]{1,0:T(8,128)(2,1)S(1)}, bf16[8,256]{1,0:T(8,128)(2,1)S(1)}, u32[]{:S(2)}, u32[]{:S(2)}) collective-permute-start(bf16[8,256]{1,0:T(8,128)(2,1)S(1)} %get-tuple-element.63), channel_id=1, source_target_pairs={{0,8},{8,0},{16,24},{24,16},{1,9},{9,1},{17,25},{25,17},{2,10},{10... | collective-permute-start | bytes 12296 | tf_op jit(solution)/shard_map/ppermute | solution.py:551
  18.7 7.6 %collective-permute-start.3 = (bf16[8,128]{1,0:T(8,128)(2,1)S(1)}, bf16[8,128]{1,0:T(8,128)(2,1)S(1)}, u32[]{:S(2)}, u32[]{:S(2)}) collective-permute-start(bf16[8,128]{1,0:T(8,128)(2,1)S(1)} %broadcast_select_fusion.4), channel_id=1, source_target_pairs={{0,1},{1,0},{2,3},{3,2},{4,5},{5,4},{6,7},{7,6},{8,9},{9,8},{10,11... | collective-permute-start | bytes 6152 | tf_op jit(solution)/shard_map/ppermute | solution.py:551
  18.8 7.5 %collective-permute-start.2 = (bf16[8,128]{1,0:T(8,128)(2,1)S(1)}, bf16[8,128]{1,0:T(8,128)(2,1)S(1)}, u32[]{:S(2)}, u32[]{:S(2)}) collective-permute-start(bf16[8,128]{1,0:T(8,128)(2,1)S(1)} %get-tuple-element.57), channel_id=1, source_target_pairs={{1,2},{2,1},{3,4},{4,3},{5,6},{6,5},{7,0},{0,7},{9,10},{10,9},{11,... | collective-permute-start | bytes 6152 | tf_op jit(solution)/shard_map/ppermute | solution.py:552
  25.6 0.6 %copy-start.2 = (bf16[3,64,192]{2,1,0:T(8,128)(2,1)}, bf16[3,64,192]{2,1,0:T(8,128)(2,1)S(1)}, u32[]{:S(2)}) copy-start(bf16[3,64,192]{2,1,0:T(8,128)(2,1)S(1)} %get-tuple-element.48.contract_ref) | copy-start | bytes 221188
  27.6 4.8 %copy-start.3 = (bf16[3,64,192]{2,1,0:T(8,128)(2,1)S(1)}, bf16[3,64,192]{2,1,0:T(8,128)(2,1)}, u32[]{:S(2)}) copy-start(bf16[3,64,192]{2,1,0:T(8,128)(2,1)} %copy-done.2) | copy-start | bytes 221188
  32.2 1.7 %collective-permute-start.4 = (f32[152,128]{1,0:T(8,128)S(1)}, f32[152,128]{1,0:T(8,128)S(1)}, u32[]{:S(2)}, u32[]{:S(2)}) collective-permute-start(f32[152,128]{1,0:T(8,128)S(1)} %slice_bitcast_fusion), channel_id=1, source_target_pairs={{0,1},{1,0},{2,3},{3,2},{4,5},{5,4},{6,7},{7,6},{8,9},{9,8},{10,11... | collective-permute-start | bytes 233480 | tf_op jit(solution)/shard_map/ppermute | solution.py:529
  34.0 6.2 %collective-permute-start.7 = (f32[152,128]{1,0:T(8,128)S(1)}, f32[152,128]{1,0:T(8,128)S(1)}, u32[]{:S(2)}, u32[]{:S(2)}) collective-permute-start(f32[152,128]{1,0:T(8,128)S(1)} %fusion), channel_id=1, source_target_pairs={{0,24},{8,16},{16,8},{24,0},{1,25},{9,17},{17,9},{25,1},{2,26},{10... | collective-permute-start | bytes 233480 | tf_op jit(solution)/shard_map/ppermute | solution.py:529
  34.9 5.9 %collective-permute-start.6 = (f32[152,128]{1,0:T(8,128)S(1)}, f32[152,128]{1,0:T(8,128)S(1)}, u32[]{:S(2)}, u32[]{:S(2)}) collective-permute-start(f32[152,128]{1,0:T(8,128)S(1)} %fusion), channel_id=1, source_target_pairs={{0,16},{8,24},{16,0},{24,8},{1,17},{9,25},{17,1},{25,9},{2,18},{10... | collective-permute-start | bytes 233480 | tf_op jit(solution)/shard_map/ppermute | solution.py:529
  36.4 4.4 %collective-permute-start.5 = (f32[152,128]{1,0:T(8,128)S(1)}, f32[152,128]{1,0:T(8,128)S(1)}, u32[]{:S(2)}, u32[]{:S(2)}) collective-permute-start(f32[152,128]{1,0:T(8,128)S(1)} %fusion), channel_id=1, source_target_pairs={{0,8},{8,0},{16,24},{24,16},{1,9},{9,1},{17,25},{25,17},{2,10},{10... | collective-permute-start | bytes 233480 | tf_op jit(solution)/shard_map/ppermute | solution.py:529
  40.8 7.0 %collective-permute-start.10 = (f32[152,128]{1,0:T(8,128)S(1)}, f32[152,128]{1,0:T(8,128)S(1)}, u32[]{:S(2)}, u32[]{:S(2)}) collective-permute-start(f32[152,128]{1,0:T(8,128)S(1)} %add_add_fusion.1), channel_id=1, source_target_pairs={{0,6},{1,7},{2,4},{3,5},{4,2},{5,3},{6,0},{7,1},{8,14},{9,15},{10,... | collective-permute-start | bytes 233480 | tf_op jit(solution)/shard_map/ppermute | solution.py:529
  42.0 8.4 %collective-permute-start.9 = (f32[152,128]{1,0:T(8,128)S(1)}, f32[152,128]{1,0:T(8,128)S(1)}, u32[]{:S(2)}, u32[]{:S(2)}) collective-permute-start(f32[152,128]{1,0:T(8,128)S(1)} %add_add_fusion.1), channel_id=1, source_target_pairs={{0,4},{1,5},{2,6},{3,7},{4,0},{5,1},{6,2},{7,3},{8,12},{9,13},{10,... | collective-permute-start | bytes 233480 | tf_op jit(solution)/shard_map/ppermute | solution.py:529
  43.6 6.7 %collective-permute-start.8 = (f32[152,128]{1,0:T(8,128)S(1)}, f32[152,128]{1,0:T(8,128)S(1)}, u32[]{:S(2)}, u32[]{:S(2)}) collective-permute-start(f32[152,128]{1,0:T(8,128)S(1)} %add_add_fusion.1), channel_id=1, source_target_pairs={{0,2},{1,3},{2,0},{3,1},{4,6},{5,7},{6,4},{7,5},{8,10},{9,11},{10,... | collective-permute-start | bytes 233480 | tf_op jit(solution)/shard_map/ppermute | solution.py:529
  50.4 1.3 %collective-permute-start.11 = (f32[152,128]{1,0:T(8,128)S(1)}, f32[152,128]{1,0:T(8,128)S(1)}, u32[]{:S(2)}, u32[]{:S(2)}) collective-permute-start(f32[152,128]{1,0:T(8,128)S(1)} %add_add_fusion.mine_ref), channel_id=1, source_target_pairs={{0,1},{1,0},{2,3},{3,2},{4,5},{5,4},{6,7},{7,6},{8,9},{9,8},{10,11... | collective-permute-start | bytes 233480 | tf_op jit(solution)/shard_map/ppermute | solution.py:529
